TPU v7x, 256 devices: a whole 4x4x8 slice. The times are simulated.
256 devices in a mesh: gauss: 64 (over z, x, core), view: 4 (over y).
Axes of the slice: x: 4, y: 4, z: 8, core: 2. Of those that a mesh axis runs over, the one named last changes fastest.
Arguments:
- params: float32 [59, 65536], P(None, 'gauss'), as said below
- first_moment: float32 [59, 65536], P(None, 'gauss'), may hold values from -6 to 6
- second_moment: float32 [59, 65536], P(None, 'gauss'), may hold values from 0.0001 to 1
- cameras: float32 [4, 16], P('view'), as said below
- target: float32 [4, 256, 3, 256], P('view', 'gauss'), may hold values from 0 to 1
- tile_index: int32 [4, 256], P('view', 'gauss'), may hold values from 0 to 255, as said below
- tile_lists: int32 [4, 256, 256], P('view', 'gauss'), may hold values from -1 to 1023, as said below
- send_slots: int32 [4, 64, 1024], P('view', 'gauss'), may hold values from 0 to 1023, as said below
- reloc_send: int32 [64, 128], P('gauss'), may hold values from -1 to 1023, as said below
- reloc_recv: int32 [64, 128], P('gauss'), may hold values from -1 to 1023, as said below
Outputs:
- new_params: float32 [59, 65536], P(None, 'gauss')
- new_first: float32 [59, 65536], P(None, 'gauss')
- new_second: float32 [59, 65536], P(None, 'gauss')
- gradient: float32 [59, 65536], P(None, 'gauss')
Inputs may be any that keep to these rules, and one draw needn't show every extreme that they name: `params`: positions lie in front of every camera at depth 2.5 or more; quaternions have norm 0.5 or more; rows are position, log scale, quaternion, opacity logit, then colour coefficients 3 k + channel. `cameras`: entries 0 to 8 a rotation matrix, 9 to 11 a translation, 12 and 13 focal lengths, 14 and 15 the principal point, in pixels of the crop. `tile_index`: each row is a permutation of the 256 screen tiles. `send_slots`: entry (v, s, d * 16 + k) names a Gaussian of device s; device d keeps it as its received row s * 16 + k. `tile_lists`: each entry is a column s * 16 + k of the tile's device's received rows, in compositing order; a tile's used entries are distinct, hold equally many rows from every device s, and the entries -1 come after all of them; in every view some tile has 256 used entries. `reloc_send`: entry (s, d * 2 + k) is a slot on device s copied to device d, or -1; the used entries of a pair (s, d) come first, and some pair uses all 2; a slot may appear several times; no slot of device s is both here and in row s of reloc_recv. `reloc_recv`: entry (d, s * 2 + k) is the slot on device d that receives the copy named by reloc_send[s, d * 2 + k], -1 exactly where that is -1; the used slots of a row are distinct.
All inputs are finite; a program needn't handle non-finite values.
Results may differ from a plain program's by a relative error of at most 0.0003.
Values sent between devices are 32-bit elements; how exact they have to be, the bound alone decides.
No kernel may reach another device: no remote copies, remote signals or barrier semaphores. Data moves between devices by JAX's collectives and lax.ppermute only.
A program may use at most 128 MiB of HBM per device.

v0:
```python
import math

import jax
import jax.numpy as jnp
from jax import lax
from jax.sharding import PartitionSpec as P

TILES_ACROSS = 16


TOP_PRECISION = lax.Precision.HIGHEST
SH_ZERO = 0.28209479177387814
SH_ONE = 0.4886025119029199
SH_TWO = (
    1.0925484305920792,
    -1.0925484305920792,
    0.31539156525252005,
    -1.0925484305920792,
    0.5462742152960396,
)
SH_THREE = (
    -0.5900435899266435,
    2.890611442640554,
    -0.4570457994644658,
    0.3731763325901154,
    -0.4570457994644658,
    1.445305721320277,
    -0.5900435899266435,
)
BIAS_ONE = 1.0 - math.exp(1000.0 * math.log(0.9))
BIAS_TWO = 1.0 - math.exp(1000.0 * math.log(0.999))


def harmonic(coeffs, direction):
    dir_x, dir_y, dir_z = (direction[0], direction[1], direction[2])
    sq_x, sq_y, sq_z = (dir_x * dir_x, dir_y * dir_y, dir_z * dir_z)
    factors = [
        SH_ZERO * jnp.ones_like(dir_x),
        -SH_ONE * dir_y,
        SH_ONE * dir_z,
        -SH_ONE * dir_x,
        SH_TWO[0] * dir_x * dir_y,
        SH_TWO[1] * dir_y * dir_z,
        SH_TWO[2] * (2.0 * sq_z - sq_x - sq_y),
        SH_TWO[3] * dir_x * dir_z,
        SH_TWO[4] * (sq_x - sq_y),
        SH_THREE[0] * dir_y * (3.0 * sq_x - sq_y),
        SH_THREE[1] * dir_x * dir_y * dir_z,
        SH_THREE[2] * dir_y * (4.0 * sq_z - sq_x - sq_y),
        SH_THREE[3] * dir_z * (2.0 * sq_z - 3.0 * sq_x - 3.0 * sq_y),
        SH_THREE[4] * dir_x * (4.0 * sq_z - sq_x - sq_y),
        SH_THREE[5] * dir_z * (sq_x - sq_y),
        SH_THREE[6] * dir_x * (sq_x - 3.0 * sq_y),
    ]
    result = jnp.zeros(coeffs.shape[1:], coeffs.dtype)
    for index_k in range(16):
        result = result + factors[index_k][None, :] * coeffs[index_k]
    return result


def project(params, camera):
    position = params[0:3]
    rotation = camera[0:9].reshape(3, 3)
    offset = camera[9:12]
    focal_x, focal_y, centre_x, centre_y = (camera[12], camera[13], camera[14], camera[15])
    in_camera = jnp.dot(rotation, position, precision=TOP_PRECISION) + offset[:, None]
    cam_x, cam_y, cam_z = (in_camera[0], in_camera[1], in_camera[2])
    inverse_z = 1.0 / cam_z
    mean_u = focal_x * cam_x * inverse_z + centre_x
    mean_w = focal_y * cam_y * inverse_z + centre_y
    quaternion = params[6:10]
    quaternion = quaternion / jnp.sqrt(jnp.sum(quaternion * quaternion, axis=0))
    quat_w, quat_x, quat_y, quat_z = (quaternion[0], quaternion[1], quaternion[2], quaternion[3])
    orient = [
        [
            1.0 - 2.0 * (quat_y * quat_y + quat_z * quat_z),
            2.0 * (quat_x * quat_y - quat_w * quat_z),
            2.0 * (quat_x * quat_z + quat_w * quat_y),
        ],
        [
            2.0 * (quat_x * quat_y + quat_w * quat_z),
            1.0 - 2.0 * (quat_x * quat_x + quat_z * quat_z),
            2.0 * (quat_y * quat_z - quat_w * quat_x),
        ],
        [
            2.0 * (quat_x * quat_z - quat_w * quat_y),
            2.0 * (quat_y * quat_z + quat_w * quat_x),
            1.0 - 2.0 * (quat_x * quat_x + quat_y * quat_y),
        ],
    ]
    scales = jnp.exp(params[3:6])
    factor_m = [[orient[row_i][col_j] * scales[col_j] for col_j in range(3)] for row_i in range(3)]
    sigma = [
        [
            factor_m[row_i][0] * factor_m[col_j][0]
            + factor_m[row_i][1] * factor_m[col_j][1]
            + factor_m[row_i][2] * factor_m[col_j][2]
            for col_j in range(3)
        ]
        for row_i in range(3)
    ]
    jac_a0 = focal_x * inverse_z
    jac_a2 = -focal_x * cam_x * inverse_z * inverse_z
    jac_b1 = focal_y * inverse_z
    jac_b2 = -focal_y * cam_y * inverse_z * inverse_z
    row_a = [jac_a0 * rotation[0, col_i] + jac_a2 * rotation[2, col_i] for col_i in range(3)]
    row_b = [jac_b1 * rotation[1, col_i] + jac_b2 * rotation[2, col_i] for col_i in range(3)]

    def quadratic(leftmost_row, right_row):
        total = jnp.zeros_like(cam_x)
        for row_i in range(3):
            for col_j in range(3):
                total = total + leftmost_row[row_i] * sigma[row_i][col_j] * right_row[col_j]
        return total

    cov_aa = quadratic(row_a, row_a) + 0.3
    cov_ab = quadratic(row_a, row_b)
    cov_bb = quadratic(row_b, row_b) + 0.3
    determinant = cov_aa * cov_bb - cov_ab * cov_ab
    opacity = jax.nn.sigmoid(params[10])
    centre = jnp.stack(
        [
            -(
                rotation[0, col_i] * offset[0]
                + rotation[1, col_i] * offset[1]
                + rotation[2, col_i] * offset[2]
            )
            for col_i in range(3)
        ]
    )
    direction = position - centre[:, None]
    direction = direction / jnp.sqrt(jnp.sum(direction * direction, axis=0))
    colour_values = jnp.maximum(harmonic(params[11:59].reshape(16, 3, -1), direction) + 0.5, 0.0)
    head = jnp.stack(
        [mean_u, mean_w, cov_bb / determinant, -cov_ab / determinant, cov_aa / determinant, opacity]
    )
    return jnp.concatenate([head, colour_values], axis=0)


def render_group(received, tile_rows, tile_ids, target_tile):
    live_entry = tile_rows >= 0
    safe_index = jnp.where(live_entry, tile_rows, 0)
    listed = received[:, safe_index]
    live_mask = live_entry.astype(received.dtype)
    pixels = jnp.arange(256, dtype=jnp.int32)
    left_edge = (tile_ids % TILES_ACROSS * 16).astype(received.dtype)
    top_edge = (tile_ids // TILES_ACROSS * 16).astype(received.dtype)
    pixel_u = left_edge[:, None] + (pixels % 16).astype(received.dtype)[None, :] + 0.5
    pixel_w = top_edge[:, None] + (pixels // 16).astype(received.dtype)[None, :] + 0.5
    block_extent = 128
    index_row = jnp.arange(block_extent)
    strict_upper = (index_row[:, None] < index_row[None, :]).astype(received.dtype)
    carried = jnp.zeros(pixel_u.shape, received.dtype)
    colour_values = jnp.zeros((tile_ids.shape[0], 3, 256), received.dtype)
    for block_index in range(tile_rows.shape[1] // block_extent):
        lower = block_index * block_extent
        rows_per_block = listed[:, :, lower : lower + block_extent]
        block_live = live_mask[:, lower : lower + block_extent]
        off_u = pixel_u[:, :, None] - rows_per_block[0][:, None, :]
        off_w = pixel_w[:, :, None] - rows_per_block[1][:, None, :]
        exponent = (
            -0.5
            * (
                rows_per_block[2][:, None, :] * off_u * off_u
                + rows_per_block[4][:, None, :] * off_w * off_w
            )
            - rows_per_block[3][:, None, :] * off_u * off_w
        )
        alphas = rows_per_block[5][:, None, :] * jnp.exp(exponent) * block_live[:, None, :]
        log_keep = jnp.log1p(-alphas)
        before = jnp.einsum("gpj,ji->gpi", log_keep, strict_upper, precision=TOP_PRECISION)
        blend_weights = jnp.exp(carried[:, :, None] + before) * alphas
        colour_values = colour_values + jnp.einsum(
            "xuo,sxo->xsu", blend_weights, rows_per_block[6:9], precision=TOP_PRECISION
        )
        carried = carried + jnp.sum(log_keep, axis=2)
    residual = colour_values - target_tile
    return 0.5 * jnp.sum(residual * residual)


def adam_update(params, gradient, first, second):
    rates = jnp.concatenate(
        [
            jnp.full((3, 1), 0.00016),
            jnp.full((3, 1), 0.005),
            jnp.full((4, 1), 0.001),
            jnp.full((1, 1), 0.05),
            jnp.full((3, 1), 0.0025),
            jnp.full((45, 1), 0.000125),
        ]
    ).astype(params.dtype)
    first_new = 0.9 * first + 0.1 * gradient
    second_new = 0.999 * second + 0.001 * gradient * gradient
    stepped = params - rates * (first_new / BIAS_ONE) / (jnp.sqrt(second_new / BIAS_TWO) + 1e-15)
    return (stepped, first_new, second_new)


def shards(
    params,
    first_moment,
    second_moment,
    cameras,
    target,
    tile_index,
    tile_lists,
    send_slots,
    reloc_send,
    reloc_recv,
):
    local_count = params.shape[1]
    camera = cameras[0]
    slot_list = send_slots.reshape(-1)
    peers = lax.axis_size("gauss")
    per_peer = slot_list.shape[0] // peers
    projected = project(params, camera)
    everything = lax.all_gather(projected, "gauss", axis=1, tiled=True)
    remote = lax.all_to_all(slot_list, "gauss", split_axis=0, concat_axis=0, tiled=True)
    source = jnp.arange(slot_list.shape[0], dtype=jnp.int32) // per_peer * local_count + remote
    received = everything[:, source]
    tile_rows = tile_lists[0]
    tile_ids = tile_index[0]
    target_tiles = target[0]
    group_count = tile_rows.shape[0] // 2

    def device_loss(arrived):
        render_step = jax.checkpoint(lambda item: render_group(arrived, item[0], item[1], item[2]))
        group_losses = lax.map(
            render_step,
            (
                tile_rows.reshape(group_count, 2, -1),
                tile_ids.reshape(group_count, 2),
                target_tiles.reshape(group_count, 2, 3, -1),
            ),
        )
        return jnp.sum(group_losses)

    device_total, pullback = jax.vjp(device_loss, received)
    (row_grads,) = pullback(jnp.ones((), device_total.dtype))
    returned = lax.all_to_all(row_grads, "gauss", split_axis=1, concat_axis=1, tiled=True)
    projected_grads = jnp.zeros_like(projected).at[:, slot_list].add(returned)
    unused_value, pull_project = jax.vjp(lambda values: project(values, camera), params)
    (local_grads,) = pull_project(projected_grads)
    gradient = lax.psum(local_grads, "view")
    stepped, first_new, second_new = adam_update(params, gradient, first_moment, second_moment)
    sources = reloc_send.reshape(-1)
    targets_local = reloc_recv.reshape(-1)
    slot_numbers = jnp.arange(local_count, dtype=jnp.int32)
    counts = jnp.sum((sources[None, :] == slot_numbers[:, None]).astype(jnp.int32), axis=1)
    sampled = counts > 0
    logit = stepped[10]
    share_log = -jax.nn.softplus(logit) / (counts.astype(stepped.dtype) + 1.0)
    spread_logit = jnp.log(-jnp.expm1(share_log)) - share_log
    stepped = stepped.at[10].set(jnp.where(sampled, spread_logit, logit))
    first_new = jnp.where(sampled[None, :], 0.0, first_new)
    second_new = jnp.where(sampled[None, :], 0.0, second_new)
    valid_source = sources >= 0
    outgoing = jnp.where(
        valid_source[None, :], stepped[:, jnp.where(valid_source, sources, 0)], 0.0
    )
    arrived_rows = lax.all_to_all(outgoing, "gauss", split_axis=1, concat_axis=1, tiled=True)
    landing = jnp.where(targets_local >= 0, targets_local, local_count)
    new_params = stepped.at[:, landing].set(arrived_rows, mode="drop")
    new_first = first_new.at[:, landing].set(0.0, mode="drop")
    new_second = second_new.at[:, landing].set(0.0, mode="drop")
    return (new_params, new_first, new_second, gradient)


def solution(mesh):
    in_specs = (
        P(None, "gauss"),
        P(None, "gauss"),
        P(None, "gauss"),
        P("view", None),
        P("view", "gauss", None, None),
        P("view", "gauss"),
        P("view", "gauss", None),
        P("view", "gauss", None),
        P("gauss", None),
        P("gauss", None),
    )
    out_specs = (P(None, "gauss"), P(None, "gauss"), P(None, "gauss"), P(None, "gauss"))
    return jax.shard_map(shards, mesh=mesh, in_specs=in_specs, out_specs=out_specs, check_vma=False)
```

profile of v0, /device:TPU:1, one launch (start us, length us, event | category | flops | bytes accessed | tf_op | source)
XLA Modules:
  0.0 404.1 jit_solution(4106005178710629555)
XLA Ops:
  7.9 1.6 fusion.164
  25.7 1.2 fusion.162
  27.2 1.3 multiply_add_fusion.1
  32.4 3.1 fusion.145
  35.5 7.8 %fusion.158 = (f32[1,1024]{1,0:T(1,128)S(1)}, f32[1,1024]{1,0:T(1,128)S(1)}, f32[1,1024]{1,0:T(1,128)}, f32[1,1024]{1,0:T(1,128)S(1)}, f32[1,1024]{1,0:T(1,128)}...) fusion(f32[1,1024]{1,0:T(1,128)S(1)} %get-tuple-element.341, ...), kind=kLoop, calls=%fused_computation.431 | loop fusion | flops 167936 | bytes 249900 | tf_op jit(solution)/shard_map/div | solution.py:135
  47.1 2.7 concatenate.5
  50.3 1.3 reduce.20
  52.4 13.0 %all-to-all-start = ((s32[64,16,1]{1,2,0:T(1,128)}), s32[64,16,1]{1,2,0:T(1,128)S(1)}, u32[]{:S(2)}, u32[]{:S(2)}) async-start(s32[64,16,1]{1,2,0:T(1,128)} %bitcast.72), calls=%async_computation | async-start | bytes 65536 | tf_op jit(solution)/shard_map/all_to_all | solution.py:217
  66.9 1.3 compare_select_fusion.7
  69.3 1.3 reduce.19
  72.0 1.3 reshape_squeeze.9
  87.4 109.3 %all-gather.2.cloned.1.call-done = f32[9,65536]{0,1:T(8,128)} async-done(((f32[9,1024]{0,1:T(8,128)}), f32[9,65536]{0,1:T(8,128)}) %all-gather.2.cloned.1.call-update) | async-done | bytes 2359312 | tf_op jit(solution)/shard_map/all_gather | solution.py:216
  196.7 13.3 %gather_fusion.1 = f32[1024,9]{1,0:T(8,128)S(1)} fusion(f32[9,65536]{0,1:T(8,128)} %all-gather.2.cloned.1.call-done, s32[1024]{0:T(1024)S(1)} %broadcast_clamp_fusion), kind=kCustom, calls=%fused_computation.1 | custom fusion | bytes 77824 | tf_op jit(solution)/shard_map/gather | solution.py:219
  210.1 46.7 %while.16 = (s32[]{:T(128)}, f32[9,1024]{0,1:T(8,128)S(1)}, s32[2,2,256]{2,1,0:T(2,128)}, s32[2,2]{1,0:T(2,128)}, f32[2,2,3,256]{3,2,1,0:T(4,128)S(1)}, /*index=...) while((s32[]{:T(128)}, f32[9,1024]{0,1:T(8,128)S(1)}, s32[2,2,256]{2,1,0:T(2,128)}, ...), condition=%wide.region_18.19_spmd, body=%wide.region_2.18_spmd.sunk | while | flops 433375424 | bytes 7886069 | solution.py:227
  214.4 1.2 fusion.228
  217.3 1.5 fusion.229
  218.9 1.4 convolution_bitcast_fusion.6
  221.5 1.4 fusion.231
  222.9 4.1 %fusion.233 = f32[2,256,128]{2,1,0:T(8,128)S(1)} fusion(f32[2,256,128]{2,1,0:T(8,128)S(1)} %fusion.231, f32[2,256,128]{2,1,0:T(8,128)} %copy-done.93, f32[2,256,128]{2,1,0:T(8,128)S(1)} %fusion.230, f32[2,128]{1,0:T(2,128)S(1)} %get-tuple-element.547, f32[2,128]{1,0:T(2,128)S(1)} %bitcast.349, f32[2,128]{1,0:T(2,128)S(1)} %bitcast.356, ...), kind=kOutput, calls=%fused_computation.19.clone.1 | output fusion | flops 2359935 | bytes 1591296 | tf_op jit(solution)/shard_map/transpose(jvp())/while/body/eval_jaxpr/checkpoint/broadcast_in_dim | solution.py:176
  227.0 2.2 fusion.234
  229.9 3.6 scatter_fusion
  237.7 1.2 fusion.228
  240.7 1.5 fusion.229
  242.3 1.4 convolution_bitcast_fusion.6
  244.9 1.4 fusion.231
  246.3 4.1 %fusion.233 = f32[2,256,128]{2,1,0:T(8,128)S(1)} fusion(f32[2,256,128]{2,1,0:T(8,128)S(1)} %fusion.231, f32[2,256,128]{2,1,0:T(8,128)} %copy-done.93, f32[2,256,128]{2,1,0:T(8,128)S(1)} %fusion.230, f32[2,128]{1,0:T(2,128)S(1)} %get-tuple-element.547, f32[2,128]{1,0:T(2,128)S(1)} %bitcast.349, f32[2,128]{1,0:T(2,128)S(1)} %bitcast.356, ...), kind=kOutput, calls=%fused_computation.19.clone.1 | output fusion | flops 2359935 | bytes 1591296 | tf_op jit(solution)/shard_map/transpose(jvp())/while/body/eval_jaxpr/checkpoint/broadcast_in_dim | solution.py:176
  250.4 2.2 fusion.234
  253.2 3.5 scatter_fusion
  258.2 6.5 %all-to-all-start.1 = ((f32[64,1,144]{2,1,0:T(1,128)}), f32[64,1,144]{2,1,0:T(1,128)S(1)}, u32[]{:S(2)}, u32[]{:S(2)}) async-start(f32[64,1,144]{2,1,0:T(1,128)} %reshape.755), calls=%async_computation.1 | async-start | bytes 131072 | tf_op jit(solution)/shard_map/all_to_all | solution.py:239
  266.0 8.8 %all-to-all-done.1 = f32[64,1,144]{2,1,0:T(1,128)S(1)} async-done(((f32[64,1,144]{2,1,0:T(1,128)}), f32[64,1,144]{2,1,0:T(1,128)S(1)}, u32[]{:S(2)}, u32[]{:S(2)}) %all-to-all-start.1) | async-done | bytes 36896 | tf_op jit(solution)/shard_map/all_to_all | solution.py:239
  276.4 6.3 %scatter_custom_fusion.1 = f32[9,1024]{0,1:T(8,128)S(1)} fusion(s32[1024]{0:T(1024)} %bitcast.424, f32[1024,9]{1,0:T(8,128)S(1)} %bitcast.269, f32[]{:T(128)} %constant.259.clone.1), kind=kCustom, calls=%fused_computation.197 | custom fusion | flops 9216 | bytes 37376 | tf_op jit(solution)/shard_map/scatter-add | solution.py:240
  282.7 1.8 multiply_bitcast_fusion.15
  284.5 2.2 fusion.161
  286.7 1.3 copy.241
  288.0 1.2 copy.242
  293.2 2.2 multiply_bitcast_fusion.14
  295.4 4.8 %pad_add_fusion.2 = f32[16,3,1024]{1,2,0:T(8,128)} fusion(f32[1,3,1024]{1,2,0:T(8,128)S(1)} %get-tuple-element.365, f32[1,3,1024]{1,2,0:T(8,128)S(1)} %get-tuple-element.366, f32[1,3,1024]{1,2,0:T(8,128)S(1)} %get-tuple-element.367, f32[1,3,1024]{1,2,0:T(8,128)S(1)} %get-tuple-element.368, f32[1,3,1024]{1,2,0:T(8,128)S(1)} %get-tuple-element.369, ...), kind=kLoop, calls=%fused_computation.153 | loop fusion | flops 737280 | bytes 393216 | tf_op jit(solution)/shard_map/transpose(jvp())/add_any | solution.py:57
  300.4 5.3 %copy.207 = f32[16,3,1024]{2,1,0:T(4,128)S(1)} copy(f32[16,3,1024]{1,2,0:T(8,128)} %pad_add_fusion.2) | data formatting | bytes 393216 | tf_op jit(solution)/shard_map/transpose(jvp())/add_any | solution.py:57
  306.0 4.8 %multiply_reduce_fusion.11 = (f32[1024]{0:T(1024)S(1)}, f32[1024]{0:T(1024)S(1)}, f32[1024]{0:T(1024)S(1)}, f32[1024]{0:T(1024)S(1)}, f32[1024]{0:T(1024)S(1)}, ...) fusion(f32[3,1024]{0,1:T(8,128)S(1)} %get-tuple-element.234, ...), kind=kLoop, calls=%fused_computation.169 | loop fusion | flops 76800 | bytes 258048 | tf_op jit(solution)/shard_map/transpose(jvp())/reduce_sum | solution.py:57
  311.9 1.2 copy.244
  313.1 1.2 copy.245
  314.3 1.2 copy.240
  315.8 7.9 %fusion.135 = (f32[1,1024]{1,0:T(1,128)S(1)}, f32[1,1024]{1,0:T(1,128)S(1)}, f32[1,1024]{1,0:T(1,128)S(1)}, f32[1,1024]{1,0:T(1,128)S(1)}, f32[1,1024]{1,0:T(1,1...) fusion(f32[1,1024]{1,0:T(1,128)S(1)} %copy.245, f32[1,1024]{1,0:T(1,128)S(1)} %copy.244, ...), kind=kLoop, calls=%fused_computation.358 | loop fusion | flops 153600 | bytes 200756 | tf_op jit(solution)/shard_map/transpose(jvp())/neg | solution.py:68
  323.7 3.2 multiply_add_fusion.9
  328.7 39.0 %all-reduce.58.cloned.1.call-done = f32[59,1024]{1,0:T(8,128)} async-done(((f32[59,1024]{1,0:T(8,128)}), f32[59,1024]{1,0:T(8,128)}) %all-reduce.58.cloned.1.call-update) | async-done | bytes 241680 | tf_op jit(solution)/shard_map/psum | solution.py:243
  367.7 1.4 broadcast_select_fusion
  371.7 12.8 %all-to-all-start.2 = ((f32[59,64,2]{0,2,1:T(2,128)}), f32[59,64,2]{0,2,1:T(2,128)S(1)}, u32[]{:S(2)}, u32[]{:S(2)}) async-start(f32[59,64,2]{0,2,1:T(2,128)} %broadcast_select_fusion.2), calls=%async_computation.2 | async-start | bytes 131072 | tf_op jit(solution)/shard_map/all_to_all | solution.py:260
  389.6 5.0 %all-to-all-done.2 = f32[59,64,2]{0,2,1:T(2,128)S(1)} async-done(((f32[59,64,2]{0,2,1:T(2,128)}), f32[59,64,2]{0,2,1:T(2,128)S(1)}, u32[]{:S(2)}, u32[]{:S(2)}) %all-to-all-start.2) | async-done | bytes 30240 | tf_op jit(solution)/shard_map/all_to_all | solution.py:260
  (355 shorter events, 67.9 us)
Async XLA Ops:
  7.2 189.5 %all-gather.2.cloned.1.call-start = ((), (), s32[]{:S(2)}) async-start(), calls=%async_computation.3 | async-start | bytes 34078720 | tf_op jit(solution)/shard_map/all_gather | solution.py:216
  27.0 56.3 %copy-start.6 = (f32[1,1024]{1,0:T(1,128)}, f32[1,1024]{1,0:T(1,128)S(1)}, u32[]{:S(2)}) copy-start(f32[1,1024]{1,0:T(1,128)S(1)} %get-tuple-element.417) | copy-start | bytes 12292
  27.1 56.3 %copy-start.8 = (f32[1,1024]{1,0:T(1,128)}, f32[1,1024]{1,0:T(1,128)S(1)}, u32[]{:S(2)}) copy-start(f32[1,1024]{1,0:T(1,128)S(1)} %get-tuple-element.418) | copy-start | bytes 12292
  27.1 56.3 %copy-start.24 = (f32[1,1024]{1,0:T(1,128)}, f32[1,1024]{1,0:T(1,128)S(1)}, u32[]{:S(2)}) copy-start(f32[1,1024]{1,0:T(1,128)S(1)} %get-tuple-element.427) | copy-start | bytes 12292
  27.1 56.2 %copy-start.26 = (f32[1,1024]{1,0:T(1,128)}, f32[1,1024]{1,0:T(1,128)S(1)}, u32[]{:S(2)}) copy-start(f32[1,1024]{1,0:T(1,128)S(1)} %get-tuple-element.428) | copy-start | bytes 12292
  27.1 56.2 %copy-start.28 = (f32[1,1024]{1,0:T(1,128)}, f32[1,1024]{1,0:T(1,128)S(1)}, u32[]{:S(2)}) copy-start(f32[1,1024]{1,0:T(1,128)S(1)} %get-tuple-element.429) | copy-start | bytes 12292
  27.1 56.2 %copy-start.30 = (f32[1,1024]{1,0:T(1,128)}, f32[1,1024]{1,0:T(1,128)S(1)}, u32[]{:S(2)}) copy-start(f32[1,1024]{1,0:T(1,128)S(1)} %get-tuple-element.430) | copy-start | bytes 12292
  27.2 56.2 %copy-start.32 = (f32[1,1024]{1,0:T(1,128)}, f32[1,1024]{1,0:T(1,128)S(1)}, u32[]{:S(2)}) copy-start(f32[1,1024]{1,0:T(1,128)S(1)} %get-tuple-element.431) | copy-start | bytes 12292
  27.2 56.2 %copy-start.34 = (f32[1,1024]{1,0:T(1,128)}, f32[1,1024]{1,0:T(1,128)S(1)}, u32[]{:S(2)}) copy-start(f32[1,1024]{1,0:T(1,128)S(1)} %get-tuple-element.432) | copy-start | bytes 12292
  30.3 40.4 %copy-start.4 = (f32[3,1024]{1,0:T(4,128)}, f32[3,1024]{1,0:T(4,128)S(1)}, u32[]{:S(2)}) copy-start(f32[3,1024]{1,0:T(4,128)S(1)} %convolution_add_fusion.2) | copy-start | bytes 36868
  43.4 44.0 %copy-start.36 = (f32[1,1024]{1,0:T(1,128)}, f32[1,1024]{1,0:T(1,128)S(1)}, u32[]{:S(2)}) copy-start(f32[1,1024]{1,0:T(1,128)S(1)} %get-tuple-element.291) | copy-start | bytes 12292
  43.4 44.0 %copy-start.38 = (f32[1,1024]{1,0:T(1,128)}, f32[1,1024]{1,0:T(1,128)S(1)}, u32[]{:S(2)}) copy-start(f32[1,1024]{1,0:T(1,128)S(1)} %get-tuple-element.293) | copy-start | bytes 12292
  43.4 44.0 %copy-start.40 = (f32[1,1024]{1,0:T(1,128)}, f32[1,1024]{1,0:T(1,128)S(1)}, u32[]{:S(2)}) copy-start(f32[1,1024]{1,0:T(1,128)S(1)} %get-tuple-element.306) | copy-start | bytes 12292
  52.4 34.1 %all-to-all-start = ((s32[64,16,1]{1,2,0:T(1,128)}), s32[64,16,1]{1,2,0:T(1,128)S(1)}, u32[]{:S(2)}, u32[]{:S(2)}) async-start(s32[64,16,1]{1,2,0:T(1,128)} %bitcast.72), calls=%async_computation | async-start | bytes 65536 | tf_op jit(solution)/shard_map/all_to_all | solution.py:217
  256.8 32.7 %copy-start.35 = (f32[1,1024]{1,0:T(1,128)S(1)}, f32[1,1024]{1,0:T(1,128)}, u32[]{:S(2)}) copy-start(f32[1,1024]{1,0:T(1,128)} %get-tuple-element.340) | copy-start | bytes 12292
  256.8 32.7 %copy-start.37 = (f32[1,1024]{1,0:T(1,128)S(1)}, f32[1,1024]{1,0:T(1,128)}, u32[]{:S(2)}) copy-start(f32[1,1024]{1,0:T(1,128)} %copy-done.36) | copy-start | bytes 12292
  256.8 32.7 %copy-start.39 = (f32[1,1024]{1,0:T(1,128)S(1)}, f32[1,1024]{1,0:T(1,128)}, u32[]{:S(2)}) copy-start(f32[1,1024]{1,0:T(1,128)} %copy-done.38) | copy-start | bytes 12292
  256.8 33.4 %copy-start.89 = (f32[1,1024]{1,0:T(1,128)S(1)}, f32[1,1024]{1,0:T(1,128)}, u32[]{:S(2)}) copy-start(f32[1,1024]{1,0:T(1,128)} %get-tuple-element.331) | copy-start | bytes 12292
  256.8 34.0 %copy-start.81 = (f32[1,1024]{1,0:T(1,128)S(1)}, f32[1,1024]{1,0:T(1,128)}, u32[]{:S(2)}) copy-start(f32[1,1024]{1,0:T(1,128)} %get-tuple-element.318) | copy-start | bytes 12292
  256.9 34.7 %copy-start.42 = (f32[1,1024]{1,0:T(1,128)S(1)}, f32[1,1024]{1,0:T(1,128)}, u32[]{:S(2)}) copy-start(f32[1,1024]{1,0:T(1,128)} %get-tuple-element.313) | copy-start | bytes 12292
  256.9 34.7 %copy-start.43 = (f32[1,1024]{1,0:T(1,128)S(1)}, f32[1,1024]{1,0:T(1,128)}, u32[]{:S(2)}) copy-start(f32[1,1024]{1,0:T(1,128)} %get-tuple-element.315) | copy-start | bytes 12292
  256.9 34.7 %copy-start.44 = (f32[1,1024]{1,0:T(1,128)S(1)}, f32[1,1024]{1,0:T(1,128)}, u32[]{:S(2)}) copy-start(f32[1,1024]{1,0:T(1,128)} %get-tuple-element.326) | copy-start | bytes 12292
  256.9 34.6 %copy-start.45 = (f32[1,1024]{1,0:T(1,128)S(1)}, f32[1,1024]{1,0:T(1,128)}, u32[]{:S(2)}) copy-start(f32[1,1024]{1,0:T(1,128)} %get-tuple-element.328) | copy-start | bytes 12292
  256.9 34.6 %copy-start.46 = (f32[1,1024]{1,0:T(1,128)S(1)}, f32[1,1024]{1,0:T(1,128)}, u32[]{:S(2)}) copy-start(f32[1,1024]{1,0:T(1,128)} %get-tuple-element.334) | copy-start | bytes 12292
  256.9 34.6 %copy-start.47 = (f32[1,1024]{1,0:T(1,128)S(1)}, f32[1,1024]{1,0:T(1,128)}, u32[]{:S(2)}) copy-start(f32[1,1024]{1,0:T(1,128)} %get-tuple-element.336) | copy-start | bytes 12292
  256.9 34.6 %copy-start.79 = (f32[1,1024]{1,0:T(1,128)S(1)}, f32[1,1024]{1,0:T(1,128)}, u32[]{:S(2)}) copy-start(f32[1,1024]{1,0:T(1,128)} %get-tuple-element.314) | copy-start | bytes 12292
  256.9 34.6 %copy-start.80 = (f32[1,1024]{1,0:T(1,128)S(1)}, f32[1,1024]{1,0:T(1,128)}, u32[]{:S(2)}) copy-start(f32[1,1024]{1,0:T(1,128)} %get-tuple-element.316) | copy-start | bytes 12292
  256.9 35.3 %copy-start.85 = (f32[1,1024]{1,0:T(1,128)S(1)}, f32[1,1024]{1,0:T(1,128)}, u32[]{:S(2)}) copy-start(f32[1,1024]{1,0:T(1,128)} %get-tuple-element.327) | copy-start | bytes 12292
  256.9 35.3 %copy-start.86 = (f32[1,1024]{1,0:T(1,128)S(1)}, f32[1,1024]{1,0:T(1,128)}, u32[]{:S(2)}) copy-start(f32[1,1024]{1,0:T(1,128)} %get-tuple-element.329) | copy-start | bytes 12292
  257.0 35.2 %copy-start.87 = (f32[1,1024]{1,0:T(1,128)S(1)}, f32[1,1024]{1,0:T(1,128)}, u32[]{:S(2)}) copy-start(f32[1,1024]{1,0:T(1,128)} %get-tuple-element.335) | copy-start | bytes 12292
  257.0 35.2 %copy-start.88 = (f32[1,1024]{1,0:T(1,128)S(1)}, f32[1,1024]{1,0:T(1,128)}, u32[]{:S(2)}) copy-start(f32[1,1024]{1,0:T(1,128)} %get-tuple-element.337) | copy-start | bytes 12292
  257.0 36.1 %copy-start.7 = (f32[1,1024]{1,0:T(1,128)S(1)}, f32[1,1024]{1,0:T(1,128)}, u32[]{:S(2)}) copy-start(f32[1,1024]{1,0:T(1,128)} %copy-done.6) | copy-start | bytes 12292
  257.0 36.1 %copy-start.9 = (f32[1,1024]{1,0:T(1,128)S(1)}, f32[1,1024]{1,0:T(1,128)}, u32[]{:S(2)}) copy-start(f32[1,1024]{1,0:T(1,128)} %copy-done.8) | copy-start | bytes 12292
  257.0 36.1 %copy-start.11 = (f32[1,1024]{1,0:T(1,128)S(1)}, f32[1,1024]{1,0:T(1,128)}, u32[]{:S(2)}) copy-start(f32[1,1024]{1,0:T(1,128)} %copy-done.10) | copy-start | bytes 12292
  257.0 36.1 %copy-start.13 = (f32[1,1024]{1,0:T(1,128)S(1)}, f32[1,1024]{1,0:T(1,128)}, u32[]{:S(2)}) copy-start(f32[1,1024]{1,0:T(1,128)} %copy-done.12) | copy-start | bytes 12292
  257.0 36.1 %copy-start.15 = (f32[1,1024]{1,0:T(1,128)S(1)}, f32[1,1024]{1,0:T(1,128)}, u32[]{:S(2)}) copy-start(f32[1,1024]{1,0:T(1,128)} %copy-done.14) | copy-start | bytes 12292
  257.0 36.1 %copy-start.17 = (f32[1,1024]{1,0:T(1,128)S(1)}, f32[1,1024]{1,0:T(1,128)}, u32[]{:S(2)}) copy-start(f32[1,1024]{1,0:T(1,128)} %copy-done.16) | copy-start | bytes 12292
  257.0 36.1 %copy-start.19 = (f32[1,1024]{1,0:T(1,128)S(1)}, f32[1,1024]{1,0:T(1,128)}, u32[]{:S(2)}) copy-start(f32[1,1024]{1,0:T(1,128)} %copy-done.18) | copy-start | bytes 12292
  257.0 36.1 %copy-start.21 = (f32[1,1024]{1,0:T(1,128)S(1)}, f32[1,1024]{1,0:T(1,128)}, u32[]{:S(2)}) copy-start(f32[1,1024]{1,0:T(1,128)} %copy-done.20) | copy-start | bytes 12292
  257.1 36.1 %copy-start.23 = (f32[1,1024]{1,0:T(1,128)S(1)}, f32[1,1024]{1,0:T(1,128)}, u32[]{:S(2)}) copy-start(f32[1,1024]{1,0:T(1,128)} %copy-done.22) | copy-start | bytes 12292
  257.1 36.1 %copy-start.25 = (f32[1,1024]{1,0:T(1,128)S(1)}, f32[1,1024]{1,0:T(1,128)}, u32[]{:S(2)}) copy-start(f32[1,1024]{1,0:T(1,128)} %copy-done.24) | copy-start | bytes 12292
  257.1 36.1 %copy-start.27 = (f32[1,1024]{1,0:T(1,128)S(1)}, f32[1,1024]{1,0:T(1,128)}, u32[]{:S(2)}) copy-start(f32[1,1024]{1,0:T(1,128)} %copy-done.26) | copy-start | bytes 12292
  257.1 36.1 %copy-start.29 = (f32[1,1024]{1,0:T(1,128)S(1)}, f32[1,1024]{1,0:T(1,128)}, u32[]{:S(2)}) copy-start(f32[1,1024]{1,0:T(1,128)} %copy-done.28) | copy-start | bytes 12292
  257.1 36.1 %copy-start.31 = (f32[1,1024]{1,0:T(1,128)S(1)}, f32[1,1024]{1,0:T(1,128)}, u32[]{:S(2)}) copy-start(f32[1,1024]{1,0:T(1,128)} %copy-done.30) | copy-start | bytes 12292
  257.1 36.1 %copy-start.33 = (f32[1,1024]{1,0:T(1,128)S(1)}, f32[1,1024]{1,0:T(1,128)}, u32[]{:S(2)}) copy-start(f32[1,1024]{1,0:T(1,128)} %copy-done.32) | copy-start | bytes 12292
  258.2 16.6 %all-to-all-start.1 = ((f32[64,1,144]{2,1,0:T(1,128)}), f32[64,1,144]{2,1,0:T(1,128)S(1)}, u32[]{:S(2)}, u32[]{:S(2)}) async-start(f32[64,1,144]{2,1,0:T(1,128)} %reshape.755), calls=%async_computation.1 | async-start | bytes 131072 | tf_op jit(solution)/shard_map/all_to_all | solution.py:239
  264.7 103.0 %all-reduce.58.cloned.1.call-start = ((), (), s32[]{:S(2)}) async-start(), calls=%async_computation.4 | async-start | bytes 524288 | tf_op jit(solution)/shard_map/psum | solution.py:243
  371.7 22.9 %all-to-all-start.2 = ((f32[59,64,2]{0,2,1:T(2,128)}), f32[59,64,2]{0,2,1:T(2,128)S(1)}, u32[]{:S(2)}, u32[]{:S(2)}) async-start(f32[59,64,2]{0,2,1:T(2,128)} %broadcast_select_fusion.2), calls=%async_computation.2 | async-start | bytes 131072 | tf_op jit(solution)/shard_map/all_to_all | solution.py:260
  (54 other events, 752.5 us)
Sparse Core Ops, SparseCore 0:
  50.0 146.6 all-gather.1
  328.7 39.0 all-reduce.57
where the time goes:
time: 406 us; the launch traced here: 404 us
  waiting for transfers between devices  162 us (40%)
  other arithmetic  85.2 us (21%)
  local copies, waits for them, and re-layouts  73.1 us (18%)
  starting transfers between devices  32.4 us (8%)
  between operations  28.4 us (7%)
  matrix products  22.6 us (6%)
    all_gather x1, waiting for transfers between devices, shards(): everything = lax.all_gather(projected, 'gauss', axis=1, tiled=True)  109 us
    psum x1, waiting for transfers between devices, shards(): gradient = lax.psum(local_grads, 'view')  39 us
    gather x1, local copies, waits for them, and re-layouts, shards(): received = everything[:, source]  13.3 us
    slice x15, local copies, waits for them, and re-layouts, harmonic(): result = result + factors[index_k][None, :] * coeffs[index_k]  13.1 us
    all_to_all x1, starting transfers between devices, shards(): lax.all_to_all(slot_list, 'gauss', split_axis=0, concat_axis=0, tiled=True)  13 us
    unnamed x200, local copies, waits for them, and re-layouts  12.8 us
    all_to_all x1, starting transfers between devices, shards(): lax.all_to_all(outgoing, 'gauss', split_axis=1, concat_axis=1, tiled=True)  12.8 us
    dot_general x8, matrix products, render_group(): jnp.einsum('gpj,ji->gpi', log_keep, strict_upper, precision=TOP_PRECISION)  10.7 us
  transfers between devices with their start and end apart: 5, of which 4 were waited for; matrix products, arithmetic and copies ran while one was open for 7% of the time, Pallas kernels for 0%

commit v1 on v0

v1 whole, which is shorter than its diff:
```python
import math

import jax
import jax.numpy as jnp
from jax import lax
from jax.experimental import pallas as pl
from jax.experimental.pallas import tpu as pltpu
from jax.sharding import PartitionSpec as P

F32 = jnp.float32
BF16 = jnp.bfloat16
I32 = jnp.int32
PEERS = 64
LOCAL = 1024
CAP = 16
VIEWS = 4
TILES = 4
ACROSS = 16
ROWS = 16

SH_ZERO = 0.28209479177387814
SH_ONE = 0.4886025119029199
SH_TWO = (
    1.0925484305920792,
    -1.0925484305920792,
    0.31539156525252005,
    -1.0925484305920792,
    0.5462742152960396,
)
SH_THREE = (
    -0.5900435899266435,
    2.890611442640554,
    -0.4570457994644658,
    0.3731763325901154,
    -0.4570457994644658,
    1.445305721320277,
    -0.5900435899266435,
)
BIAS_ONE = 1.0 - math.exp(1000.0 * math.log(0.9))
BIAS_TWO = 1.0 - math.exp(1000.0 * math.log(0.999))
VMEM_LIMIT = 16 * 1024 * 1024


def split(x, parts):
    out = []
    for index in range(parts):
        piece = x.astype(BF16)
        out.append(piece)
        if index + 1 < parts:
            x = x - piece.astype(F32)
    return out


def low_onehot(idx):
    lane = lax.broadcasted_iota(I32, (128, idx.shape[1]), 0)
    return jnp.where(lane == (idx & 127), 1.0, 0.0).astype(BF16)


def take_columns(table, idx, hot):
    rows = table.shape[0]
    high = idx >> 7
    parts = split(table, 3)
    lhs = jnp.concatenate(
        [
            jnp.concatenate([p[:, c * 128 : (c + 1) * 128] for p in parts], axis=1)
            for c in range(8)
        ],
        axis=0,
    )
    rhs = jnp.concatenate([hot, hot, hot], axis=0)
    wide = jnp.dot(lhs, rhs, preferred_element_type=F32)
    total = None
    for c in range(8):
        term = jnp.where(high == c, wide[c * rows : (c + 1) * rows], 0.0)
        total = term if total is None else total + term
    return total


def add_columns(values, idx, hot):
    rows = values.shape[0]
    high = idx >> 7
    masked = jnp.concatenate([jnp.where(high == c, values, 0.0) for c in range(8)], axis=0)
    lhs = jnp.concatenate(split(masked, 3), axis=1)
    rhs = jnp.concatenate([hot, hot, hot], axis=1)
    wide = lax.dot_general(lhs, rhs, (((1,), (1,)), ((), ())), preferred_element_type=F32)
    return jnp.concatenate([wide[c * rows : (c + 1) * rows] for c in range(8)], axis=1)


def pack_peers(table):
    pieces = [table[:, k * PEERS : (k + 1) * PEERS] for k in range(CAP)]
    return jnp.concatenate(pieces, axis=0).T


def unpack_peers(block):
    flat = block.T
    return jnp.concatenate([flat[k * ROWS : (k + 1) * ROWS] for k in range(CAP)], axis=1)


def slots_by_rank(slots):
    source = lax.broadcasted_iota(I32, (128, LOCAL), 0)
    col = lax.broadcasted_iota(I32, (128, LOCAL), 1)
    pick = jnp.where(source == (col & 7) * 16 + (col >> 6), 1.0, 0.0).astype(BF16)
    upper = jnp.dot((slots >> 5).astype(F32).astype(BF16), pick, preferred_element_type=F32)
    lower = jnp.dot((slots & 31).astype(F32).astype(BF16), pick, preferred_element_type=F32)
    wide = upper * 32.0 + lower
    row = lax.broadcasted_iota(I32, (8, LOCAL), 0)
    column = lax.broadcasted_iota(I32, (8, LOCAL), 1)
    kept = jnp.where(row == ((column >> 3) & 7), wide, 0.0)
    return jnp.sum(kept, axis=0, keepdims=True).astype(I32)


def covariance(log_scale, quat):
    norm = jnp.sqrt(quat[0] * quat[0] + quat[1] * quat[1] + quat[2] * quat[2] + quat[3] * quat[3])
    quat_w, quat_x, quat_y, quat_z = [q / norm for q in quat]
    orient = [
        [
            1.0 - 2.0 * (quat_y * quat_y + quat_z * quat_z),
            2.0 * (quat_x * quat_y - quat_w * quat_z),
            2.0 * (quat_x * quat_z + quat_w * quat_y),
        ],
        [
            2.0 * (quat_x * quat_y + quat_w * quat_z),
            1.0 - 2.0 * (quat_x * quat_x + quat_z * quat_z),
            2.0 * (quat_y * quat_z - quat_w * quat_x),
        ],
        [
            2.0 * (quat_x * quat_z - quat_w * quat_y),
            2.0 * (quat_y * quat_z + quat_w * quat_x),
            1.0 - 2.0 * (quat_x * quat_x + quat_y * quat_y),
        ],
    ]
    scales = [jnp.exp(s) for s in log_scale]
    factor = [[orient[i][j] * scales[j] for j in range(3)] for i in range(3)]

    def entry(i, j):
        return (
            factor[i][0] * factor[j][0] + factor[i][1] * factor[j][1] + factor[i][2] * factor[j][2]
        )

    return [entry(0, 0), entry(0, 1), entry(0, 2), entry(1, 1), entry(1, 2), entry(2, 2)]


def harmonics(dir_x, dir_y, dir_z):
    sq_x, sq_y, sq_z = (dir_x * dir_x, dir_y * dir_y, dir_z * dir_z)
    return [
        -SH_ONE * dir_y,
        SH_ONE * dir_z,
        -SH_ONE * dir_x,
        SH_TWO[0] * dir_x * dir_y,
        SH_TWO[1] * dir_y * dir_z,
        SH_TWO[2] * (2.0 * sq_z - sq_x - sq_y),
        SH_TWO[3] * dir_x * dir_z,
        SH_TWO[4] * (sq_x - sq_y),
        SH_THREE[0] * dir_y * (3.0 * sq_x - sq_y),
        SH_THREE[1] * dir_x * dir_y * dir_z,
        SH_THREE[2] * dir_y * (4.0 * sq_z - sq_x - sq_y),
        SH_THREE[3] * dir_z * (2.0 * sq_z - 3.0 * sq_x - 3.0 * sq_y),
        SH_THREE[4] * dir_x * (4.0 * sq_z - sq_x - sq_y),
        SH_THREE[5] * dir_z * (sq_x - sq_y),
        SH_THREE[6] * dir_x * (sq_x - 3.0 * sq_y),
    ]


def view_rows(position, sigma, coeffs, cam):
    rot = [cam[0:3], cam[3:6], cam[6:9]]
    offset = cam[9:12]
    focal_x, focal_y, centre_x, centre_y = cam[12:16]
    cam_x, cam_y, cam_z = [
        rot[i][0] * position[0] + rot[i][1] * position[1] + rot[i][2] * position[2] + offset[i]
        for i in range(3)
    ]
    inverse_z = 1.0 / cam_z
    mean_u = focal_x * cam_x * inverse_z + centre_x
    mean_w = focal_y * cam_y * inverse_z + centre_y
    jac_a0 = focal_x * inverse_z
    jac_a2 = -focal_x * cam_x * inverse_z * inverse_z
    jac_b1 = focal_y * inverse_z
    jac_b2 = -focal_y * cam_y * inverse_z * inverse_z
    row_a = [jac_a0 * rot[0][i] + jac_a2 * rot[2][i] for i in range(3)]
    row_b = [jac_b1 * rot[1][i] + jac_b2 * rot[2][i] for i in range(3)]
    full = [
        [sigma[0], sigma[1], sigma[2]],
        [sigma[1], sigma[3], sigma[4]],
        [sigma[2], sigma[4], sigma[5]],
    ]

    def through(row):
        return [full[i][0] * row[0] + full[i][1] * row[1] + full[i][2] * row[2] for i in range(3)]

    def dot3(left, right):
        return left[0] * right[0] + left[1] * right[1] + left[2] * right[2]

    sigma_a = through(row_a)
    sigma_b = through(row_b)
    cov_aa = dot3(row_a, sigma_a) + 0.3
    cov_ab = dot3(row_a, sigma_b)
    cov_bb = dot3(row_b, sigma_b) + 0.3
    determinant = cov_aa * cov_bb - cov_ab * cov_ab
    inverse_det = 1.0 / determinant
    ray = [
        position[i] + (rot[0][i] * offset[0] + rot[1][i] * offset[1] + rot[2][i] * offset[2])
        for i in range(3)
    ]
    inverse_norm = 1.0 / jnp.sqrt(dot3(ray, ray))
    basis = harmonics(*[r * inverse_norm for r in ray])
    colours = []
    for channel in range(3):
        total = SH_ZERO * coeffs[channel]
        for index in range(15):
            total = total + basis[index] * coeffs[3 + 3 * index + channel]
        colours.append(jnp.maximum(total + 0.5, 0.0))
    return [
        mean_u,
        mean_w,
        cov_bb * inverse_det,
        -cov_ab * inverse_det,
        cov_aa * inverse_det,
    ] + colours


def send_kernel(params_ref, slots_ref, camera_ref, out_ref, order_ref):
    dense = params_ref[...].reshape(59, 8, 128)
    rows = [dense[i] for i in range(59)]
    cam = [camera_ref[0, i] for i in range(16)]
    sigma = covariance(rows[3:6], rows[6:10])
    seen = view_rows(rows[0:3], sigma, rows[11:59], cam)
    opacity = 1.0 / (1.0 + jnp.exp(-rows[10]))
    listed = seen[0:5] + [opacity] + seen[5:8]
    blank = jnp.zeros((8, 128), F32)
    table = jnp.stack(listed + [blank] * (ROWS - 9)).reshape(ROWS, LOCAL)
    order = slots_by_rank(slots_ref[...])
    order_ref[...] = order
    out_ref[...] = pack_peers(take_columns(table, order, low_onehot(order)))


def render_kernel(recv_ref, lists_ref, tiles_ref, target_ref, out_ref, alpha_ref, grad_ref):
    table = unpack_peers(recv_ref[...])
    entries = lists_ref[...]
    idx = jnp.where(entries < 0, -1, (entries & 15) * PEERS + (entries >> 4))
    hot = low_onehot(idx)
    listed = take_columns(table, idx, hot)
    iota_r = lax.broadcasted_iota(I32, (256, 256), 0)
    iota_c = lax.broadcasted_iota(I32, (256, 256), 1)
    before_mask = jnp.where(iota_r < iota_c, 1.0, 0.0).astype(BF16)
    after_mask = jnp.where(iota_r > iota_c, 1.0, 0.0).astype(BF16)
    steps = lax.broadcasted_iota(I32, (16, 256), 0).astype(F32)
    results = []
    for tile in range(TILES):
        here = listed[:, tile * 256 : (tile + 1) * 256]
        number = tiles_ref[0, tile]
        left = ((number & (ACROSS - 1)) * 16).astype(F32)
        top = ((number >> 4) * 16).astype(F32)
        con_a, con_b, con_c, opacity = here[2:3], here[3:4], here[4:5], here[5:6]
        off_u = (steps + left + 0.5) - here[0:1]
        off_w = (steps + top + 0.5) - here[1:2]
        quad_u = -0.5 * con_a * off_u * off_u
        cross = -con_b * off_u
        quad_w = -0.5 * con_c * off_w * off_w
        for j in range(16):
            exponent = quad_u + quad_w[j : j + 1] + cross * off_w[j : j + 1]
            alpha_ref[j * 16 : (j + 1) * 16, :] = opacity * jnp.exp(exponent)
        alpha = alpha_ref[...]
        keep = 1.0 - alpha
        logs = split(jnp.log(keep), 2)
        before = jnp.dot(logs[0], before_mask, preferred_element_type=F32) + jnp.dot(
            logs[1], before_mask, preferred_element_type=F32
        )
        weight = jnp.exp(before) * alpha
        weights = split(weight, 2)
        colour = here[6:9]
        colour_parts = split(colour, 3)
        stacked = jnp.concatenate(
            [p.astype(F32) for p in colour_parts] + [jnp.zeros((7, 256), F32)], axis=0
        ).astype(BF16)
        nt = (((1,), (1,)), ((), ()))
        summed = lax.dot_general(
            stacked, weights[0], nt, preferred_element_type=F32
        ) + lax.dot_general(stacked, weights[1], nt, preferred_element_type=F32)
        rendered = summed[0:3] + summed[3:6] + summed[6:9]
        residual = rendered - target_ref[tile]
        residual_parts = [p.astype(F32) for p in split(residual, 3)]
        colour_wide = [p.astype(F32) for p in colour_parts]
        pairs = ((0, 0), (0, 1), (1, 0), (1, 1), (0, 2), (2, 0))
        blank = jnp.zeros((14, 256), F32)
        left_side = jnp.concatenate([residual_parts[a] for a, _ in pairs] + [blank], axis=0)
        right_side = jnp.concatenate([colour_wide[b] for _, b in pairs] + [blank], axis=0)
        pull = lax.dot_general(
            left_side.astype(BF16),
            right_side.astype(BF16),
            (((0,), (0,)), ((), ())),
            preferred_element_type=F32,
        )
        weighted = pull * weight
        flows = split(weighted, 2)
        after = jnp.dot(flows[0], after_mask, preferred_element_type=F32) + jnp.dot(
            flows[1], after_mask, preferred_element_type=F32
        )
        grad_ref[...] = weighted - after * (alpha / keep)
        stacked_res = jnp.concatenate(residual_parts + [jnp.zeros((7, 256), F32)], axis=0).astype(
            BF16
        )
        colour_sum = jnp.dot(stacked_res, weights[0], preferred_element_type=F32) + jnp.dot(
            stacked_res, weights[1], preferred_element_type=F32
        )
        colour_grad = colour_sum[0:3] + colour_sum[3:6] + colour_sum[6:9]
        zeroth = first = second = None
        for j in range(16):
            piece = grad_ref[j * 16 : (j + 1) * 16, :]
            lifted = piece * off_w[j : j + 1]
            twice = lifted * off_w[j : j + 1]
            zeroth = piece if zeroth is None else zeroth + piece
            first = lifted if first is None else first + lifted
            second = twice if second is None else second + twice

        def over(values):
            return jnp.sum(values, axis=0, keepdims=True)

        along = zeroth * off_u
        m_00, m_10, m_20 = over(zeroth), over(along), over(along * off_u)
        m_01, m_11, m_02 = over(first), over(first * off_u), over(second)
        results.append(
            jnp.concatenate(
                [
                    con_a * m_10 + con_b * m_01,
                    con_c * m_01 + con_b * m_10,
                    -0.5 * m_20,
                    -m_11,
                    -0.5 * m_02,
                    m_00,
                    colour_grad,
                    jnp.zeros((ROWS - 9, 256), F32),
                ],
                axis=0,
            )
        )
    grads = jnp.concatenate(results, axis=1)
    out_ref[...] = pack_peers(add_columns(grads, idx, hot))


def owner_kernel(recv_ref, order_ref, camera_ref, out_ref):
    values = unpack_peers(recv_ref[...])
    order = order_ref[...]
    out_ref[...] = add_columns(values, order, low_onehot(order))
    for i in range(16):
        out_ref[9 + i // 8 : 10 + i // 8, (i % 8) * 128 : (i % 8 + 1) * 128] = jnp.full(
            (1, 128), camera_ref[0, i], F32
        )


def log_one_plus(t):
    s = t / (2.0 + t)
    square = s * s
    total = jnp.full_like(s, 1.0 / 17.0)
    for odd in (15, 13, 11, 9, 7, 5, 3, 1):
        total = total * square + 1.0 / odd
    return 2.0 * s * total


def one_minus_exp(x):
    small = jnp.ones_like(x)
    for n in range(10, 1, -1):
        small = 1.0 + small * x * (1.0 / n)
    return jnp.where(x > -0.5, -x * small, 1.0 - jnp.exp(x))


def rates_column():
    row = lax.broadcasted_iota(I32, (59, 1), 0)
    rate = jnp.where(row < 14, 0.0025, 0.000125)
    rate = jnp.where(row < 11, 0.05, rate)
    rate = jnp.where(row < 10, 0.001, rate)
    rate = jnp.where(row < 6, 0.005, rate)
    return jnp.where(row < 3, 0.00016, rate)


def tree_sum(values):
    return (values[0] + values[1]) + (values[2] + values[3])


def step_kernel(
    params_ref,
    first_ref,
    second_ref,
    own_ref,
    near_ref,
    far_ref,
    last_ref,
    sources_ref,
    targets_ref,
    spread_ref,
    new_first_ref,
    new_second_ref,
    gradient_ref,
    out_ref,
):
    dense = params_ref[...].reshape(59, 8, 128)
    rows = [dense[i] for i in range(59)]
    sigma, pull_sigma = jax.vjp(covariance, rows[3:6], rows[6:10])
    position, coeffs = rows[0:3], rows[11:59]
    pos_parts, sigma_parts, coeff_parts, opacity_parts = [], [], [], []
    for ref in (own_ref, near_ref, far_ref, last_ref):
        got = ref[...].reshape(ROWS, 8, 128)
        cam = [jnp.broadcast_to(got[9 + i // 8, i % 8 : i % 8 + 1, :], (8, 128)) for i in range(16)]
        _, pull = jax.vjp(lambda p, s, c: view_rows(p, s, c, cam), position, sigma, coeffs)
        d_pos, d_sigma, d_coeff = pull([got[i] for i in (0, 1, 2, 3, 4, 6, 7, 8)])
        pos_parts.append(d_pos)
        sigma_parts.append(d_sigma)
        coeff_parts.append(d_coeff)
        opacity_parts.append(got[5])
    d_pos = [tree_sum([p[i] for p in pos_parts]) for i in range(3)]
    d_sigma = [tree_sum([p[i] for p in sigma_parts]) for i in range(6)]
    d_coeff = [tree_sum([p[i] for p in coeff_parts]) for i in range(48)]
    d_scale, d_quat = pull_sigma(d_sigma)
    opacity = 1.0 / (1.0 + jnp.exp(-rows[10]))
    d_logit = tree_sum(opacity_parts) * (1.0 - opacity)
    gradient = jnp.stack(d_pos + list(d_scale) + list(d_quat) + [d_logit] + d_coeff).reshape(
        59, LOCAL
    )
    gradient_ref[...] = gradient
    first = 0.9 * first_ref[...] + 0.1 * gradient
    second = 0.999 * second_ref[...] + 0.001 * gradient * gradient
    stepped = params_ref[...] - rates_column() * (first / BIAS_ONE) / (
        jnp.sqrt(second / BIAS_TWO) + 1e-15
    )
    sources = sources_ref[...]
    targets = targets_ref[...]
    ones = jnp.ones((8, 128), F32)
    source_hot = low_onehot(sources)
    counts = add_columns(ones, sources, source_hot)[0:1]
    landing = add_columns(ones, targets, low_onehot(targets))[0:1]
    sampled = counts > 0.5
    cleared = (counts + landing) > 0.5
    logit = stepped[10:11]
    soft = jnp.maximum(logit, 0.0) + log_one_plus(jnp.exp(-jnp.abs(logit)))
    share = -soft / (counts + 1.0)
    shared_logit = jnp.log(one_minus_exp(share)) - share
    row = lax.broadcasted_iota(I32, (59, LOCAL), 0)
    spread = jnp.where((row == 10) & sampled, shared_logit, stepped)
    spread_ref[...] = spread
    new_first_ref[...] = jnp.where(cleared, 0.0, first)
    new_second_ref[...] = jnp.where(cleared, 0.0, second)
    table = jnp.concatenate([spread, jnp.ones((5, LOCAL), F32)], axis=0)
    moved = take_columns(table, sources, source_hot)
    out_ref[...] = jnp.concatenate([moved[:, 0:PEERS], moved[:, PEERS : 2 * PEERS]], axis=0).T


def landing_kernel(recv_ref, targets_ref, spread_ref, out_ref):
    flat = recv_ref[...].T
    moved = jnp.concatenate([flat[0:64], flat[64:128]], axis=1)
    targets = targets_ref[...]
    placed = add_columns(moved, targets, low_onehot(targets))
    out_ref[...] = jnp.where(placed[59:60] > 0.5, placed[0:59], spread_ref[...])


def by_rank(pairs):
    return jnp.transpose(pairs.reshape(PEERS, 2)).reshape(1, 2 * PEERS)


def call(kernel, shapes, smem=(), scratch=(), count=0):
    vmem = pl.BlockSpec(memory_space=pltpu.VMEM)
    scalar = pl.BlockSpec(memory_space=pltpu.SMEM)
    out_shape = [jax.ShapeDtypeStruct(shape, dtype) for shape, dtype in shapes]
    return pl.pallas_call(
        kernel,
        out_shape=out_shape,
        in_specs=[scalar if i in smem else vmem for i in range(count)],
        out_specs=[vmem] * len(out_shape),
        scratch_shapes=list(scratch),
        compiler_params=pltpu.CompilerParams(vmem_limit_bytes=VMEM_LIMIT),
    )


def exchange(block):
    return lax.all_to_all(block, "gauss", split_axis=0, concat_axis=0, tiled=True)


def shards(
    params,
    first_moment,
    second_moment,
    cameras,
    target,
    tile_index,
    tile_lists,
    send_slots,
    reloc_send,
    reloc_recv,
):
    outgoing, order = call(
        send_kernel,
        [((PEERS, CAP * ROWS), F32), ((1, LOCAL), I32)],
        smem=(2,),
        count=3,
    )(params, send_slots.reshape(8, 128), cameras)
    received = exchange(outgoing)
    (row_grads,) = call(
        render_kernel,
        [((PEERS, CAP * ROWS), F32)],
        smem=(2,),
        scratch=[pltpu.VMEM((256, 256), F32), pltpu.VMEM((256, 256), F32)],
        count=4,
    )(received, tile_lists.reshape(1, LOCAL), tile_index, target.reshape(TILES, 3, 256))
    returned = exchange(row_grads)
    (own,) = call(owner_kernel, [((ROWS, LOCAL), F32)], smem=(2,), count=3)(
        returned, order, cameras
    )
    others = [
        lax.ppermute(own, "view", [(i, i ^ flip) for i in range(VIEWS)]) for flip in (1, 2, 3)
    ]
    sources = by_rank(reloc_send)
    targets = by_rank(reloc_recv)
    whole = ((59, LOCAL), F32)
    spread, new_first, new_second, gradient, moving = call(
        step_kernel,
        [whole, whole, whole, whole, ((PEERS, 128), F32)],
        count=9,
    )(params, first_moment, second_moment, own, *others, sources, targets)
    arrived = exchange(moving)
    (new_params,) = call(landing_kernel, [whole], count=3)(arrived, targets, spread)
    return (new_params, new_first, new_second, gradient)


def solution(mesh):
    in_specs = (
        P(None, "gauss"),
        P(None, "gauss"),
        P(None, "gauss"),
        P("view", None),
        P("view", "gauss", None, None),
        P("view", "gauss"),
        P("view", "gauss", None),
        P("view", "gauss", None),
        P("gauss", None),
        P("gauss", None),
    )
    out_specs = (P(None, "gauss"), P(None, "gauss"), P(None, "gauss"), P(None, "gauss"))
    return jax.shard_map(shards, mesh=mesh, in_specs=in_specs, out_specs=out_specs, check_vma=False)
```

time: 406 us -> 74.2 us (0.18)
  waiting for transfers between devices: 162 us -> 11.5 us
  other arithmetic: 85.2 us -> 1.33 us
  local copies, waits for them, and re-layouts: 73.1 us -> 4.87 us
  blocking collectives: 0 us -> 28.7 us
  between operations: 28.4 us -> 0.79 us
  matrix products: 22.6 us -> 0 us
  starting transfers between devices: 32.4 us -> 16.6 us
  Pallas kernels: 0 us -> 10 us
    all_gather x1 -> x0, waiting for transfers between devices: 109 us -> none  [shards(): everything = lax.all_gather(projected, 'gauss', axis=1, tiled=True)]
    psum x1 -> x0, waiting for transfers between devices: 39 us -> none  [shards(): gradient = lax.psum(local_grads, 'view')]
    all_to_all x0 -> x2, blocking collectives: none -> 28.7 us  [exchange(): lax.all_to_all(block, 'gauss', split_axis=0, concat_axis=0, tiled=True)]
    dot_general x22 -> x0, matrix products: 22.6 us -> none  [the longest x8 10.7 us: render_group(): jnp.einsum('gpj,ji->gpi', log_keep, strict_upper, precision=TOP_PRECISION)]
    all_to_all x3 -> x1, starting transfers between devices: 32.3 us -> 13.1 us  [exchange(): lax.all_to_all(block, 'gauss', split_axis=0, concat_axis=0, tiled=True)]
    gather x6 -> x0, local copies, waits for them, and re-layouts: 16.4 us -> none  [the longest x1 13.3 us: shards(): received = everything[:, source]]
    slice x22 -> x0, local copies, waits for them, and re-layouts: 16.1 us -> none  [the longest x15 13.1 us: harmonic(): result = result + factors[index_k][None, :] * coeffs[index_k]]
    scatter-add x3 -> x0, other arithmetic: 13.4 us -> none  [the longest x2 7.08 us: render_group(): listed = received[:, safe_index]]
  transfers between devices with their start and end apart: 5 -> 4, of which waited for: 4 -> 2; matrix products, arithmetic and copies ran while one was open for 7% -> 3% of each run, Pallas kernels for 0% -> 0%
where the time goes in v1:
time: 74.2 us; the launch traced here: 73.9 us
  blocking collectives  28.7 us (39%)
  starting transfers between devices  16.6 us (22%)
  waiting for transfers between devices  11.5 us (15%)
  Pallas kernels  10 us (13%)
  local copies, waits for them, and re-layouts  4.87 us (7%)
  other arithmetic  1.33 us (2%)
  between operations  0.79 us (1%)
    all_to_all x2, blocking collectives, exchange(): lax.all_to_all(block, 'gauss', split_axis=0, concat_axis=0, tiled=True)  28.7 us
    all_to_all x1, starting transfers between devices, exchange(): lax.all_to_all(block, 'gauss', split_axis=0, concat_axis=0, tiled=True)  13.1 us
    all_to_all x1, waiting for transfers between devices, exchange(): lax.all_to_all(block, 'gauss', split_axis=0, concat_axis=0, tiled=True)  10 us
    pallas_call x1, Pallas kernels, shards(): call(render_kernel, [((PEERS, CAP * ROWS), F32)], smem=(2,), scratch=[plt...  4.74 us
    unnamed x27, local copies, waits for them, and re-layouts  3.51 us
    ppermute x3, starting transfers between devices, shards(): lax.ppermute(own, 'view', [(i, i ^ flip) for i in range(VIEWS)])  3.5 us
    pallas_call x1, Pallas kernels, shards(): call(step_kernel, [whole, whole, whole, whole, ((PEERS, 128), F32)], coun...  1.87 us
    ppermute x3, waiting for transfers between devices, shards(): lax.ppermute(own, 'view', [(i, i ^ flip) for i in range(VIEWS)])  1.49 us
  transfers between devices with their start and end apart: 4, of which 2 were waited for; matrix products, arithmetic and copies ran while one was open for 3% of the time, Pallas kernels for 0%

profile of v1, /device:TPU:1, one launch (start us, length us, event | category | flops | bytes accessed | tf_op | source)
XLA Modules:
  0.0 73.9 jit_solution(8701133272649220628)
XLA Ops:
  0.6 0.0 copy-start.5
  0.6 0.6 copy-done.5
  1.3 0.0 copy-start
  1.3 0.9 %copy-done = f32[59,1024]{1,0:T(8,128)S(1)} copy-done((f32[59,1024]{1,0:T(8,128)S(1)}, f32[59,1024]{1,0:T(8,128)}, u32[]{:S(2)}) %copy-start) | copy-done | bytes 241688
  2.2 0.0 copy-start.4
  2.2 0.7 copy-done.4
  2.9 1.2 %shard_map.129 = (f32[64,256]{1,0:T(8,128)S(1)}, s32[1,1024]{1,0:T(1,128)S(1)}) custom-call(f32[59,1024]{1,0:T(8,128)S(1)} %copy-done, s32[8,128]{1,0:T(8,128)S(1)} %bitcast.28, f32[1,16]{1,0:T(1,128)S(1)} %copy-done.5), custom_call_target="tpu_custom_call" | custom-call | tf_op jit(solution)/shard_map/pallas_call | solution.py:488
  4.2 0.7 copy.20
  4.9 0.0 copy-start.8
  4.9 0.0 copy-start.7
  4.9 13.1 %all-to-all-start = ((f32[64,1,256]{2,1,0:T(1,128)}), f32[64,1,256]{2,1,0:T(1,128)S(1)}, u32[]{:S(2)}, u32[]{:S(2)}) async-start(f32[64,1,256]{2,1,0:T(1,128)} %copy.20), calls=%async_computation | async-start | bytes 131072 | tf_op jit(solution)/shard_map/all_to_all | solution.py:473
  18.0 0.0 copy-done.8
  18.0 0.0 copy-done.7
  18.1 10.0 %all-to-all-done = f32[64,1,256]{2,1,0:T(1,128)S(1)} async-done(((f32[64,1,256]{2,1,0:T(1,128)}), f32[64,1,256]{2,1,0:T(1,128)S(1)}, u32[]{:S(2)}, u32[]{:S(2)}) %all-to-all-start) | async-done | bytes 65568 | tf_op jit(solution)/shard_map/all_to_all | solution.py:473
  28.1 0.0 copy-start.6
  28.1 0.7 copy-done.6
  28.8 0.0 copy-start.3
  28.8 4.7 %shard_map.130 = f32[64,256]{1,0:T(8,128)S(1)} custom-call(f32[64,256]{1,0:T(8,128)S(1)} %bitcast.20, s32[1,1024]{1,0:T(1,128)S(1)} %bitcast.27, s32[1,4]{1,0:T(1,128)S(1)} %copy-done.6, f32[4,3,256]{2,1,0:T(4,128)S(1)} %bitcast.24), custom_call_target="tpu_custom_call" | custom-call | tf_op jit(solution)/shard_map/pallas_call | solution.py:495
  33.5 0.0 copy-start.9
  33.5 0.0 copy-start.10
  33.5 0.1 copy.22
  33.6 0.0 copy-start.1
  33.6 0.0 copy-start.2
  33.6 13.9 %all_to_all.33 = f32[64,1,256]{2,1,0:T(1,128)S(1)} all-to-all(f32[64,1,256]{2,1,0:T(1,128)S(1)} %copy.22), channel_id=1, replica_groups=mesh['gauss'=64,'view'=4] {'gauss'}, dimensions={0} | all-to-all | bytes 131072 | tf_op jit(solution)/shard_map/all_to_all | solution.py:473
  47.5 1.1 %shard_map.131.own_ref = f32[16,1024]{1,0:T(8,128)S(1)} custom-call(f32[64,256]{1,0:T(8,128)S(1)} %bitcast.22, s32[1,1024]{1,0:T(1,128)S(1)} %get-tuple-element.12.order_ref, f32[1,16]{1,0:T(1,128)S(1)} %copy-done.5), custom_call_target="tpu_custom_call" | custom-call | tf_op jit(solution)/shard_map/pallas_call | solution.py:503
  48.6 2.8 %collective-permute-start.2 = (f32[16,1024]{1,0:T(8,128)S(1)}, f32[16,1024]{1,0:T(8,128)S(1)}, u32[]{:S(2)}, u32[]{:S(2)}) collective-permute-start(f32[16,1024]{1,0:T(8,128)S(1)} %shard_map.131.own_ref), channel_id=1, source_target_pairs={{0,3},{1,2},{2,1},{3,0},{4,7},{5,6},{6,5},{7,4},{8,11},{9,10},{10,... | collective-permute-start | bytes 196616 | tf_op jit(solution)/shard_map/ppermute | solution.py:507
  51.4 0.3 collective-permute-start.1
  51.8 0.3 collective-permute-start
  52.1 0.5 broadcast.6
  52.6 0.0 copy-done.9
  52.6 0.7 reduce.6
  53.3 0.0 copy-done.10
  53.3 0.7 reduce.7
  54.0 0.1 reshape.40
  54.1 0.1 copy.24
  54.2 0.1 reshape.41.targets_ref
  54.3 0.1 reshape.38
  54.4 0.1 copy.23
  54.5 0.1 reshape.39.sources_ref
  54.6 0.0 collective-permute-done.2.last_ref
  54.6 1.5 %collective-permute-done.1.far_ref = f32[16,1024]{1,0:T(8,128)S(1)} collective-permute-done((f32[16,1024]{1,0:T(8,128)S(1)}, f32[16,1024]{1,0:T(8,128)S(1)}, u32[]{:S(2)}, u32[]{:S(2)}) %collective-permute-start.1) | collective-permute-done | bytes 65568 | tf_op jit(solution)/shard_map/ppermute | solution.py:507
  56.1 0.0 collective-permute-done.near_ref
  56.1 0.0 copy-done.3
  56.1 0.0 copy-done.1
  56.1 0.0 copy-done.2
  56.1 1.9 %shard_map.132 = (f32[59,1024]{1,0:T(8,128)S(1)}, f32[59,1024]{1,0:T(8,128)}, f32[59,1024]{1,0:T(8,128)}, f32[59,1024]{1,0:T(8,128)}, f32[64,128]{1,0:T(8,128)S(1)}) custom-call(f32[59,1024]{1,0:T(8,128)S(1)} %copy-done.1, f32[59,1024]{1,0:T(8,128)S(1)} %copy-done.2, f32[59,1024]{1,0:T(8,128)S(1)} %copy-done.3, f32[16,1024]{1,0:T(8,128)S(1)} %shard_map.131.own_ref, ...), custom_call_target="tpu_custom_call" | custom-call | tf_op jit(solution)/shard_map/pallas_call | solution.py:512
  58.0 14.8 %all_to_all.34 = f32[64,1,128]{2,1,0:T(1,128)S(1)} all-to-all(f32[64,1,128]{2,1,0:T(1,128)S(1)} %bitcast.26), channel_id=1, replica_groups=mesh['gauss'=64,'view'=4] {'gauss'}, dimensions={0} | all-to-all | bytes 65536 | tf_op jit(solution)/shard_map/all_to_all | solution.py:473
  72.8 1.1 %shard_map.133 = f32[59,1024]{1,0:T(8,128)} custom-call(f32[64,128]{1,0:T(8,128)S(1)} %bitcast.23, s32[1,128]{1,0:T(1,128)S(1)} %reshape.41.targets_ref, f32[59,1024]{1,0:T(8,128)S(1)} %get-tuple-element.14.spread_ref), custom_call_target="tpu_custom_call" | custom-call | tf_op jit(solution)/shard_map/pallas_call | solution.py:518
  (4 shorter events, 0.0 us)
Async XLA Ops:
  0.6 0.7 copy-start.5
  1.3 0.9 %copy-start = (f32[59,1024]{1,0:T(8,128)S(1)}, f32[59,1024]{1,0:T(8,128)}, u32[]{:S(2)}) copy-start(f32[59,1024]{1,0:T(8,128)} %params_ref.3) | copy-start | bytes 724996
  2.2 0.7 copy-start.4
  4.9 13.1 %copy-start.8 = (s32[1,4,256]{2,1,0:T(4,128)S(1)}, s32[1,4,256]{2,1,0:T(4,128)}, u32[]{:S(2)}) copy-start(s32[1,4,256]{2,1,0:T(4,128)} %param.16) | copy-start | bytes 12292
  4.9 13.2 %copy-start.7 = (f32[1,4,3,256]{3,1,2,0:T(4,128)S(1)}, f32[1,4,3,256]{3,1,2,0:T(4,128)}, u32[]{:S(2)}) copy-start(f32[1,4,3,256]{3,1,2,0:T(4,128)} %param.14) | copy-start | bytes 36868
  4.9 23.2 %all-to-all-start = ((f32[64,1,256]{2,1,0:T(1,128)}), f32[64,1,256]{2,1,0:T(1,128)S(1)}, u32[]{:S(2)}, u32[]{:S(2)}) async-start(f32[64,1,256]{2,1,0:T(1,128)} %copy.20), calls=%async_computation | async-start | bytes 131072 | tf_op jit(solution)/shard_map/all_to_all | solution.py:473
  28.1 0.7 copy-start.6
  28.8 27.3 %copy-start.3 = (f32[59,1024]{1,0:T(8,128)S(1)}, f32[59,1024]{1,0:T(8,128)}, u32[]{:S(2)}) copy-start(f32[59,1024]{1,0:T(8,128)} %second_ref.1) | copy-start | bytes 724996
  33.5 19.1 %copy-start.9 = (s32[1,128]{1,0:T(1,128)S(1)}, s32[1,128]{1,0:T(1,128)}, u32[]{:S(2)}) copy-start(s32[1,128]{1,0:T(1,128)} %param.18) | copy-start | bytes 1540
  33.5 19.8 %copy-start.10 = (s32[1,128]{1,0:T(1,128)S(1)}, s32[1,128]{1,0:T(1,128)}, u32[]{:S(2)}) copy-start(s32[1,128]{1,0:T(1,128)} %param.19) | copy-start | bytes 1540
  33.6 22.5 %copy-start.1 = (f32[59,1024]{1,0:T(8,128)S(1)}, f32[59,1024]{1,0:T(8,128)}, u32[]{:S(2)}) copy-start(f32[59,1024]{1,0:T(8,128)} %params_ref.3) | copy-start | bytes 724996
  33.6 22.5 %copy-start.2 = (f32[59,1024]{1,0:T(8,128)S(1)}, f32[59,1024]{1,0:T(8,128)}, u32[]{:S(2)}) copy-start(f32[59,1024]{1,0:T(8,128)} %first_ref.1) | copy-start | bytes 724996
  48.6 6.0 %collective-permute-start.2 = (f32[16,1024]{1,0:T(8,128)S(1)}, f32[16,1024]{1,0:T(8,128)S(1)}, u32[]{:S(2)}, u32[]{:S(2)}) collective-permute-start(f32[16,1024]{1,0:T(8,128)S(1)} %shard_map.131.own_ref), channel_id=1, source_target_pairs={{0,3},{1,2},{2,1},{3,0},{4,7},{5,6},{6,5},{7,4},{8,11},{9,10},{10,... | collective-permute-start | bytes 196616 | tf_op jit(solution)/shard_map/ppermute | solution.py:507
  51.4 4.6 %collective-permute-start.1 = (f32[16,1024]{1,0:T(8,128)S(1)}, f32[16,1024]{1,0:T(8,128)S(1)}, u32[]{:S(2)}, u32[]{:S(2)}) collective-permute-start(f32[16,1024]{1,0:T(8,128)S(1)} %shard_map.131.own_ref), channel_id=1, source_target_pairs={{0,2},{1,3},{2,0},{3,1},{4,6},{5,7},{6,4},{7,5},{8,10},{9,11},{10,... | collective-permute-start | bytes 196616 | tf_op jit(solution)/shard_map/ppermute | solution.py:507
  51.8 4.3 %collective-permute-start = (f32[16,1024]{1,0:T(8,128)S(1)}, f32[16,1024]{1,0:T(8,128)S(1)}, u32[]{:S(2)}, u32[]{:S(2)}) collective-permute-start(f32[16,1024]{1,0:T(8,128)S(1)} %shard_map.131.own_ref), channel_id=1, source_target_pairs={{0,1},{1,0},{2,3},{3,2},{4,5},{5,4},{6,7},{7,6},{8,9},{9,8},{10,11... | collective-permute-start | bytes 196616 | tf_op jit(solution)/shard_map/ppermute | solution.py:507

commit v2 on v1

--- a/solution.py
+++ b/solution.py
@@ -88,11 +88,11 @@
 
 def pack_peers(table):
     pieces = [table[:, k * PEERS : (k + 1) * PEERS] for k in range(CAP)]
-    return jnp.concatenate(pieces, axis=0).T
+    return jnp.concatenate(pieces, axis=0).T.reshape(2 * PEERS, 128)
 
 
 def unpack_peers(block):
-    flat = block.T
+    flat = block.reshape(PEERS, 256).T
     return jnp.concatenate([flat[k * ROWS : (k + 1) * ROWS] for k in range(CAP)], axis=1)
 
 
@@ -218,7 +218,42 @@
     ] + colours
 
 
-def send_kernel(params_ref, slots_ref, camera_ref, out_ref, order_ref):
+def send_kernel(
+    params_hbm,
+    slots_hbm,
+    camera_hbm,
+    lists_hbm,
+    tiles_hbm,
+    target_hbm,
+    out_ref,
+    order_ref,
+    entries_ref,
+    corner_ref,
+    target_ref,
+    params_ref,
+    slots_ref,
+    lists_ref,
+    camera_ref,
+    tiles_ref,
+    sems,
+):
+    pairs = (
+        (slots_hbm, slots_ref),
+        (params_hbm, params_ref),
+        (camera_hbm, camera_ref),
+        (lists_hbm, lists_ref),
+        (tiles_hbm, tiles_ref),
+        (target_hbm, target_ref),
+    )
+    copies = [pltpu.make_async_copy(a, b, sems.at[i]) for i, (a, b) in enumerate(pairs)]
+    for copy in copies:
+        copy.start()
+    copies[0].wait()
+    order = slots_by_rank(slots_ref[...])
+    order_ref[...] = order
+    hot = low_onehot(order)
+    copies[1].wait()
+    copies[2].wait()
     dense = params_ref[...].reshape(59, 8, 128)
     rows = [dense[i] for i in range(59)]
     cam = [camera_ref[0, i] for i in range(16)]
@@ -228,14 +263,24 @@
     listed = seen[0:5] + [opacity] + seen[5:8]
     blank = jnp.zeros((8, 128), F32)
     table = jnp.stack(listed + [blank] * (ROWS - 9)).reshape(ROWS, LOCAL)
-    order = slots_by_rank(slots_ref[...])
-    order_ref[...] = order
-    out_ref[...] = pack_peers(take_columns(table, order, low_onehot(order)))
-
-
-def render_kernel(recv_ref, lists_ref, tiles_ref, target_ref, out_ref, alpha_ref, grad_ref):
+    out_ref[...] = pack_peers(take_columns(table, order, hot))
+    copies[3].wait()
+    entries_ref[...] = jnp.concatenate([lists_ref[0, i : i + 1] for i in range(TILES)], axis=1)
+    copies[4].wait()
+    for tile in range(TILES):
+        number = tiles_ref[0, tile]
+        corner_ref[tile : tile + 1, :] = jnp.full(
+            (1, 256), ((number & (ACROSS - 1)) * 16).astype(F32)
+        )
+        corner_ref[TILES + tile : TILES + tile + 1, :] = jnp.full(
+            (1, 256), ((number >> 4) * 16).astype(F32)
+        )
+    copies[5].wait()
+
+
+def render_kernel(recv_ref, entries_ref, corner_ref, target_ref, out_ref, alpha_ref, grad_ref):
     table = unpack_peers(recv_ref[...])
-    entries = lists_ref[...]
+    entries = entries_ref[...]
     idx = jnp.where(entries < 0, -1, (entries & 15) * PEERS + (entries >> 4))
     hot = low_onehot(idx)
     listed = take_columns(table, idx, hot)
@@ -247,9 +292,8 @@
     results = []
     for tile in range(TILES):
         here = listed[:, tile * 256 : (tile + 1) * 256]
-        number = tiles_ref[0, tile]
-        left = ((number & (ACROSS - 1)) * 16).astype(F32)
-        top = ((number >> 4) * 16).astype(F32)
+        left = corner_ref[tile : tile + 1]
+        top = corner_ref[TILES + tile : TILES + tile + 1]
         con_a, con_b, con_c, opacity = here[2:3], here[3:4], here[4:5], here[5:6]
         off_u = (steps + left + 0.5) - here[0:1]
         off_w = (steps + top + 0.5) - here[1:2]
@@ -277,7 +321,7 @@
             stacked, weights[0], nt, preferred_element_type=F32
         ) + lax.dot_general(stacked, weights[1], nt, preferred_element_type=F32)
         rendered = summed[0:3] + summed[3:6] + summed[6:9]
-        residual = rendered - target_ref[tile]
+        residual = rendered - target_ref[:, tile]
         residual_parts = [p.astype(F32) for p in split(residual, 3)]
         colour_wide = [p.astype(F32) for p in colour_parts]
         pairs = ((0, 0), (0, 1), (1, 0), (1, 1), (0, 2), (2, 0))
@@ -345,6 +389,16 @@
         out_ref[9 + i // 8 : 10 + i // 8, (i % 8) * 128 : (i % 8 + 1) * 128] = jnp.full(
             (1, 128), camera_ref[0, i], F32
         )
+
+
+def pairs_by_rank(pairs):
+    source = lax.broadcasted_iota(I32, (128, 128), 0)
+    col = lax.broadcasted_iota(I32, (128, 128), 1)
+    pick = jnp.where(source == (col & (PEERS - 1)) * 2 + (col >> 6), 1.0, 0.0).astype(BF16)
+    wide = jnp.broadcast_to(pairs + 1, (8, 128))
+    upper = jnp.dot((wide >> 5).astype(F32).astype(BF16), pick, preferred_element_type=F32)
+    lower = jnp.dot((wide & 31).astype(F32).astype(BF16), pick, preferred_element_type=F32)
+    return (upper * 32.0 + lower)[0:1].astype(I32) - 1
 
 
 def log_one_plus(t):
@@ -421,8 +475,8 @@
     stepped = params_ref[...] - rates_column() * (first / BIAS_ONE) / (
         jnp.sqrt(second / BIAS_TWO) + 1e-15
     )
-    sources = sources_ref[...]
-    targets = targets_ref[...]
+    sources = pairs_by_rank(sources_ref[...])
+    targets = pairs_by_rank(targets_ref[...])
     ones = jnp.ones((8, 128), F32)
     source_hot = low_onehot(sources)
     counts = add_columns(ones, sources, source_hot)[0:1]
@@ -446,31 +500,36 @@
 def landing_kernel(recv_ref, targets_ref, spread_ref, out_ref):
     flat = recv_ref[...].T
     moved = jnp.concatenate([flat[0:64], flat[64:128]], axis=1)
-    targets = targets_ref[...]
+    targets = pairs_by_rank(targets_ref[...])
     placed = add_columns(moved, targets, low_onehot(targets))
     out_ref[...] = jnp.where(placed[59:60] > 0.5, placed[0:59], spread_ref[...])
 
 
-def by_rank(pairs):
-    return jnp.transpose(pairs.reshape(PEERS, 2)).reshape(1, 2 * PEERS)
-
-
-def call(kernel, shapes, smem=(), scratch=(), count=0):
-    vmem = pl.BlockSpec(memory_space=pltpu.VMEM)
-    scalar = pl.BlockSpec(memory_space=pltpu.SMEM)
+def call(kernel, shapes, ins, scratch=()):
+    spec = {
+        "v": pl.BlockSpec(memory_space=pltpu.VMEM),
+        "s": pl.BlockSpec(memory_space=pltpu.SMEM),
+        "h": pl.BlockSpec(memory_space=pltpu.HBM),
+    }
     out_shape = [jax.ShapeDtypeStruct(shape, dtype) for shape, dtype in shapes]
     return pl.pallas_call(
         kernel,
         out_shape=out_shape,
-        in_specs=[scalar if i in smem else vmem for i in range(count)],
-        out_specs=[vmem] * len(out_shape),
+        in_specs=[spec[kind] for kind in ins],
+        out_specs=[spec["v"]] * len(out_shape),
         scratch_shapes=list(scratch),
         compiler_params=pltpu.CompilerParams(vmem_limit_bytes=VMEM_LIMIT),
     )
 
 
+def in_hbm(array):
+    return pltpu.with_memory_space_constraint(array, pltpu.HBM)
+
+
 def exchange(block):
-    return lax.all_to_all(block, "gauss", split_axis=0, concat_axis=0, tiled=True)
+    parts = block.reshape(PEERS, -1, 128)
+    got = lax.all_to_all(parts, "gauss", split_axis=0, concat_axis=0, tiled=True)
+    return got.reshape(block.shape)
 
 
 def shards(
@@ -485,37 +544,51 @@
     reloc_send,
     reloc_recv,
 ):
-    outgoing, order = call(
+    packed = ((2 * PEERS, 128), F32)
+    outgoing, order, entries, corners, wanted = call(
         send_kernel,
-        [((PEERS, CAP * ROWS), F32), ((1, LOCAL), I32)],
-        smem=(2,),
-        count=3,
-    )(params, send_slots.reshape(8, 128), cameras)
+        [
+            packed,
+            ((1, LOCAL), I32),
+            ((1, LOCAL), I32),
+            ((2 * TILES, 256), F32),
+            ((3, TILES, 256), F32),
+        ],
+        "hhhhhh",
+        [
+            pltpu.VMEM((59, LOCAL), F32),
+            pltpu.VMEM((8, 128), I32),
+            pltpu.VMEM((1, TILES, 256), I32),
+            pltpu.SMEM((1, 16), F32),
+            pltpu.SMEM((1, TILES), I32),
+            pltpu.SemaphoreType.DMA((6,)),
+        ],
+    )(
+        in_hbm(params),
+        in_hbm(send_slots.reshape(8, 128)),
+        in_hbm(cameras),
+        in_hbm(tile_lists),
+        in_hbm(tile_index),
+        in_hbm(jnp.transpose(target[0], (1, 0, 2))),
+    )
     received = exchange(outgoing)
     (row_grads,) = call(
         render_kernel,
-        [((PEERS, CAP * ROWS), F32)],
-        smem=(2,),
-        scratch=[pltpu.VMEM((256, 256), F32), pltpu.VMEM((256, 256), F32)],
-        count=4,
-    )(received, tile_lists.reshape(1, LOCAL), tile_index, target.reshape(TILES, 3, 256))
+        [packed],
+        "vvvv",
+        [pltpu.VMEM((256, 256), F32), pltpu.VMEM((256, 256), F32)],
+    )(received, entries, corners, wanted)
     returned = exchange(row_grads)
-    (own,) = call(owner_kernel, [((ROWS, LOCAL), F32)], smem=(2,), count=3)(
-        returned, order, cameras
-    )
+    (own,) = call(owner_kernel, [((ROWS, LOCAL), F32)], "vvs")(returned, order, cameras)
     others = [
         lax.ppermute(own, "view", [(i, i ^ flip) for i in range(VIEWS)]) for flip in (1, 2, 3)
     ]
-    sources = by_rank(reloc_send)
-    targets = by_rank(reloc_recv)
     whole = ((59, LOCAL), F32)
     spread, new_first, new_second, gradient, moving = call(
-        step_kernel,
-        [whole, whole, whole, whole, ((PEERS, 128), F32)],
-        count=9,
-    )(params, first_moment, second_moment, own, *others, sources, targets)
+        step_kernel, [whole, whole, whole, whole, ((PEERS, 128), F32)], "vvvvvvvvv"
+    )(params, first_moment, second_moment, own, *others, reloc_send, reloc_recv)
     arrived = exchange(moving)
-    (new_params,) = call(landing_kernel, [whole], count=3)(arrived, targets, spread)
+    (new_params,) = call(landing_kernel, [whole], "vvv")(arrived, reloc_recv, spread)
     return (new_params, new_first, new_second, gradient)
 
 

time: 74.2 us -> 70.1 us (0.945)
  blocking collectives: 28.7 us -> 51.6 us
  starting transfers between devices: 16.6 us -> 3.5 us
  waiting for transfers between devices: 11.5 us -> 3.94 us
  local copies, waits for them, and re-layouts: 4.87 us -> 0.03 us
  other arithmetic: 1.33 us -> 0 us
    all_to_all x2 -> x3, blocking collectives: 28.7 us -> 51.6 us  [exchange(): lax.all_to_all(parts, 'gauss', split_axis=0, concat_axis=0, tiled=True)]
    all_to_all x1 -> x0, starting transfers between devices: 13.1 us -> none  [exchange(): lax.all_to_all(block, 'gauss', split_axis=0, concat_axis=0, tiled=True)]
    all_to_all x1 -> x0, waiting for transfers between devices: 10 us -> none  [exchange(): lax.all_to_all(block, 'gauss', split_axis=0, concat_axis=0, tiled=True)]
    unnamed x27 -> x12, local copies, waits for them, and re-layouts: 3.51 us -> 0.03 us
    ppermute x3, waiting for transfers between devices: 1.49 us -> 3.94 us  [shards(): lax.ppermute(own, 'view', [(i, i ^ flip) for i in range(VIEWS)])]
    unnamed x2 -> x0, other arithmetic: 1.33 us -> none
    all_to_all x2 -> x0, local copies, waits for them, and re-layouts: 0.78 us -> none  [exchange(): lax.all_to_all(block, 'gauss', split_axis=0, concat_axis=0, tiled=True)]
  transfers between devices with their start and end apart: 4 -> 3, of which waited for: 2 -> 2; matrix products, arithmetic and copies ran while one was open for 3% -> 0% of each run, Pallas kernels for 0% -> 0%
where the time goes in v2:
time: 70.1 us; the launch traced here: 69.8 us
  blocking collectives  51.6 us (74%)
  Pallas kernels  10.1 us (14%)
  waiting for transfers between devices  3.94 us (6%)
  starting transfers between devices  3.5 us (5%)
  between operations  0.72 us (1%)
    all_to_all x3, blocking collectives, exchange(): lax.all_to_all(parts, 'gauss', split_axis=0, concat_axis=0, tiled=True)  51.6 us
    pallas_call x1, Pallas kernels, shards(): call(render_kernel, [packed], 'vvvv', [pltpu.VMEM((256, 256), F32), pltpu...  4.22 us
    ppermute x3, waiting for transfers between devices, shards(): lax.ppermute(own, 'view', [(i, i ^ flip) for i in range(VIEWS)])  3.94 us
    ppermute x3, starting transfers between devices, shards(): lax.ppermute(own, 'view', [(i, i ^ flip) for i in range(VIEWS)])  3.5 us
    pallas_call x1, Pallas kernels, shards(): call(step_kernel, [whole, whole, whole, whole, ((PEERS, 128), F32)], 'vvv...  2 us
    pallas_call x1, Pallas kernels, shards(): call(send_kernel, [packed, ((1, LOCAL), I32), ((1, LOCAL), I32), ((2 * TI...  1.64 us
  transfers between devices with their start and end apart: 3, of which 2 were waited for; matrix products, arithmetic and copies ran while one was open for 0% of the time, Pallas kernels for 0%

profile of v2, /device:TPU:1, one launch (start us, length us, event | category | flops | bytes accessed | tf_op | source)
XLA Modules:
  0.0 69.8 jit_solution(4977521836486370746)
XLA Ops:
  0.6 0.0 copy-start.4
  0.6 0.0 copy-start.2
  0.7 1.6 %shard_map.129 = (f32[128,128]{1,0:T(8,128)S(1)}, s32[1,1024]{1,0:T(1,128)S(1)}, s32[1,1024]{1,0:T(1,128)S(1)}, f32[8,256]{1,0:T(8,128)S(1)}, f32[3,4,256]{2,1,0:T(4,128)S(1)}) custom-call(f32[59,1024]{1,0:T(8,128)} %params_ref.1, s32[8,128]{1,0:T(8,128)} %bitcast.19, f32[1,16]{1,0:T(1,128)} %camera_ref.1, s32[1,4,256]{2,1,0:T(4,128)} %lists_hbm.1, ...), custom_call_target="tpu_custom_call" | custom-call | tf_op jit(solution)/shard_map/pallas_call | solution.py:548
  2.3 0.0 copy-start
  2.3 0.0 copy-start.1
  2.3 23.0 %all_to_all.15 = f32[64,2,128]{2,1,0:T(2,128)S(1)} all-to-all(f32[64,2,128]{2,1,0:T(2,128)S(1)} %bitcast.16), channel_id=1, replica_groups=mesh['gauss'=64,'view'=4] {'gauss'}, dimensions={0} | all-to-all | bytes 131072 | tf_op jit(solution)/shard_map/all_to_all | solution.py:531
  25.3 4.2 %shard_map.130 = f32[128,128]{1,0:T(8,128)S(1)} custom-call(f32[128,128]{1,0:T(8,128)S(1)} %bitcast.12, s32[1,1024]{1,0:T(1,128)S(1)} %get-tuple-element.15.entries_ref, f32[8,256]{1,0:T(8,128)S(1)} %get-tuple-element.16.corner_ref, f32[3,4,256]{2,1,0:T(4,128)S(1)} %get-tuple-element.17.target_ref), custom_call_target="tpu_custom_call" | custom-call | tf_op jit(solution)/shard_map/pallas_call | solution.py:575
  29.6 13.8 %all_to_all.16 = f32[64,2,128]{2,1,0:T(2,128)S(1)} all-to-all(f32[64,2,128]{2,1,0:T(2,128)S(1)} %bitcast.13), channel_id=1, replica_groups=mesh['gauss'=64,'view'=4] {'gauss'}, dimensions={0} | all-to-all | bytes 131072 | tf_op jit(solution)/shard_map/all_to_all | solution.py:531
  43.3 0.0 copy-done.4
  43.3 0.0 copy-start.3
  43.3 0.0 copy-start.5
  43.3 1.1 %shard_map.131.own_ref = f32[16,1024]{1,0:T(8,128)S(1)} custom-call(f32[128,128]{1,0:T(8,128)S(1)} %bitcast.14, s32[1,1024]{1,0:T(1,128)S(1)} %get-tuple-element.18.order_ref, f32[1,16]{1,0:T(1,128)S(1)} %copy-done.4), custom_call_target="tpu_custom_call" | custom-call | tf_op jit(solution)/shard_map/pallas_call | solution.py:582
  44.4 2.8 %collective-permute-start.2 = (f32[16,1024]{1,0:T(8,128)S(1)}, f32[16,1024]{1,0:T(8,128)S(1)}, u32[]{:S(2)}, u32[]{:S(2)}) collective-permute-start(f32[16,1024]{1,0:T(8,128)S(1)} %shard_map.131.own_ref), channel_id=1, source_target_pairs={{0,3},{1,2},{2,1},{3,0},{4,7},{5,6},{6,5},{7,4},{8,11},{9,10},{10,... | collective-permute-start | bytes 196616 | tf_op jit(solution)/shard_map/ppermute | solution.py:584
  47.2 0.4 collective-permute-start.1
  47.6 0.3 collective-permute-start
  47.9 1.0 %collective-permute-done.2.last_ref = f32[16,1024]{1,0:T(8,128)S(1)} collective-permute-done((f32[16,1024]{1,0:T(8,128)S(1)}, f32[16,1024]{1,0:T(8,128)S(1)}, u32[]{:S(2)}, u32[]{:S(2)}) %collective-permute-start.2) | collective-permute-done | bytes 65568 | tf_op jit(solution)/shard_map/ppermute | solution.py:584
  48.9 3.0 %collective-permute-done.1.far_ref = f32[16,1024]{1,0:T(8,128)S(1)} collective-permute-done((f32[16,1024]{1,0:T(8,128)S(1)}, f32[16,1024]{1,0:T(8,128)S(1)}, u32[]{:S(2)}, u32[]{:S(2)}) %collective-permute-start.1) | collective-permute-done | bytes 65568 | tf_op jit(solution)/shard_map/ppermute | solution.py:584
  51.9 0.0 collective-permute-done.near_ref
  51.9 0.0 copy-done.2
  51.9 0.0 copy-done
  51.9 0.0 copy-done.1
  51.9 0.0 copy-done.3
  51.9 0.0 copy-done.5
  51.9 2.0 %shard_map.132 = (f32[59,1024]{1,0:T(8,128)S(1)}, f32[59,1024]{1,0:T(8,128)}, f32[59,1024]{1,0:T(8,128)}, f32[59,1024]{1,0:T(8,128)}, f32[64,128]{1,0:T(8,128)S(1)}) custom-call(f32[59,1024]{1,0:T(8,128)S(1)} %copy-done, f32[59,1024]{1,0:T(8,128)S(1)} %copy-done.1, f32[59,1024]{1,0:T(8,128)S(1)} %copy-done.2, f32[16,1024]{1,0:T(8,128)S(1)} %shard_map.131.own_ref, ...), custom_call_target="tpu_custom_call" | custom-call | tf_op jit(solution)/shard_map/pallas_call | solution.py:587
  53.9 14.8 %all_to_all.17 = f32[64,1,128]{2,1,0:T(1,128)S(1)} all-to-all(f32[64,1,128]{2,1,0:T(1,128)S(1)} %bitcast.17), channel_id=1, replica_groups=mesh['gauss'=64,'view'=4] {'gauss'}, dimensions={0} | all-to-all | bytes 65536 | tf_op jit(solution)/shard_map/all_to_all | solution.py:531
  68.7 1.1 %shard_map.133 = f32[59,1024]{1,0:T(8,128)} custom-call(f32[64,128]{1,0:T(8,128)S(1)} %bitcast.15, s32[1,128]{1,0:T(1,128)S(1)} %copy-done.3, f32[59,1024]{1,0:T(8,128)S(1)} %get-tuple-element.20.spread_ref), custom_call_target="tpu_custom_call" | custom-call | tf_op jit(solution)/shard_map/pallas_call | solution.py:591
Async XLA Ops:
  0.6 42.7 %copy-start.4 = (f32[1,16]{1,0:T(1,128)S(1)}, f32[1,16]{1,0:T(1,128)}, u32[]{:S(2)}) copy-start(f32[1,16]{1,0:T(1,128)} %camera_ref.1) | copy-start | bytes 196
  0.6 51.2 %copy-start.2 = (f32[59,1024]{1,0:T(8,128)S(1)}, f32[59,1024]{1,0:T(8,128)}, u32[]{:S(2)}) copy-start(f32[59,1024]{1,0:T(8,128)} %second_ref.1) | copy-start | bytes 724996
  2.3 49.6 %copy-start = (f32[59,1024]{1,0:T(8,128)S(1)}, f32[59,1024]{1,0:T(8,128)}, u32[]{:S(2)}) copy-start(f32[59,1024]{1,0:T(8,128)} %params_ref.1) | copy-start | bytes 724996
  2.3 49.6 %copy-start.1 = (f32[59,1024]{1,0:T(8,128)S(1)}, f32[59,1024]{1,0:T(8,128)}, u32[]{:S(2)}) copy-start(f32[59,1024]{1,0:T(8,128)} %first_ref.1) | copy-start | bytes 724996
  43.3 8.6 %copy-start.3 = (s32[1,128]{1,0:T(1,128)S(1)}, s32[1,128]{1,0:T(1,128)}, u32[]{:S(2)}) copy-start(s32[1,128]{1,0:T(1,128)} %targets_ref.3) | copy-start | bytes 1540
  43.3 8.6 %copy-start.5 = (s32[1,128]{1,0:T(1,128)S(1)}, s32[1,128]{1,0:T(1,128)}, u32[]{:S(2)}) copy-start(s32[1,128]{1,0:T(1,128)} %sources_ref.1) | copy-start | bytes 1540
  44.4 4.5 %collective-permute-start.2 = (f32[16,1024]{1,0:T(8,128)S(1)}, f32[16,1024]{1,0:T(8,128)S(1)}, u32[]{:S(2)}, u32[]{:S(2)}) collective-permute-start(f32[16,1024]{1,0:T(8,128)S(1)} %shard_map.131.own_ref), channel_id=1, source_target_pairs={{0,3},{1,2},{2,1},{3,0},{4,7},{5,6},{6,5},{7,4},{8,11},{9,10},{10,... | collective-permute-start | bytes 196616 | tf_op jit(solution)/shard_map/ppermute | solution.py:584
  47.2 4.6 %collective-permute-start.1 = (f32[16,1024]{1,0:T(8,128)S(1)}, f32[16,1024]{1,0:T(8,128)S(1)}, u32[]{:S(2)}, u32[]{:S(2)}) collective-permute-start(f32[16,1024]{1,0:T(8,128)S(1)} %shard_map.131.own_ref), channel_id=1, source_target_pairs={{0,2},{1,3},{2,0},{3,1},{4,6},{5,7},{6,4},{7,5},{8,10},{9,11},{10,... | collective-permute-start | bytes 196616 | tf_op jit(solution)/shard_map/ppermute | solution.py:584
  47.6 4.3 %collective-permute-start = (f32[16,1024]{1,0:T(8,128)S(1)}, f32[16,1024]{1,0:T(8,128)S(1)}, u32[]{:S(2)}, u32[]{:S(2)}) collective-permute-start(f32[16,1024]{1,0:T(8,128)S(1)} %shard_map.131.own_ref), channel_id=1, source_target_pairs={{0,1},{1,0},{2,3},{3,2},{4,5},{5,4},{6,7},{7,6},{8,9},{9,8},{10,11... | collective-permute-start | bytes 196616 | tf_op jit(solution)/shard_map/ppermute | solution.py:584

commit v3 on v2

--- a/solution.py
+++ b/solution.py
@@ -17,6 +17,12 @@
 TILES = 4
 ACROSS = 16
 ROWS = 16
+SHARE = 48
+BLOCKS = 11
+AT_CAMERA = 72
+AT_MOVED = 88
+AT_SHARE = 104
+SENT = 152
 
 SH_ZERO = 0.28209479177387814
 SH_ONE = 0.4886025119029199
@@ -88,12 +94,12 @@
 
 def pack_peers(table):
     pieces = [table[:, k * PEERS : (k + 1) * PEERS] for k in range(CAP)]
-    return jnp.concatenate(pieces, axis=0).T.reshape(2 * PEERS, 128)
+    return jnp.concatenate(pieces, axis=0).T
 
 
 def unpack_peers(block):
-    flat = block.reshape(PEERS, 256).T
-    return jnp.concatenate([flat[k * ROWS : (k + 1) * ROWS] for k in range(CAP)], axis=1)
+    flat = block.T
+    return jnp.concatenate([flat[k * 8 : (k + 1) * 8] for k in range(CAP)], axis=1)
 
 
 def slots_by_rank(slots):
@@ -107,6 +113,16 @@
     column = lax.broadcasted_iota(I32, (8, LOCAL), 1)
     kept = jnp.where(row == ((column >> 3) & 7), wide, 0.0)
     return jnp.sum(kept, axis=0, keepdims=True).astype(I32)
+
+
+def pairs_by_rank(pairs):
+    source = lax.broadcasted_iota(I32, (128, 128), 0)
+    col = lax.broadcasted_iota(I32, (128, 128), 1)
+    pick = jnp.where(source == (col & (PEERS - 1)) * 2 + (col >> 6), 1.0, 0.0).astype(BF16)
+    wide = jnp.broadcast_to(pairs + 1, (8, 128))
+    upper = jnp.dot((wide >> 5).astype(F32).astype(BF16), pick, preferred_element_type=F32)
+    lower = jnp.dot((wide & 31).astype(F32).astype(BF16), pick, preferred_element_type=F32)
+    return (upper * 32.0 + lower)[0:1].astype(I32) - 1
 
 
 def covariance(log_scale, quat):
@@ -220,30 +236,46 @@
 
 def send_kernel(
     params_hbm,
+    first_hbm,
+    second_hbm,
     slots_hbm,
+    sources_hbm,
+    targets_hbm,
     camera_hbm,
     lists_hbm,
     tiles_hbm,
-    target_hbm,
+    wanted_hbm,
     out_ref,
     order_ref,
     entries_ref,
     corner_ref,
-    target_ref,
+    wanted_ref,
+    counts_ref,
+    landing_ref,
+    shown_ref,
     params_ref,
+    first_ref,
+    second_ref,
     slots_ref,
+    sources_ref,
+    targets_ref,
+    camera_ref,
     lists_ref,
-    camera_ref,
     tiles_ref,
+    stack_ref,
     sems,
 ):
     pairs = (
         (slots_hbm, slots_ref),
+        (sources_hbm, sources_ref),
+        (targets_hbm, targets_ref),
+        (camera_hbm, camera_ref),
         (params_hbm, params_ref),
-        (camera_hbm, camera_ref),
+        (first_hbm, first_ref),
+        (second_hbm, second_ref),
         (lists_hbm, lists_ref),
         (tiles_hbm, tiles_ref),
-        (target_hbm, target_ref),
+        (wanted_hbm, wanted_ref),
     )
     copies = [pltpu.make_async_copy(a, b, sems.at[i]) for i, (a, b) in enumerate(pairs)]
     for copy in copies:
@@ -253,7 +285,15 @@
     order_ref[...] = order
     hot = low_onehot(order)
     copies[1].wait()
+    sources = pairs_by_rank(sources_ref[...])
+    source_hot = low_onehot(sources)
+    counts = add_columns(jnp.ones((8, 128), F32), sources, source_hot)[0:1]
+    counts_ref[...] = counts
+    out_ref[pl.ds(2, PEERS, stride=3), :] = jnp.broadcast_to(sources.astype(F32), (PEERS, 128))
     copies[2].wait()
+    landing_ref[...] = pairs_by_rank(targets_ref[...])
+    copies[3].wait()
+    copies[4].wait()
     dense = params_ref[...].reshape(59, 8, 128)
     rows = [dense[i] for i in range(59)]
     cam = [camera_ref[0, i] for i in range(16)]
@@ -263,10 +303,30 @@
     listed = seen[0:5] + [opacity] + seen[5:8]
     blank = jnp.zeros((8, 128), F32)
     table = jnp.stack(listed + [blank] * (ROWS - 9)).reshape(ROWS, LOCAL)
-    out_ref[...] = pack_peers(take_columns(table, order, hot))
-    copies[3].wait()
+    taken = take_columns(table, order, hot)
+    out_ref[pl.ds(0, PEERS, stride=3), :] = pack_peers(taken[0:8])
+    for copy in copies[5:7]:
+        copy.wait()
+    stack_ref[0:59, :] = params_ref[...]
+    stack_ref[59:60, :] = counts
+    stack_ref[60:64, :] = jnp.zeros((4, LOCAL), F32)
+    stack_ref[64:123, :] = first_ref[...]
+    stack_ref[123:128, :] = jnp.zeros((5, LOCAL), F32)
+    stack_ref[128:187, :] = second_ref[...]
+    stack_ref[187:192, :] = jnp.zeros((5, LOCAL), F32)
+    plane = lax.axis_index("view")
+    share = stack_ref[pl.ds(pl.multiple_of(plane * SHARE, 8), SHARE), :]
+    moved = take_columns(share, sources, source_hot)
+    moved = jnp.concatenate([moved[:, 0:PEERS], moved[:, PEERS:]], axis=0)
+    numbers = order.astype(F32)
+    pieces = []
+    for k in range(CAP):
+        span = slice(k * PEERS, (k + 1) * PEERS)
+        pieces += [taken[8:9, span], numbers[:, span], moved[6 * k : 6 * k + 6]]
+    out_ref[pl.ds(1, PEERS, stride=3), :] = jnp.concatenate(pieces, axis=0).T
+    copies[7].wait()
     entries_ref[...] = jnp.concatenate([lists_ref[0, i : i + 1] for i in range(TILES)], axis=1)
-    copies[4].wait()
+    copies[8].wait()
     for tile in range(TILES):
         number = tiles_ref[0, tile]
         corner_ref[tile : tile + 1, :] = jnp.full(
@@ -275,11 +335,21 @@
         corner_ref[TILES + tile : TILES + tile + 1, :] = jnp.full(
             (1, 256), ((number >> 4) * 16).astype(F32)
         )
-    copies[5].wait()
-
-
-def render_kernel(recv_ref, entries_ref, corner_ref, target_ref, out_ref, alpha_ref, grad_ref):
-    table = unpack_peers(recv_ref[...])
+    for i in range(16):
+        shown_ref[i : i + 1, :] = jnp.full((1, 128), cam[i], F32)
+    copies[9].wait()
+
+
+def render_kernel(
+    recv_ref, entries_ref, corner_ref, target_ref, out_ref, share_ref, alpha_ref, grad_ref
+):
+    lead = recv_ref[pl.ds(0, PEERS, stride=3), :]
+    tail = recv_ref[pl.ds(1, PEERS, stride=3), :]
+    sources = recv_ref[pl.ds(2, PEERS, stride=3), :]
+    flat = tail.T
+    mine = jnp.concatenate([flat[8 * k + 2 : 8 * k + 8] for k in range(CAP)], axis=0)
+    share_ref[...] = jnp.concatenate([mine[0:SHARE], mine[SHARE:]], axis=1)
+    table = jnp.concatenate([unpack_peers(lead), unpack_peers(tail)], axis=0)
     entries = entries_ref[...]
     idx = jnp.where(entries < 0, -1, (entries & 15) * PEERS + (entries >> 4))
     hot = low_onehot(idx)
@@ -378,27 +448,44 @@
             )
         )
     grads = jnp.concatenate(results, axis=1)
-    out_ref[...] = pack_peers(add_columns(grads, idx, hot))
-
-
-def owner_kernel(recv_ref, order_ref, camera_ref, out_ref):
-    values = unpack_peers(recv_ref[...])
+    summed = add_columns(grads, idx, hot)
+    packed = [pack_peers(summed[0:8]), pack_peers(summed[8:16])]
+    out_ref[pl.ds(0, PEERS, stride=BLOCKS), :] = packed[0]
+    out_ref[pl.ds(1, PEERS, stride=BLOCKS), :] = packed[1]
+    gathered = [[] for _ in range(9)]
+    for group in range(PEERS // 8):
+        span = slice(group * 8, (group + 1) * 8)
+        wanted = sources[span]
+        totals = [None] * 9
+        for k in range(CAP):
+            same = tail[span, 8 * k + 1 : 8 * k + 2] == wanted
+            for row in range(9):
+                column = packed[row // 8][span, 8 * k + row % 8 : 8 * k + row % 8 + 1]
+                term = jnp.where(same, column, 0.0)
+                totals[row] = term if totals[row] is None else totals[row] + term
+        for row in range(9):
+            gathered[row].append(totals[row])
+    for row in range(9):
+        turned = jnp.concatenate(gathered[row], axis=0).T
+        out_ref[pl.ds(2 + row, PEERS, stride=BLOCKS), :] = jnp.concatenate(
+            [turned[0:PEERS], turned[PEERS:]], axis=1
+        )
+
+
+def owner_kernel(recv_ref, order_ref, shown_ref, share_ref, out_ref):
+    values = jnp.concatenate(
+        [unpack_peers(recv_ref[pl.ds(i, PEERS, stride=BLOCKS), :]) for i in range(2)], axis=0
+    )
     order = order_ref[...]
-    out_ref[...] = add_columns(values, order, low_onehot(order))
-    for i in range(16):
-        out_ref[9 + i // 8 : 10 + i // 8, (i % 8) * 128 : (i % 8 + 1) * 128] = jnp.full(
-            (1, 128), camera_ref[0, i], F32
-        )
-
-
-def pairs_by_rank(pairs):
-    source = lax.broadcasted_iota(I32, (128, 128), 0)
-    col = lax.broadcasted_iota(I32, (128, 128), 1)
-    pick = jnp.where(source == (col & (PEERS - 1)) * 2 + (col >> 6), 1.0, 0.0).astype(BF16)
-    wide = jnp.broadcast_to(pairs + 1, (8, 128))
-    upper = jnp.dot((wide >> 5).astype(F32).astype(BF16), pick, preferred_element_type=F32)
-    lower = jnp.dot((wide & 31).astype(F32).astype(BF16), pick, preferred_element_type=F32)
-    return (upper * 32.0 + lower)[0:1].astype(I32) - 1
+    owned = add_columns(values, order, low_onehot(order))
+    out_ref[0:AT_CAMERA, :] = owned[0:9].reshape(9, 8, 128).reshape(AT_CAMERA, 128)
+    out_ref[AT_CAMERA:AT_MOVED, :] = shown_ref[...]
+    for row in range(9):
+        out_ref[AT_MOVED + row : AT_MOVED + row + 1, :] = jnp.sum(
+            recv_ref[pl.ds(2 + row, PEERS, stride=BLOCKS), :], axis=0, keepdims=True
+        )
+    out_ref[AT_MOVED + 9 : AT_SHARE, :] = jnp.zeros((AT_SHARE - AT_MOVED - 9, 128), F32)
+    out_ref[AT_SHARE:SENT, :] = share_ref[...]
 
 
 def log_one_plus(t):
@@ -428,6 +515,68 @@
 
 def tree_sum(values):
     return (values[0] + values[1]) + (values[2] + values[3])
+
+
+def adam(params, first_old, second_old, gradient):
+    first = 0.9 * first_old + 0.1 * gradient
+    second = 0.999 * second_old + 0.001 * gradient * gradient
+    stepped = params - rates_column() * (first / BIAS_ONE) / (jnp.sqrt(second / BIAS_TWO) + 1e-15)
+    return stepped, first, second
+
+
+def spread_logit(logit, counts):
+    soft = jnp.maximum(logit, 0.0) + log_one_plus(jnp.exp(-jnp.abs(logit)))
+    share = -soft / (counts + 1.0)
+    return jnp.log(one_minus_exp(share)) - share
+
+
+def sigmoid_rest(logit):
+    return 1.0 - 1.0 / (1.0 + jnp.exp(-logit))
+
+
+def incoming_columns(parts):
+    def stacked(row):
+        return jnp.concatenate([ref[row : row + 1, :] for ref in parts], axis=0)
+
+    def folded(x):
+        return (x[0:1] + x[1:2]) + (x[2:3] + x[3:4])
+
+    def wide(x):
+        return jnp.broadcast_to(x, (VIEWS, 128))
+
+    plane = jnp.full((SHARE, 128), lax.axis_index("view"), I32)
+    shares = [ref[AT_SHARE:SENT, :] for ref in parts]
+    for bit in (1, 2):
+        flip = (plane & bit) > 0
+        shares = [jnp.where(flip, shares[i ^ bit], shares[i]) for i in range(VIEWS)]
+    stack = jnp.concatenate(shares, axis=0)
+    rows = [stack[i : i + 1] for i in range(59)]
+    cam = [stacked(AT_CAMERA + i) for i in range(16)]
+    sigma, pull_sigma = jax.vjp(covariance, rows[3:6], rows[6:10])
+    _, pull = jax.vjp(
+        lambda p, s, c: view_rows(p, s, c, cam),
+        [wide(x) for x in rows[0:3]],
+        [wide(x) for x in sigma],
+        [wide(x) for x in rows[11:59]],
+    )
+    got = [stacked(AT_MOVED + i) for i in range(9)]
+    d_pos, d_sigma, d_coeff = pull([got[i] for i in (0, 1, 2, 3, 4, 6, 7, 8)])
+    d_scale, d_quat = pull_sigma([folded(x) for x in d_sigma])
+    d_logit = folded(got[5]) * sigmoid_rest(rows[10])
+    gradient = jnp.concatenate(
+        [folded(x) for x in d_pos]
+        + list(d_scale)
+        + list(d_quat)
+        + [d_logit]
+        + [folded(x) for x in d_coeff],
+        axis=0,
+    )
+    stepped, _, _ = adam(stack[0:59], stack[64:123], stack[128:187], gradient)
+    logit = spread_logit(stepped[10:11], stack[59:60])
+    row = lax.broadcasted_iota(I32, (59, 128), 0)
+    return jnp.concatenate(
+        [jnp.where(row == 10, logit, stepped), jnp.ones((5, 128), F32)], axis=0
+    )
 
 
 def step_kernel(
@@ -438,22 +587,26 @@
     near_ref,
     far_ref,
     last_ref,
-    sources_ref,
+    counts_ref,
     targets_ref,
-    spread_ref,
+    new_params_ref,
     new_first_ref,
     new_second_ref,
     gradient_ref,
-    out_ref,
 ):
+    parts = (own_ref, near_ref, far_ref, last_ref)
+    targets = targets_ref[...]
+    placed = add_columns(incoming_columns(parts), targets, low_onehot(targets))
     dense = params_ref[...].reshape(59, 8, 128)
     rows = [dense[i] for i in range(59)]
     sigma, pull_sigma = jax.vjp(covariance, rows[3:6], rows[6:10])
     position, coeffs = rows[0:3], rows[11:59]
     pos_parts, sigma_parts, coeff_parts, opacity_parts = [], [], [], []
-    for ref in (own_ref, near_ref, far_ref, last_ref):
-        got = ref[...].reshape(ROWS, 8, 128)
-        cam = [jnp.broadcast_to(got[9 + i // 8, i % 8 : i % 8 + 1, :], (8, 128)) for i in range(16)]
+    for ref in parts:
+        got = [ref[8 * i : 8 * i + 8, :] for i in range(9)]
+        cam = [
+            jnp.broadcast_to(ref[AT_CAMERA + i : AT_CAMERA + i + 1, :], (8, 128)) for i in range(16)
+        ]
         _, pull = jax.vjp(lambda p, s, c: view_rows(p, s, c, cam), position, sigma, coeffs)
         d_pos, d_sigma, d_coeff = pull([got[i] for i in (0, 1, 2, 3, 4, 6, 7, 8)])
         pos_parts.append(d_pos)
@@ -464,45 +617,22 @@
     d_sigma = [tree_sum([p[i] for p in sigma_parts]) for i in range(6)]
     d_coeff = [tree_sum([p[i] for p in coeff_parts]) for i in range(48)]
     d_scale, d_quat = pull_sigma(d_sigma)
-    opacity = 1.0 / (1.0 + jnp.exp(-rows[10]))
-    d_logit = tree_sum(opacity_parts) * (1.0 - opacity)
+    d_logit = tree_sum(opacity_parts) * sigmoid_rest(rows[10])
     gradient = jnp.stack(d_pos + list(d_scale) + list(d_quat) + [d_logit] + d_coeff).reshape(
         59, LOCAL
     )
     gradient_ref[...] = gradient
-    first = 0.9 * first_ref[...] + 0.1 * gradient
-    second = 0.999 * second_ref[...] + 0.001 * gradient * gradient
-    stepped = params_ref[...] - rates_column() * (first / BIAS_ONE) / (
-        jnp.sqrt(second / BIAS_TWO) + 1e-15
-    )
-    sources = pairs_by_rank(sources_ref[...])
-    targets = pairs_by_rank(targets_ref[...])
-    ones = jnp.ones((8, 128), F32)
-    source_hot = low_onehot(sources)
-    counts = add_columns(ones, sources, source_hot)[0:1]
-    landing = add_columns(ones, targets, low_onehot(targets))[0:1]
-    sampled = counts > 0.5
-    cleared = (counts + landing) > 0.5
-    logit = stepped[10:11]
-    soft = jnp.maximum(logit, 0.0) + log_one_plus(jnp.exp(-jnp.abs(logit)))
-    share = -soft / (counts + 1.0)
-    shared_logit = jnp.log(one_minus_exp(share)) - share
+    stepped, first, second = adam(params_ref[...], first_ref[...], second_ref[...], gradient)
+    counts = counts_ref[...]
+    landed = placed[59:60] > 0.5
+    cleared = (counts + placed[59:60]) > 0.5
     row = lax.broadcasted_iota(I32, (59, LOCAL), 0)
-    spread = jnp.where((row == 10) & sampled, shared_logit, stepped)
-    spread_ref[...] = spread
+    spread = jnp.where(
+        (row == 10) & (counts > 0.5), spread_logit(stepped[10:11], counts), stepped
+    )
+    new_params_ref[...] = jnp.where(landed, placed[0:59], spread)
     new_first_ref[...] = jnp.where(cleared, 0.0, first)
     new_second_ref[...] = jnp.where(cleared, 0.0, second)
-    table = jnp.concatenate([spread, jnp.ones((5, LOCAL), F32)], axis=0)
-    moved = take_columns(table, sources, source_hot)
-    out_ref[...] = jnp.concatenate([moved[:, 0:PEERS], moved[:, PEERS : 2 * PEERS]], axis=0).T
-
-
-def landing_kernel(recv_ref, targets_ref, spread_ref, out_ref):
-    flat = recv_ref[...].T
-    moved = jnp.concatenate([flat[0:64], flat[64:128]], axis=1)
-    targets = pairs_by_rank(targets_ref[...])
-    placed = add_columns(moved, targets, low_onehot(targets))
-    out_ref[...] = jnp.where(placed[59:60] > 0.5, placed[0:59], spread_ref[...])
 
 
 def call(kernel, shapes, ins, scratch=()):
@@ -527,7 +657,7 @@
 
 
 def exchange(block):
-    parts = block.reshape(PEERS, -1, 128)
+    parts = block.reshape(PEERS, 1, -1)
     got = lax.all_to_all(parts, "gauss", split_axis=0, concat_axis=0, tiled=True)
     return got.reshape(block.shape)
 
@@ -544,52 +674,61 @@
     reloc_send,
     reloc_recv,
 ):
-    packed = ((2 * PEERS, 128), F32)
-    outgoing, order, entries, corners, wanted = call(
+    columns = ((1, LOCAL), I32)
+    whole = ((59, LOCAL), F32)
+    outgoing, order, entries, corners, wanted, counts, landing, shown = call(
         send_kernel,
         [
-            packed,
-            ((1, LOCAL), I32),
-            ((1, LOCAL), I32),
+            ((3 * PEERS, 128), F32),
+            columns,
+            columns,
             ((2 * TILES, 256), F32),
             ((3, TILES, 256), F32),
+            ((1, LOCAL), F32),
+            ((1, 128), I32),
+            ((16, 128), F32),
         ],
-        "hhhhhh",
+        "hhhhhhhhhh",
         [
             pltpu.VMEM((59, LOCAL), F32),
+            pltpu.VMEM((59, LOCAL), F32),
+            pltpu.VMEM((59, LOCAL), F32),
             pltpu.VMEM((8, 128), I32),
+            pltpu.VMEM((1, 128), I32),
+            pltpu.VMEM((1, 128), I32),
+            pltpu.SMEM((1, 16), F32),
             pltpu.VMEM((1, TILES, 256), I32),
-            pltpu.SMEM((1, 16), F32),
             pltpu.SMEM((1, TILES), I32),
-            pltpu.SemaphoreType.DMA((6,)),
+            pltpu.VMEM((VIEWS * SHARE, LOCAL), F32),
+            pltpu.SemaphoreType.DMA((10,)),
         ],
     )(
         in_hbm(params),
+        in_hbm(first_moment),
+        in_hbm(second_moment),
         in_hbm(send_slots.reshape(8, 128)),
+        in_hbm(reloc_send),
+        in_hbm(reloc_recv),
         in_hbm(cameras),
         in_hbm(tile_lists),
         in_hbm(tile_index),
         in_hbm(jnp.transpose(target[0], (1, 0, 2))),
     )
     received = exchange(outgoing)
-    (row_grads,) = call(
+    row_grads, share = call(
         render_kernel,
-        [packed],
+        [((BLOCKS * PEERS, 128), F32), ((SHARE, 128), F32)],
         "vvvv",
         [pltpu.VMEM((256, 256), F32), pltpu.VMEM((256, 256), F32)],
     )(received, entries, corners, wanted)
     returned = exchange(row_grads)
-    (own,) = call(owner_kernel, [((ROWS, LOCAL), F32)], "vvs")(returned, order, cameras)
+    (own,) = call(owner_kernel, [((SENT, 128), F32)], "vvvv")(returned, order, shown, share)
     others = [
         lax.ppermute(own, "view", [(i, i ^ flip) for i in range(VIEWS)]) for flip in (1, 2, 3)
     ]
-    whole = ((59, LOCAL), F32)
-    spread, new_first, new_second, gradient, moving = call(
-        step_kernel, [whole, whole, whole, whole, ((PEERS, 128), F32)], "vvvvvvvvv"
-    )(params, first_moment, second_moment, own, *others, reloc_send, reloc_recv)
-    arrived = exchange(moving)
-    (new_params,) = call(landing_kernel, [whole], "vvv")(arrived, reloc_recv, spread)
-    return (new_params, new_first, new_second, gradient)
+    return call(step_kernel, [whole, whole, whole, whole], "vvvvvvvvv")(
+        params, first_moment, second_moment, own, *others, counts, landing
+    )
 
 
 def solution(mesh):

time: 70.1 us -> 62.9 us (0.90)
  blocking collectives: 51.6 us -> 41.8 us
  Pallas kernels: 10.1 us -> 12.1 us
    all_to_all x3 -> x2, blocking collectives: 51.6 us -> 41.8 us  [exchange(): lax.all_to_all(parts, 'gauss', split_axis=0, concat_axis=0, tiled=True)]
    pallas_call x5 -> x4, Pallas kernels: 10.1 us -> 12.1 us  [the longest x1 6.74 us: shards(): call(render_kernel, [((BLOCKS * PEERS, 128), F32), ((SHARE, 128), F32)],...]
where the time goes in v3:
time: 62.9 us; the launch traced here: 62.1 us
  blocking collectives  41.8 us (66%)
  Pallas kernels  12.1 us (19%)
  waiting for transfers between devices  4.08 us (6%)
  starting transfers between devices  3.5 us (6%)
  between operations  0.69 us (1%)
    all_to_all x2, blocking collectives, exchange(): lax.all_to_all(parts, 'gauss', split_axis=0, concat_axis=0, tiled=True)  41.8 us
    pallas_call x1, Pallas kernels, shards(): call(render_kernel, [((BLOCKS * PEERS, 128), F32), ((SHARE, 128), F32)],...  6.74 us
    ppermute x3, waiting for transfers between devices, shards(): lax.ppermute(own, 'view', [(i, i ^ flip) for i in range(VIEWS)])  4.08 us
    ppermute x3, starting transfers between devices, shards(): lax.ppermute(own, 'view', [(i, i ^ flip) for i in range(VIEWS)])  3.5 us
    pallas_call x1, Pallas kernels, shards(): call(send_kernel, [((3 * PEERS, 128), F32), columns, columns, ((2 * TILES...  2.54 us
    pallas_call x1, Pallas kernels, shards(): call(step_kernel, [whole, whole, whole, whole], 'vvvvvvvvv')  2.23 us
  transfers between devices with their start and end apart: 3, of which 2 were waited for; matrix products, arithmetic and copies ran while one was open for 0% of the time, Pallas kernels for 0%

profile of v3, /device:TPU:1, one launch (start us, length us, event | category | flops | bytes accessed | tf_op | source)
XLA Modules:
  0.0 62.1 jit_solution(3825354331106480995)
XLA Ops:
  0.6 2.5 %shard_map.129 = (f32[192,128]{1,0:T(8,128)S(1)}, s32[1,1024]{1,0:T(1,128)S(1)}, s32[1,1024]{1,0:T(1,128)S(1)}, f32[8,256]{1,0:T(8,128)S(1)}, f32[3,4,256]{2,1,0...) custom-call(f32[59,1024]{1,0:T(8,128)} %params_ref.1, f32[59,1024]{1,0:T(8,128)} %first_ref.1, ...), custom_call_target="tpu_custom_call" | custom-call | tf_op jit(solution)/shard_map/pallas_call | solution.py:679
  3.2 23.3 %all_to_all.10 = f32[64,1,384]{2,1,0:T(1,128)S(1)} all-to-all(f32[64,1,384]{2,1,0:T(1,128)S(1)} %bitcast.11), channel_id=1, replica_groups=mesh['gauss'=64,'view'=4] {'gauss'}, dimensions={0} | all-to-all | bytes 196608 | tf_op jit(solution)/shard_map/all_to_all | solution.py:661
  26.5 6.7 %shard_map.130 = (f32[704,128]{1,0:T(8,128)S(1)}, f32[48,128]{1,0:T(8,128)S(1)}) custom-call(f32[192,128]{1,0:T(8,128)S(1)} %bitcast.9, s32[1,1024]{1,0:T(1,128)S(1)} %get-tuple-element.15.entries_ref, f32[8,256]{1,0:T(8,128)S(1)} %get-tuple-element.16.corner_ref, f32[3,4,256]{2,1,0:T(4,128)S(1)} %get-tuple-element.17.target_ref), custom_call_target="tpu_custom_call" | custom-call | tf_op jit(solution)/shard_map/pallas_call | solution.py:718
  33.3 0.0 copy-start.1
  33.3 0.0 copy-start.2
  33.3 18.4 %all_to_all.11 = f32[64,1,1408]{2,1,0:T(1,128)S(1)} all-to-all(f32[64,1,1408]{2,1,0:T(1,128)S(1)} %bitcast.10), channel_id=1, replica_groups=mesh['gauss'=64,'view'=4] {'gauss'}, dimensions={0} | all-to-all | bytes 720896 | tf_op jit(solution)/shard_map/all_to_all | solution.py:661
  51.7 0.0 copy-start
  51.7 0.5 shard_map.131.own_ref
  52.3 2.8 %collective-permute-start.2 = (f32[152,128]{1,0:T(8,128)S(1)}, f32[152,128]{1,0:T(8,128)S(1)}, u32[]{:S(2)}, u32[]{:S(2)}) collective-permute-start(f32[152,128]{1,0:T(8,128)S(1)} %shard_map.131.own_ref), channel_id=1, source_target_pairs={{0,3},{1,2},{2,1},{3,0},{4,7},{5,6},{6,5},{7,4},{8,11},{9,10},{10,... | collective-permute-start | bytes 233480 | tf_op jit(solution)/shard_map/ppermute | solution.py:727
  55.1 0.3 collective-permute-start.1
  55.4 0.3 collective-permute-start
  55.8 2.4 %collective-permute-done.2.last_ref = f32[152,128]{1,0:T(8,128)S(1)} collective-permute-done((f32[152,128]{1,0:T(8,128)S(1)}, f32[152,128]{1,0:T(8,128)S(1)}, u32[]{:S(2)}, u32[]{:S(2)}) %collective-permute-start.2) | collective-permute-done | bytes 77856 | tf_op jit(solution)/shard_map/ppermute | solution.py:727
  58.2 1.7 %collective-permute-done.1.far_ref = f32[152,128]{1,0:T(8,128)S(1)} collective-permute-done((f32[152,128]{1,0:T(8,128)S(1)}, f32[152,128]{1,0:T(8,128)S(1)}, u32[]{:S(2)}, u32[]{:S(2)}) %collective-permute-start.1) | collective-permute-done | bytes 77856 | tf_op jit(solution)/shard_map/ppermute | solution.py:727
  59.9 0.0 collective-permute-done.near_ref
  59.9 0.0 copy-done.1
  59.9 0.0 copy-done.2
  59.9 0.0 copy-done
  59.9 2.2 %shard_map.132 = (f32[59,1024]{1,0:T(8,128)}, f32[59,1024]{1,0:T(8,128)}, f32[59,1024]{1,0:T(8,128)}, f32[59,1024]{1,0:T(8,128)}) custom-call(f32[59,1024]{1,0:T(8,128)S(1)} %copy-done, f32[59,1024]{1,0:T(8,128)S(1)} %copy-done.1, f32[59,1024]{1,0:T(8,128)S(1)} %copy-done.2, f32[152,128]{1,0:T(8,128)S(1)} %shard_map.131.own_ref, ...), custom_call_target="tpu_custom_call" | custom-call | tf_op jit(solution)/shard_map/pallas_call | solution.py:729
Async XLA Ops:
  33.3 26.6 %copy-start.1 = (f32[59,1024]{1,0:T(8,128)S(1)}, f32[59,1024]{1,0:T(8,128)}, u32[]{:S(2)}) copy-start(f32[59,1024]{1,0:T(8,128)} %first_ref.1) | copy-start | bytes 724996
  33.3 26.6 %copy-start.2 = (f32[59,1024]{1,0:T(8,128)S(1)}, f32[59,1024]{1,0:T(8,128)}, u32[]{:S(2)}) copy-start(f32[59,1024]{1,0:T(8,128)} %second_ref.1) | copy-start | bytes 724996
  51.7 8.1 %copy-start = (f32[59,1024]{1,0:T(8,128)S(1)}, f32[59,1024]{1,0:T(8,128)}, u32[]{:S(2)}) copy-start(f32[59,1024]{1,0:T(8,128)} %params_ref.1) | copy-start | bytes 724996
  52.3 5.9 %collective-permute-start.2 = (f32[152,128]{1,0:T(8,128)S(1)}, f32[152,128]{1,0:T(8,128)S(1)}, u32[]{:S(2)}, u32[]{:S(2)}) collective-permute-start(f32[152,128]{1,0:T(8,128)S(1)} %shard_map.131.own_ref), channel_id=1, source_target_pairs={{0,3},{1,2},{2,1},{3,0},{4,7},{5,6},{6,5},{7,4},{8,11},{9,10},{10,... | collective-permute-start | bytes 233480 | tf_op jit(solution)/shard_map/ppermute | solution.py:727
  55.1 4.8 %collective-permute-start.1 = (f32[152,128]{1,0:T(8,128)S(1)}, f32[152,128]{1,0:T(8,128)S(1)}, u32[]{:S(2)}, u32[]{:S(2)}) collective-permute-start(f32[152,128]{1,0:T(8,128)S(1)} %shard_map.131.own_ref), channel_id=1, source_target_pairs={{0,2},{1,3},{2,0},{3,1},{4,6},{5,7},{6,4},{7,5},{8,10},{9,11},{10,... | collective-permute-start | bytes 233480 | tf_op jit(solution)/shard_map/ppermute | solution.py:727
  55.4 4.4 %collective-permute-start = (f32[152,128]{1,0:T(8,128)S(1)}, f32[152,128]{1,0:T(8,128)S(1)}, u32[]{:S(2)}, u32[]{:S(2)}) collective-permute-start(f32[152,128]{1,0:T(8,128)S(1)} %shard_map.131.own_ref), channel_id=1, source_target_pairs={{0,1},{1,0},{2,3},{3,2},{4,5},{5,4},{6,7},{7,6},{8,9},{9,8},{10,11... | collective-permute-start | bytes 233480 | tf_op jit(solution)/shard_map/ppermute | solution.py:727

commit v4 on v3

--- a/solution.py
+++ b/solution.py
@@ -17,6 +17,7 @@
 TILES = 4
 ACROSS = 16
 ROWS = 16
+LOG2E = 1.4426950408889634
 SHARE = 48
 BLOCKS = 11
 AT_CAMERA = 72
@@ -82,13 +83,17 @@
     return total
 
 
-def add_columns(values, idx, hot):
+def add_columns(values, idx, hot, parts=3):
     rows = values.shape[0]
     high = idx >> 7
-    masked = jnp.concatenate([jnp.where(high == c, values, 0.0) for c in range(8)], axis=0)
-    lhs = jnp.concatenate(split(masked, 3), axis=1)
-    rhs = jnp.concatenate([hot, hot, hot], axis=1)
-    wide = lax.dot_general(lhs, rhs, (((1,), (1,)), ((), ())), preferred_element_type=F32)
+    pieces = []
+    for piece in split(values, parts):
+        piece = piece.astype(F32)
+        pieces += [jnp.where(high == c, piece, 0.0) for c in range(8)]
+    lhs = jnp.concatenate(pieces, axis=0).astype(BF16)
+    wide = lax.dot_general(lhs, hot, (((1,), (1,)), ((), ())), preferred_element_type=F32)
+    size = 8 * rows
+    wide = sum(wide[i * size : (i + 1) * size] for i in range(1, parts)) + wide[0:size]
     return jnp.concatenate([wide[c * rows : (c + 1) * rows] for c in range(8)], axis=1)
 
 
@@ -262,7 +267,7 @@
     camera_ref,
     lists_ref,
     tiles_ref,
-    stack_ref,
+    picked_ref,
     sems,
 ):
     pairs = (
@@ -307,16 +312,20 @@
     out_ref[pl.ds(0, PEERS, stride=3), :] = pack_peers(taken[0:8])
     for copy in copies[5:7]:
         copy.wait()
-    stack_ref[0:59, :] = params_ref[...]
-    stack_ref[59:60, :] = counts
-    stack_ref[60:64, :] = jnp.zeros((4, LOCAL), F32)
-    stack_ref[64:123, :] = first_ref[...]
-    stack_ref[123:128, :] = jnp.zeros((5, LOCAL), F32)
-    stack_ref[128:187, :] = second_ref[...]
-    stack_ref[187:192, :] = jnp.zeros((5, LOCAL), F32)
     plane = lax.axis_index("view")
-    share = stack_ref[pl.ds(pl.multiple_of(plane * SHARE, 8), SHARE), :]
-    moved = take_columns(share, sources, source_hot)
+    for quarter in range(VIEWS):
+
+        @pl.when(plane == quarter)
+        def _():
+            for at, ref in enumerate((params_ref, first_ref, second_ref)):
+                size = min(16, 59 - 16 * quarter)
+                picked_ref[16 * at : 16 * at + size, :] = ref[16 * quarter : 16 * quarter + size, :]
+                if size < 16:
+                    picked_ref[16 * at + size : 16 * at + 16, :] = jnp.broadcast_to(
+                        counts, (16 - size, LOCAL)
+                    )
+
+    moved = take_columns(picked_ref[...], sources, source_hot)
     moved = jnp.concatenate([moved[:, 0:PEERS], moved[:, PEERS:]], axis=0)
     numbers = order.astype(F32)
     pieces = []
@@ -357,69 +366,85 @@
     iota_r = lax.broadcasted_iota(I32, (256, 256), 0)
     iota_c = lax.broadcasted_iota(I32, (256, 256), 1)
     before_mask = jnp.where(iota_r < iota_c, 1.0, 0.0).astype(BF16)
+    before_mask = jnp.concatenate([before_mask, before_mask], axis=0)
     after_mask = jnp.where(iota_r > iota_c, 1.0, 0.0).astype(BF16)
+    after_mask = jnp.concatenate([after_mask, after_mask], axis=0)
     steps = lax.broadcasted_iota(I32, (16, 256), 0).astype(F32)
-    results = []
-    for tile in range(TILES):
+    nt = (((1,), (1,)), ((), ()))
+    tiles = range(TILES)
+    heres, offs_u, offs_w = [], [], []
+    for tile in tiles:
         here = listed[:, tile * 256 : (tile + 1) * 256]
         left = corner_ref[tile : tile + 1]
         top = corner_ref[TILES + tile : TILES + tile + 1]
         con_a, con_b, con_c, opacity = here[2:3], here[3:4], here[4:5], here[5:6]
         off_u = (steps + left + 0.5) - here[0:1]
         off_w = (steps + top + 0.5) - here[1:2]
-        quad_u = -0.5 * con_a * off_u * off_u
-        cross = -con_b * off_u
-        quad_w = -0.5 * con_c * off_w * off_w
+        quad_u = LOG2E * (jnp.log(opacity) - 0.5 * con_a * off_u * off_u)
+        cross = -LOG2E * con_b * off_u
+        quad_w = (-0.5 * LOG2E) * con_c * off_w * off_w
         for j in range(16):
             exponent = quad_u + quad_w[j : j + 1] + cross * off_w[j : j + 1]
-            alpha_ref[j * 16 : (j + 1) * 16, :] = opacity * jnp.exp(exponent)
-        alpha = alpha_ref[...]
-        keep = 1.0 - alpha
-        logs = split(jnp.log(keep), 2)
-        before = jnp.dot(logs[0], before_mask, preferred_element_type=F32) + jnp.dot(
-            logs[1], before_mask, preferred_element_type=F32
-        )
-        weight = jnp.exp(before) * alpha
-        weights = split(weight, 2)
-        colour = here[6:9]
-        colour_parts = split(colour, 3)
+            alpha_ref[tile, j * 16 : (j + 1) * 16, :] = jnp.exp2(exponent)
+        heres.append(here)
+        offs_u.append(off_u)
+        offs_w.append(off_w)
+    log_keeps = [jnp.log(1.0 - alpha_ref[t]) for t in tiles]
+    logs = [jnp.concatenate(split(x, 2), axis=1) for x in log_keeps]
+    befores = [jnp.dot(x, before_mask, preferred_element_type=F32) for x in logs]
+    weights = [jnp.exp(befores[t]) * alpha_ref[t] for t in tiles]
+    weight_parts = [split(x, 2) for x in weights]
+    colour_parts = [split(here[6:9], 3) for here in heres]
+    residual_parts = []
+    for tile in tiles:
         stacked = jnp.concatenate(
-            [p.astype(F32) for p in colour_parts] + [jnp.zeros((7, 256), F32)], axis=0
+            [p.astype(F32) for p in colour_parts[tile]] + [jnp.zeros((7, 256), F32)], axis=0
         ).astype(BF16)
-        nt = (((1,), (1,)), ((), ()))
         summed = lax.dot_general(
-            stacked, weights[0], nt, preferred_element_type=F32
-        ) + lax.dot_general(stacked, weights[1], nt, preferred_element_type=F32)
-        rendered = summed[0:3] + summed[3:6] + summed[6:9]
-        residual = rendered - target_ref[:, tile]
-        residual_parts = [p.astype(F32) for p in split(residual, 3)]
-        colour_wide = [p.astype(F32) for p in colour_parts]
-        pairs = ((0, 0), (0, 1), (1, 0), (1, 1), (0, 2), (2, 0))
-        blank = jnp.zeros((14, 256), F32)
-        left_side = jnp.concatenate([residual_parts[a] for a, _ in pairs] + [blank], axis=0)
-        right_side = jnp.concatenate([colour_wide[b] for _, b in pairs] + [blank], axis=0)
-        pull = lax.dot_general(
-            left_side.astype(BF16),
-            right_side.astype(BF16),
-            (((0,), (0,)), ((), ())),
+            jnp.concatenate([stacked, stacked], axis=1),
+            jnp.concatenate(weight_parts[tile], axis=1),
+            nt,
             preferred_element_type=F32,
         )
-        weighted = pull * weight
-        flows = split(weighted, 2)
-        after = jnp.dot(flows[0], after_mask, preferred_element_type=F32) + jnp.dot(
-            flows[1], after_mask, preferred_element_type=F32
-        )
-        grad_ref[...] = weighted - after * (alpha / keep)
-        stacked_res = jnp.concatenate(residual_parts + [jnp.zeros((7, 256), F32)], axis=0).astype(
-            BF16
-        )
-        colour_sum = jnp.dot(stacked_res, weights[0], preferred_element_type=F32) + jnp.dot(
-            stacked_res, weights[1], preferred_element_type=F32
+        residual = summed[0:3] + summed[3:6] + summed[6:9] - target_ref[:, tile]
+        residual_parts.append([p.astype(F32) for p in split(residual, 3)])
+    pairs = ((0, 0), (0, 1), (1, 0), (1, 1), (0, 2), (2, 0))
+    blank = jnp.zeros((14, 256), F32)
+    pulls = []
+    for tile in tiles:
+        left_side = jnp.concatenate([residual_parts[tile][a] for a, _ in pairs] + [blank], axis=0)
+        right_side = jnp.concatenate(
+            [colour_parts[tile][b].astype(F32) for _, b in pairs] + [blank], axis=0
+        )
+        pulls.append(
+            lax.dot_general(
+                left_side.astype(BF16),
+                right_side.astype(BF16),
+                (((0,), (0,)), ((), ())),
+                preferred_element_type=F32,
+            )
+        )
+    weighteds = [pulls[t] * weights[t] for t in tiles]
+    flows = [jnp.concatenate(split(x, 2), axis=1) for x in weighteds]
+    afters = [jnp.dot(x, after_mask, preferred_element_type=F32) for x in flows]
+    for t in tiles:
+        grad_ref[t] = weighteds[t] - afters[t] * (alpha_ref[t] * jnp.exp(-log_keeps[t]))
+    results = []
+    for tile in tiles:
+        here, off_u, off_w = heres[tile], offs_u[tile], offs_w[tile]
+        con_a, con_b, con_c = here[2:3], here[3:4], here[4:5]
+        stacked_res = jnp.concatenate(
+            residual_parts[tile] + [jnp.zeros((7, 256), F32)], axis=0
+        ).astype(BF16)
+        colour_sum = jnp.dot(
+            jnp.concatenate([stacked_res, stacked_res], axis=1),
+            jnp.concatenate(weight_parts[tile], axis=0),
+            preferred_element_type=F32,
         )
         colour_grad = colour_sum[0:3] + colour_sum[3:6] + colour_sum[6:9]
         zeroth = first = second = None
         for j in range(16):
-            piece = grad_ref[j * 16 : (j + 1) * 16, :]
+            piece = grad_ref[tile, j * 16 : (j + 1) * 16, :]
             lifted = piece * off_w[j : j + 1]
             twice = lifted * off_w[j : j + 1]
             zeroth = piece if zeroth is None else zeroth + piece
@@ -448,27 +473,23 @@
             )
         )
     grads = jnp.concatenate(results, axis=1)
-    summed = add_columns(grads, idx, hot)
+    summed = add_columns(grads, idx, hot, 2)
     packed = [pack_peers(summed[0:8]), pack_peers(summed[8:16])]
     out_ref[pl.ds(0, PEERS, stride=BLOCKS), :] = packed[0]
     out_ref[pl.ds(1, PEERS, stride=BLOCKS), :] = packed[1]
-    gathered = [[] for _ in range(9)]
-    for group in range(PEERS // 8):
-        span = slice(group * 8, (group + 1) * 8)
-        wanted = sources[span]
-        totals = [None] * 9
-        for k in range(CAP):
-            same = tail[span, 8 * k + 1 : 8 * k + 2] == wanted
-            for row in range(9):
-                column = packed[row // 8][span, 8 * k + row % 8 : 8 * k + row % 8 + 1]
-                term = jnp.where(same, column, 0.0)
-                totals[row] = term if totals[row] is None else totals[row] + term
+    wanted = sources.T
+    wanted = jnp.concatenate([wanted, wanted], axis=1)
+    totals = [None] * 9
+    for pair in range(CAP // 2):
+        span = slice(pair * 128, (pair + 1) * 128)
+        same = wanted == table[9:10, span]
         for row in range(9):
-            gathered[row].append(totals[row])
+            term = jnp.where(same, summed[row : row + 1, span], 0.0)
+            totals[row] = term if pair == 0 else totals[row] + term
     for row in range(9):
-        turned = jnp.concatenate(gathered[row], axis=0).T
+        both = totals[row][:, 0:PEERS] + totals[row][:, PEERS:]
         out_ref[pl.ds(2 + row, PEERS, stride=BLOCKS), :] = jnp.concatenate(
-            [turned[0:PEERS], turned[PEERS:]], axis=1
+            [both[0:PEERS], both[PEERS:]], axis=1
         )
 
 
@@ -477,7 +498,7 @@
         [unpack_peers(recv_ref[pl.ds(i, PEERS, stride=BLOCKS), :]) for i in range(2)], axis=0
     )
     order = order_ref[...]
-    owned = add_columns(values, order, low_onehot(order))
+    owned = add_columns(values, order, low_onehot(order), 2)
     out_ref[0:AT_CAMERA, :] = owned[0:9].reshape(9, 8, 128).reshape(AT_CAMERA, 128)
     out_ref[AT_CAMERA:AT_MOVED, :] = shown_ref[...]
     for row in range(9):
@@ -549,8 +570,10 @@
     for bit in (1, 2):
         flip = (plane & bit) > 0
         shares = [jnp.where(flip, shares[i ^ bit], shares[i]) for i in range(VIEWS)]
-    stack = jnp.concatenate(shares, axis=0)
-    rows = [stack[i : i + 1] for i in range(59)]
+    params, first_old, second_old = [
+        jnp.concatenate([part[i : i + 16] for part in shares], axis=0) for i in (0, 16, 32)
+    ]
+    rows = [params[i : i + 1] for i in range(59)]
     cam = [stacked(AT_CAMERA + i) for i in range(16)]
     sigma, pull_sigma = jax.vjp(covariance, rows[3:6], rows[6:10])
     _, pull = jax.vjp(
@@ -571,8 +594,8 @@
         + [folded(x) for x in d_coeff],
         axis=0,
     )
-    stepped, _, _ = adam(stack[0:59], stack[64:123], stack[128:187], gradient)
-    logit = spread_logit(stepped[10:11], stack[59:60])
+    stepped, _, _ = adam(params[0:59], first_old[0:59], second_old[0:59], gradient)
+    logit = spread_logit(stepped[10:11], params[59:60])
     row = lax.broadcasted_iota(I32, (59, 128), 0)
     return jnp.concatenate(
         [jnp.where(row == 10, logit, stepped), jnp.ones((5, 128), F32)], axis=0
@@ -699,7 +722,7 @@
             pltpu.SMEM((1, 16), F32),
             pltpu.VMEM((1, TILES, 256), I32),
             pltpu.SMEM((1, TILES), I32),
-            pltpu.VMEM((VIEWS * SHARE, LOCAL), F32),
+            pltpu.VMEM((SHARE, LOCAL), F32),
             pltpu.SemaphoreType.DMA((10,)),
         ],
     )(
@@ -719,7 +742,7 @@
         render_kernel,
         [((BLOCKS * PEERS, 128), F32), ((SHARE, 128), F32)],
         "vvvv",
-        [pltpu.VMEM((256, 256), F32), pltpu.VMEM((256, 256), F32)],
+        [pltpu.VMEM((TILES, 256, 256), F32), pltpu.VMEM((TILES, 256, 256), F32)],
     )(received, entries, corners, wanted)
     returned = exchange(row_grads)
     (own,) = call(owner_kernel, [((SENT, 128), F32)], "vvvv")(returned, order, shown, share)

time: 62.9 us -> 59.2 us (0.941)
  Pallas kernels: 12.1 us -> 8.37 us
    pallas_call x1, Pallas kernels: 6.74 us -> 3.16 us  [shards(): call(render_kernel, [((BLOCKS * PEERS, 128), F32), ((SHARE, 128), F32)],...]
where the time goes in v4:
time: 59.2 us; the launch traced here: 58.4 us
  blocking collectives  41.8 us (71%)
  Pallas kernels  8.37 us (14%)
  waiting for transfers between devices  4.08 us (7%)
  starting transfers between devices  3.5 us (6%)
  between operations  0.69 us (1%)
    all_to_all x2, blocking collectives, exchange(): lax.all_to_all(parts, 'gauss', split_axis=0, concat_axis=0, tiled=True)  41.8 us
    ppermute x3, waiting for transfers between devices, shards(): lax.ppermute(own, 'view', [(i, i ^ flip) for i in range(VIEWS)])  4.08 us
    ppermute x3, starting transfers between devices, shards(): lax.ppermute(own, 'view', [(i, i ^ flip) for i in range(VIEWS)])  3.5 us
    pallas_call x1, Pallas kernels, shards(): call(render_kernel, [((BLOCKS * PEERS, 128), F32), ((SHARE, 128), F32)],...  3.16 us
    pallas_call x1, Pallas kernels, shards(): call(send_kernel, [((3 * PEERS, 128), F32), columns, columns, ((2 * TILES...  2.53 us
    pallas_call x1, Pallas kernels, shards(): call(step_kernel, [whole, whole, whole, whole], 'vvvvvvvvv')  2.24 us
  transfers between devices with their start and end apart: 3, of which 2 were waited for; matrix products, arithmetic and copies ran while one was open for 0% of the time, Pallas kernels for 0%

profile of v4, /device:TPU:1, one launch (start us, length us, event | category | flops | bytes accessed | tf_op | source)
XLA Modules:
  0.0 58.4 jit_solution(12763513894032791522)
XLA Ops:
  0.6 2.5 %shard_map.129 = (f32[192,128]{1,0:T(8,128)S(1)}, s32[1,1024]{1,0:T(1,128)S(1)}, s32[1,1024]{1,0:T(1,128)S(1)}, f32[8,256]{1,0:T(8,128)S(1)}, f32[3,4,256]{2,1,0...) custom-call(f32[59,1024]{1,0:T(8,128)} %params_ref.1, f32[59,1024]{1,0:T(8,128)} %first_ref.1, ...), custom_call_target="tpu_custom_call" | custom-call | tf_op jit(solution)/shard_map/pallas_call | solution.py:702
  3.2 23.3 %all_to_all.10 = f32[64,1,384]{2,1,0:T(1,128)S(1)} all-to-all(f32[64,1,384]{2,1,0:T(1,128)S(1)} %bitcast.11), channel_id=1, replica_groups=mesh['gauss'=64,'view'=4] {'gauss'}, dimensions={0} | all-to-all | bytes 196608 | tf_op jit(solution)/shard_map/all_to_all | solution.py:684
  26.5 3.2 %shard_map.130 = (f32[704,128]{1,0:T(8,128)S(1)}, f32[48,128]{1,0:T(8,128)S(1)}) custom-call(f32[192,128]{1,0:T(8,128)S(1)} %bitcast.9, s32[1,1024]{1,0:T(1,128)S(1)} %get-tuple-element.15.entries_ref, f32[8,256]{1,0:T(8,128)S(1)} %get-tuple-element.16.corner_ref, f32[3,4,256]{2,1,0:T(4,128)S(1)} %get-tuple-element.17.target_ref), custom_call_target="tpu_custom_call" | custom-call | tf_op jit(solution)/shard_map/pallas_call | solution.py:741
  29.7 0.0 copy-start.1
  29.7 0.0 copy-start.2
  29.7 18.4 %all_to_all.11 = f32[64,1,1408]{2,1,0:T(1,128)S(1)} all-to-all(f32[64,1,1408]{2,1,0:T(1,128)S(1)} %bitcast.10), channel_id=1, replica_groups=mesh['gauss'=64,'view'=4] {'gauss'}, dimensions={0} | all-to-all | bytes 720896 | tf_op jit(solution)/shard_map/all_to_all | solution.py:684
  48.1 0.0 copy-start
  48.1 0.4 shard_map.131.own_ref
  48.6 2.8 %collective-permute-start.2 = (f32[152,128]{1,0:T(8,128)S(1)}, f32[152,128]{1,0:T(8,128)S(1)}, u32[]{:S(2)}, u32[]{:S(2)}) collective-permute-start(f32[152,128]{1,0:T(8,128)S(1)} %shard_map.131.own_ref), channel_id=1, source_target_pairs={{0,3},{1,2},{2,1},{3,0},{4,7},{5,6},{6,5},{7,4},{8,11},{9,10},{10,... | collective-permute-start | bytes 233480 | tf_op jit(solution)/shard_map/ppermute | solution.py:750
  51.4 0.3 collective-permute-start.1
  51.7 0.3 collective-permute-start
  52.1 2.4 %collective-permute-done.2.last_ref = f32[152,128]{1,0:T(8,128)S(1)} collective-permute-done((f32[152,128]{1,0:T(8,128)S(1)}, f32[152,128]{1,0:T(8,128)S(1)}, u32[]{:S(2)}, u32[]{:S(2)}) %collective-permute-start.2) | collective-permute-done | bytes 77856 | tf_op jit(solution)/shard_map/ppermute | solution.py:750
  54.5 1.7 %collective-permute-done.1.far_ref = f32[152,128]{1,0:T(8,128)S(1)} collective-permute-done((f32[152,128]{1,0:T(8,128)S(1)}, f32[152,128]{1,0:T(8,128)S(1)}, u32[]{:S(2)}, u32[]{:S(2)}) %collective-permute-start.1) | collective-permute-done | bytes 77856 | tf_op jit(solution)/shard_map/ppermute | solution.py:750
  56.1 0.0 collective-permute-done.near_ref
  56.1 0.0 copy-done.1
  56.2 0.0 copy-done.2
  56.2 0.0 copy-done
  56.2 2.2 %shard_map.132 = (f32[59,1024]{1,0:T(8,128)}, f32[59,1024]{1,0:T(8,128)}, f32[59,1024]{1,0:T(8,128)}, f32[59,1024]{1,0:T(8,128)}) custom-call(f32[59,1024]{1,0:T(8,128)S(1)} %copy-done, f32[59,1024]{1,0:T(8,128)S(1)} %copy-done.1, f32[59,1024]{1,0:T(8,128)S(1)} %copy-done.2, f32[152,128]{1,0:T(8,128)S(1)} %shard_map.131.own_ref, ...), custom_call_target="tpu_custom_call" | custom-call | tf_op jit(solution)/shard_map/pallas_call | solution.py:752
Async XLA Ops:
  29.7 26.5 %copy-start.1 = (f32[59,1024]{1,0:T(8,128)S(1)}, f32[59,1024]{1,0:T(8,128)}, u32[]{:S(2)}) copy-start(f32[59,1024]{1,0:T(8,128)} %first_ref.1) | copy-start | bytes 724996
  29.7 26.5 %copy-start.2 = (f32[59,1024]{1,0:T(8,128)S(1)}, f32[59,1024]{1,0:T(8,128)}, u32[]{:S(2)}) copy-start(f32[59,1024]{1,0:T(8,128)} %second_ref.1) | copy-start | bytes 724996
  48.1 8.0 %copy-start = (f32[59,1024]{1,0:T(8,128)S(1)}, f32[59,1024]{1,0:T(8,128)}, u32[]{:S(2)}) copy-start(f32[59,1024]{1,0:T(8,128)} %params_ref.1) | copy-start | bytes 724996
  48.6 5.9 %collective-permute-start.2 = (f32[152,128]{1,0:T(8,128)S(1)}, f32[152,128]{1,0:T(8,128)S(1)}, u32[]{:S(2)}, u32[]{:S(2)}) collective-permute-start(f32[152,128]{1,0:T(8,128)S(1)} %shard_map.131.own_ref), channel_id=1, source_target_pairs={{0,3},{1,2},{2,1},{3,0},{4,7},{5,6},{6,5},{7,4},{8,11},{9,10},{10,... | collective-permute-start | bytes 233480 | tf_op jit(solution)/shard_map/ppermute | solution.py:750
  51.4 4.8 %collective-permute-start.1 = (f32[152,128]{1,0:T(8,128)S(1)}, f32[152,128]{1,0:T(8,128)S(1)}, u32[]{:S(2)}, u32[]{:S(2)}) collective-permute-start(f32[152,128]{1,0:T(8,128)S(1)} %shard_map.131.own_ref), channel_id=1, source_target_pairs={{0,2},{1,3},{2,0},{3,1},{4,6},{5,7},{6,4},{7,5},{8,10},{9,11},{10,... | collective-permute-start | bytes 233480 | tf_op jit(solution)/shard_map/ppermute | solution.py:750
  51.7 4.4 %collective-permute-start = (f32[152,128]{1,0:T(8,128)S(1)}, f32[152,128]{1,0:T(8,128)S(1)}, u32[]{:S(2)}, u32[]{:S(2)}) collective-permute-start(f32[152,128]{1,0:T(8,128)S(1)} %shard_map.131.own_ref), channel_id=1, source_target_pairs={{0,1},{1,0},{2,3},{3,2},{4,5},{5,4},{6,7},{7,6},{8,9},{9,8},{10,11... | collective-permute-start | bytes 233480 | tf_op jit(solution)/shard_map/ppermute | solution.py:750

commit v5 on v4

--- a/solution.py
+++ b/solution.py
@@ -20,10 +20,10 @@
 LOG2E = 1.4426950408889634
 SHARE = 48
 BLOCKS = 11
-AT_CAMERA = 72
-AT_MOVED = 88
-AT_SHARE = 104
-SENT = 152
+AT_MOVED = 72
+AT_CAMERA = 81
+AT_SHARE = 88
+SENT = 136
 
 SH_ZERO = 0.28209479177387814
 SH_ONE = 0.4886025119029199
@@ -105,6 +105,15 @@
 def unpack_peers(block):
     flat = block.T
     return jnp.concatenate([flat[k * 8 : (k + 1) * 8] for k in range(CAP)], axis=1)
+
+
+def halves(row):
+    block = row.reshape(8, 128)
+    return jnp.concatenate([block[:, 0:PEERS], block[:, PEERS:]], axis=0)
+
+
+def joined(block):
+    return jnp.concatenate([block[0:8], block[8:16]], axis=1).reshape(1, LOCAL)
 
 
 def slots_by_rank(slots):
@@ -267,38 +276,36 @@
     camera_ref,
     lists_ref,
     tiles_ref,
-    picked_ref,
     sems,
 ):
     pairs = (
         (slots_hbm, slots_ref),
+        (params_hbm, params_ref),
+        (camera_hbm, camera_ref),
         (sources_hbm, sources_ref),
         (targets_hbm, targets_ref),
-        (camera_hbm, camera_ref),
-        (params_hbm, params_ref),
-        (first_hbm, first_ref),
-        (second_hbm, second_ref),
         (lists_hbm, lists_ref),
         (tiles_hbm, tiles_ref),
         (wanted_hbm, wanted_ref),
+        (first_hbm, first_ref),
+        (second_hbm, second_ref),
     )
     copies = [pltpu.make_async_copy(a, b, sems.at[i]) for i, (a, b) in enumerate(pairs)]
     for copy in copies:
         copy.start()
-    copies[0].wait()
+    for at in (0, 3, 4):
+        copies[at].wait()
     order = slots_by_rank(slots_ref[...])
     order_ref[...] = order
     hot = low_onehot(order)
-    copies[1].wait()
     sources = pairs_by_rank(sources_ref[...])
     source_hot = low_onehot(sources)
-    counts = add_columns(jnp.ones((8, 128), F32), sources, source_hot)[0:1]
+    counts = add_columns(jnp.ones((8, 128), F32), sources, source_hot, 1)[0:1]
     counts_ref[...] = counts
     out_ref[pl.ds(2, PEERS, stride=3), :] = jnp.broadcast_to(sources.astype(F32), (PEERS, 128))
-    copies[2].wait()
     landing_ref[...] = pairs_by_rank(targets_ref[...])
-    copies[3].wait()
-    copies[4].wait()
+    for at in (1, 2, 5, 6, 7, 8, 9):
+        copies[at].wait()
     dense = params_ref[...].reshape(59, 8, 128)
     rows = [dense[i] for i in range(59)]
     cam = [camera_ref[0, i] for i in range(16)]
@@ -310,32 +317,17 @@
     table = jnp.stack(listed + [blank] * (ROWS - 9)).reshape(ROWS, LOCAL)
     taken = take_columns(table, order, hot)
     out_ref[pl.ds(0, PEERS, stride=3), :] = pack_peers(taken[0:8])
-    for copy in copies[5:7]:
-        copy.wait()
-    plane = lax.axis_index("view")
-    for quarter in range(VIEWS):
-
-        @pl.when(plane == quarter)
-        def _():
-            for at, ref in enumerate((params_ref, first_ref, second_ref)):
-                size = min(16, 59 - 16 * quarter)
-                picked_ref[16 * at : 16 * at + size, :] = ref[16 * quarter : 16 * quarter + size, :]
-                if size < 16:
-                    picked_ref[16 * at + size : 16 * at + 16, :] = jnp.broadcast_to(
-                        counts, (16 - size, LOCAL)
-                    )
-
-    moved = take_columns(picked_ref[...], sources, source_hot)
+    plane = jnp.full((16, LOCAL), lax.axis_index("view"), I32)
+    share = []
+    for ref in (params_ref, first_ref, second_ref):
+        final = jnp.concatenate([ref[48:59, :], jnp.broadcast_to(counts, (5, LOCAL))], axis=0)
+        low = jnp.where(plane == 0, ref[0:16, :], ref[16:32, :])
+        share.append(jnp.where(plane < 2, low, jnp.where(plane == 2, ref[32:48, :], final)))
+    moved = take_columns(jnp.concatenate(share, axis=0), sources, source_hot)
     moved = jnp.concatenate([moved[:, 0:PEERS], moved[:, PEERS:]], axis=0)
-    numbers = order.astype(F32)
-    pieces = []
-    for k in range(CAP):
-        span = slice(k * PEERS, (k + 1) * PEERS)
-        pieces += [taken[8:9, span], numbers[:, span], moved[6 * k : 6 * k + 6]]
-    out_ref[pl.ds(1, PEERS, stride=3), :] = jnp.concatenate(pieces, axis=0).T
-    copies[7].wait()
+    flat = jnp.concatenate([halves(taken[8:9]), halves(order.astype(F32)), moved], axis=0)
+    out_ref[pl.ds(1, PEERS, stride=3), :] = flat.T
     entries_ref[...] = jnp.concatenate([lists_ref[0, i : i + 1] for i in range(TILES)], axis=1)
-    copies[8].wait()
     for tile in range(TILES):
         number = tiles_ref[0, tile]
         corner_ref[tile : tile + 1, :] = jnp.full(
@@ -344,9 +336,11 @@
         corner_ref[TILES + tile : TILES + tile + 1, :] = jnp.full(
             (1, 256), ((number >> 4) * 16).astype(F32)
         )
+    lane = lax.broadcasted_iota(I32, (1, 128), 1)
+    shown = jnp.zeros((1, 128), F32)
     for i in range(16):
-        shown_ref[i : i + 1, :] = jnp.full((1, 128), cam[i], F32)
-    copies[9].wait()
+        shown = jnp.where(lane == i, cam[i], shown)
+    shown_ref[...] = shown
 
 
 def render_kernel(
@@ -356,9 +350,11 @@
     tail = recv_ref[pl.ds(1, PEERS, stride=3), :]
     sources = recv_ref[pl.ds(2, PEERS, stride=3), :]
     flat = tail.T
-    mine = jnp.concatenate([flat[8 * k + 2 : 8 * k + 8] for k in range(CAP)], axis=0)
-    share_ref[...] = jnp.concatenate([mine[0:SHARE], mine[SHARE:]], axis=1)
-    table = jnp.concatenate([unpack_peers(lead), unpack_peers(tail)], axis=0)
+    share_ref[...] = jnp.concatenate([flat[32 : 32 + SHARE], flat[32 + SHARE :]], axis=1)
+    numbers = joined(flat[16:32])
+    table = jnp.concatenate(
+        [unpack_peers(lead), joined(flat[0:16]), jnp.zeros((ROWS - 9, LOCAL), F32)], axis=0
+    )
     entries = entries_ref[...]
     idx = jnp.where(entries < 0, -1, (entries & 15) * PEERS + (entries >> 4))
     hot = low_onehot(idx)
@@ -474,15 +470,15 @@
         )
     grads = jnp.concatenate(results, axis=1)
     summed = add_columns(grads, idx, hot, 2)
-    packed = [pack_peers(summed[0:8]), pack_peers(summed[8:16])]
-    out_ref[pl.ds(0, PEERS, stride=BLOCKS), :] = packed[0]
-    out_ref[pl.ds(1, PEERS, stride=BLOCKS), :] = packed[1]
+    out_ref[pl.ds(0, PEERS, stride=BLOCKS), :] = pack_peers(summed[0:8])
+    flat = jnp.concatenate([halves(summed[8:9]), jnp.zeros((112, PEERS), F32)], axis=0)
+    out_ref[pl.ds(1, PEERS, stride=BLOCKS), :] = flat.T
     wanted = sources.T
     wanted = jnp.concatenate([wanted, wanted], axis=1)
     totals = [None] * 9
     for pair in range(CAP // 2):
         span = slice(pair * 128, (pair + 1) * 128)
-        same = wanted == table[9:10, span]
+        same = wanted == numbers[:, span]
         for row in range(9):
             term = jnp.where(same, summed[row : row + 1, span], 0.0)
             totals[row] = term if pair == 0 else totals[row] + term
@@ -494,18 +490,18 @@
 
 
 def owner_kernel(recv_ref, order_ref, shown_ref, share_ref, out_ref):
-    values = jnp.concatenate(
-        [unpack_peers(recv_ref[pl.ds(i, PEERS, stride=BLOCKS), :]) for i in range(2)], axis=0
-    )
+    lead = unpack_peers(recv_ref[pl.ds(0, PEERS, stride=BLOCKS), :])
+    last = joined(recv_ref[pl.ds(1, PEERS, stride=BLOCKS), :].T[0:16])
+    values = jnp.concatenate([lead, last, jnp.zeros((ROWS - 9, LOCAL), F32)], axis=0)
     order = order_ref[...]
     owned = add_columns(values, order, low_onehot(order), 2)
-    out_ref[0:AT_CAMERA, :] = owned[0:9].reshape(9, 8, 128).reshape(AT_CAMERA, 128)
-    out_ref[AT_CAMERA:AT_MOVED, :] = shown_ref[...]
+    out_ref[0:AT_MOVED, :] = owned[0:9].reshape(9, 8, 128).reshape(AT_MOVED, 128)
     for row in range(9):
         out_ref[AT_MOVED + row : AT_MOVED + row + 1, :] = jnp.sum(
             recv_ref[pl.ds(2 + row, PEERS, stride=BLOCKS), :], axis=0, keepdims=True
         )
-    out_ref[AT_MOVED + 9 : AT_SHARE, :] = jnp.zeros((AT_SHARE - AT_MOVED - 9, 128), F32)
+    out_ref[AT_CAMERA : AT_CAMERA + 1, :] = shown_ref[...]
+    out_ref[AT_CAMERA + 1 : AT_SHARE, :] = jnp.zeros((AT_SHARE - AT_CAMERA - 1, 128), F32)
     out_ref[AT_SHARE:SENT, :] = share_ref[...]
 
 
@@ -574,7 +570,8 @@
         jnp.concatenate([part[i : i + 16] for part in shares], axis=0) for i in (0, 16, 32)
     ]
     rows = [params[i : i + 1] for i in range(59)]
-    cam = [stacked(AT_CAMERA + i) for i in range(16)]
+    shown = stacked(AT_CAMERA)
+    cam = [wide(shown[:, i : i + 1]) for i in range(16)]
     sigma, pull_sigma = jax.vjp(covariance, rows[3:6], rows[6:10])
     _, pull = jax.vjp(
         lambda p, s, c: view_rows(p, s, c, cam),
@@ -627,9 +624,8 @@
     pos_parts, sigma_parts, coeff_parts, opacity_parts = [], [], [], []
     for ref in parts:
         got = [ref[8 * i : 8 * i + 8, :] for i in range(9)]
-        cam = [
-            jnp.broadcast_to(ref[AT_CAMERA + i : AT_CAMERA + i + 1, :], (8, 128)) for i in range(16)
-        ]
+        shown = jnp.broadcast_to(ref[AT_CAMERA : AT_CAMERA + 1, :], (8, 128))
+        cam = [jnp.broadcast_to(shown[:, i : i + 1], (8, 128)) for i in range(16)]
         _, pull = jax.vjp(lambda p, s, c: view_rows(p, s, c, cam), position, sigma, coeffs)
         d_pos, d_sigma, d_coeff = pull([got[i] for i in (0, 1, 2, 3, 4, 6, 7, 8)])
         pos_parts.append(d_pos)
@@ -709,7 +705,7 @@
             ((3, TILES, 256), F32),
             ((1, LOCAL), F32),
             ((1, 128), I32),
-            ((16, 128), F32),
+            ((1, 128), F32),
         ],
         "hhhhhhhhhh",
         [
@@ -722,7 +718,6 @@
             pltpu.SMEM((1, 16), F32),
             pltpu.VMEM((1, TILES, 256), I32),
             pltpu.SMEM((1, TILES), I32),
-            pltpu.VMEM((SHARE, LOCAL), F32),
             pltpu.SemaphoreType.DMA((10,)),
         ],
     )(

time: 59.2 us -> 58.3 us (0.985)
  Pallas kernels: 8.37 us -> 7.76 us
where the time goes in v5:
time: 58.3 us; the launch traced here: 57.7 us
  blocking collectives  41.7 us (72%)
  Pallas kernels  7.76 us (13%)
  waiting for transfers between devices  3.99 us (7%)
  starting transfers between devices  3.5 us (6%)
  between operations  0.68 us (1%)
    all_to_all x2, blocking collectives, exchange(): lax.all_to_all(parts, 'gauss', split_axis=0, concat_axis=0, tiled=True)  41.7 us
    ppermute x3, waiting for transfers between devices, shards(): lax.ppermute(own, 'view', [(i, i ^ flip) for i in range(VIEWS)])  3.99 us
    ppermute x3, starting transfers between devices, shards(): lax.ppermute(own, 'view', [(i, i ^ flip) for i in range(VIEWS)])  3.5 us
    pallas_call x1, Pallas kernels, shards(): call(render_kernel, [((BLOCKS * PEERS, 128), F32), ((SHARE, 128), F32)],...  3.16 us
    pallas_call x1, Pallas kernels, shards(): call(step_kernel, [whole, whole, whole, whole], 'vvvvvvvvv')  2.22 us
    pallas_call x1, Pallas kernels, shards(): call(send_kernel, [((3 * PEERS, 128), F32), columns, columns, ((2 * TILES...  1.96 us
  transfers between devices with their start and end apart: 3, of which 2 were waited for; matrix products, arithmetic and copies ran while one was open for 0% of the time, Pallas kernels for 0%

profile of v5, /device:TPU:1, one launch (start us, length us, event | category | flops | bytes accessed | tf_op | source)
XLA Modules:
  0.0 57.7 jit_solution(12774702807176120105)
XLA Ops:
  0.6 2.0 %shard_map.129 = (f32[192,128]{1,0:T(8,128)S(1)}, s32[1,1024]{1,0:T(1,128)S(1)}, s32[1,1024]{1,0:T(1,128)S(1)}, f32[8,256]{1,0:T(8,128)S(1)}, f32[3,4,256]{2,1,0...) custom-call(f32[59,1024]{1,0:T(8,128)} %params_ref.1, f32[59,1024]{1,0:T(8,128)} %first_ref.1, ...), custom_call_target="tpu_custom_call" | custom-call | tf_op jit(solution)/shard_map/pallas_call | solution.py:698
  2.6 23.3 %all_to_all.10 = f32[64,1,384]{2,1,0:T(1,128)S(1)} all-to-all(f32[64,1,384]{2,1,0:T(1,128)S(1)} %bitcast.11), channel_id=1, replica_groups=mesh['gauss'=64,'view'=4] {'gauss'}, dimensions={0} | all-to-all | bytes 196608 | tf_op jit(solution)/shard_map/all_to_all | solution.py:680
  25.9 3.2 %shard_map.130 = (f32[704,128]{1,0:T(8,128)S(1)}, f32[48,128]{1,0:T(8,128)S(1)}) custom-call(f32[192,128]{1,0:T(8,128)S(1)} %bitcast.9, s32[1,1024]{1,0:T(1,128)S(1)} %get-tuple-element.15.entries_ref, f32[8,256]{1,0:T(8,128)S(1)} %get-tuple-element.16.corner_ref, f32[3,4,256]{2,1,0:T(4,128)S(1)} %get-tuple-element.17.target_ref), custom_call_target="tpu_custom_call" | custom-call | tf_op jit(solution)/shard_map/pallas_call | solution.py:736
  29.1 0.0 copy-start.1
  29.1 0.0 copy-start.2
  29.1 18.4 %all_to_all.11 = f32[64,1,1408]{2,1,0:T(1,128)S(1)} all-to-all(f32[64,1,1408]{2,1,0:T(1,128)S(1)} %bitcast.10), channel_id=1, replica_groups=mesh['gauss'=64,'view'=4] {'gauss'}, dimensions={0} | all-to-all | bytes 720896 | tf_op jit(solution)/shard_map/all_to_all | solution.py:680
  47.5 0.0 copy-start
  47.5 0.4 shard_map.131.own_ref
  48.0 2.8 %collective-permute-start.2 = (f32[136,128]{1,0:T(8,128)S(1)}, f32[136,128]{1,0:T(8,128)S(1)}, u32[]{:S(2)}, u32[]{:S(2)}) collective-permute-start(f32[136,128]{1,0:T(8,128)S(1)} %shard_map.131.own_ref), channel_id=1, source_target_pairs={{0,3},{1,2},{2,1},{3,0},{4,7},{5,6},{6,5},{7,4},{8,11},{9,10},{10,... | collective-permute-start | bytes 208904 | tf_op jit(solution)/shard_map/ppermute | solution.py:745
  50.8 0.4 collective-permute-start.1
  51.1 0.3 collective-permute-start
  51.5 1.9 %collective-permute-done.2.last_ref = f32[136,128]{1,0:T(8,128)S(1)} collective-permute-done((f32[136,128]{1,0:T(8,128)S(1)}, f32[136,128]{1,0:T(8,128)S(1)}, u32[]{:S(2)}, u32[]{:S(2)}) %collective-permute-start.2) | collective-permute-done | bytes 69664 | tf_op jit(solution)/shard_map/ppermute | solution.py:745
  53.4 2.1 %collective-permute-done.1.far_ref = f32[136,128]{1,0:T(8,128)S(1)} collective-permute-done((f32[136,128]{1,0:T(8,128)S(1)}, f32[136,128]{1,0:T(8,128)S(1)}, u32[]{:S(2)}, u32[]{:S(2)}) %collective-permute-start.1) | collective-permute-done | bytes 69664 | tf_op jit(solution)/shard_map/ppermute | solution.py:745
  55.4 0.0 collective-permute-done.near_ref
  55.4 0.0 copy-done.1
  55.5 0.0 copy-done.2
  55.5 0.0 copy-done
  55.5 2.2 %shard_map.132 = (f32[59,1024]{1,0:T(8,128)}, f32[59,1024]{1,0:T(8,128)}, f32[59,1024]{1,0:T(8,128)}, f32[59,1024]{1,0:T(8,128)}) custom-call(f32[59,1024]{1,0:T(8,128)S(1)} %copy-done, f32[59,1024]{1,0:T(8,128)S(1)} %copy-done.1, f32[59,1024]{1,0:T(8,128)S(1)} %copy-done.2, f32[136,128]{1,0:T(8,128)S(1)} %shard_map.131.own_ref, ...), custom_call_target="tpu_custom_call" | custom-call | tf_op jit(solution)/shard_map/pallas_call | solution.py:747
Async XLA Ops:
  29.1 26.3 %copy-start.1 = (f32[59,1024]{1,0:T(8,128)S(1)}, f32[59,1024]{1,0:T(8,128)}, u32[]{:S(2)}) copy-start(f32[59,1024]{1,0:T(8,128)} %first_ref.1) | copy-start | bytes 724996
  29.1 26.3 %copy-start.2 = (f32[59,1024]{1,0:T(8,128)S(1)}, f32[59,1024]{1,0:T(8,128)}, u32[]{:S(2)}) copy-start(f32[59,1024]{1,0:T(8,128)} %second_ref.1) | copy-start | bytes 724996
  47.5 7.9 %copy-start = (f32[59,1024]{1,0:T(8,128)S(1)}, f32[59,1024]{1,0:T(8,128)}, u32[]{:S(2)}) copy-start(f32[59,1024]{1,0:T(8,128)} %params_ref.1) | copy-start | bytes 724996
  48.0 5.4 %collective-permute-start.2 = (f32[136,128]{1,0:T(8,128)S(1)}, f32[136,128]{1,0:T(8,128)S(1)}, u32[]{:S(2)}, u32[]{:S(2)}) collective-permute-start(f32[136,128]{1,0:T(8,128)S(1)} %shard_map.131.own_ref), channel_id=1, source_target_pairs={{0,3},{1,2},{2,1},{3,0},{4,7},{5,6},{6,5},{7,4},{8,11},{9,10},{10,... | collective-permute-start | bytes 208904 | tf_op jit(solution)/shard_map/ppermute | solution.py:745
  50.8 4.7 %collective-permute-start.1 = (f32[136,128]{1,0:T(8,128)S(1)}, f32[136,128]{1,0:T(8,128)S(1)}, u32[]{:S(2)}, u32[]{:S(2)}) collective-permute-start(f32[136,128]{1,0:T(8,128)S(1)} %shard_map.131.own_ref), channel_id=1, source_target_pairs={{0,2},{1,3},{2,0},{3,1},{4,6},{5,7},{6,4},{7,5},{8,10},{9,11},{10,... | collective-permute-start | bytes 208904 | tf_op jit(solution)/shard_map/ppermute | solution.py:745
  51.1 4.3 %collective-permute-start = (f32[136,128]{1,0:T(8,128)S(1)}, f32[136,128]{1,0:T(8,128)S(1)}, u32[]{:S(2)}, u32[]{:S(2)}) collective-permute-start(f32[136,128]{1,0:T(8,128)S(1)} %shard_map.131.own_ref), channel_id=1, source_target_pairs={{0,1},{1,0},{2,3},{3,2},{4,5},{5,4},{6,7},{7,6},{8,9},{9,8},{10,11... | collective-permute-start | bytes 208904 | tf_op jit(solution)/shard_map/ppermute | solution.py:745

commit v6 on v5

--- a/solution.py
+++ b/solution.py
@@ -19,7 +19,7 @@
 ROWS = 16
 LOG2E = 1.4426950408889634
 SHARE = 48
-BLOCKS = 11
+BLOCKS = 6
 AT_MOVED = 72
 AT_CAMERA = 81
 AT_SHARE = 88
@@ -344,7 +344,7 @@
 
 
 def render_kernel(
-    recv_ref, entries_ref, corner_ref, target_ref, out_ref, share_ref, alpha_ref, grad_ref
+    recv_ref, entries_ref, corner_ref, target_ref, out_ref, give_ref, share_ref, alpha_ref, grad_ref
 ):
     lead = recv_ref[pl.ds(0, PEERS, stride=3), :]
     tail = recv_ref[pl.ds(1, PEERS, stride=3), :]
@@ -438,14 +438,16 @@
             preferred_element_type=F32,
         )
         colour_grad = colour_sum[0:3] + colour_sum[3:6] + colour_sum[6:9]
-        zeroth = first = second = None
-        for j in range(16):
-            piece = grad_ref[tile, j * 16 : (j + 1) * 16, :]
-            lifted = piece * off_w[j : j + 1]
-            twice = lifted * off_w[j : j + 1]
-            zeroth = piece if zeroth is None else zeroth + piece
-            first = lifted if first is None else first + lifted
-            second = twice if second is None else second + twice
+        zeroth = first = second = grad_ref[tile, 240:256, :]
+        for j in range(14, -1, -1):
+            zeroth = zeroth + grad_ref[tile, j * 16 : (j + 1) * 16, :]
+            first = first + zeroth
+            second = second + first
+        start = off_w[0:1]
+        by_step = first - zeroth
+        by_square = 2.0 * second - 3.0 * by_step - 2.0 * zeroth
+        first = start * zeroth + by_step
+        second = start * (first + by_step) + by_square
 
         def over(values):
             return jnp.sum(values, axis=0, keepdims=True)
@@ -471,22 +473,39 @@
     grads = jnp.concatenate(results, axis=1)
     summed = add_columns(grads, idx, hot, 2)
     out_ref[pl.ds(0, PEERS, stride=BLOCKS), :] = pack_peers(summed[0:8])
+    give_ref[pl.ds(0, PEERS, stride=BLOCKS), :] = jnp.zeros((PEERS, 128), F32)
     flat = jnp.concatenate([halves(summed[8:9]), jnp.zeros((112, PEERS), F32)], axis=0)
-    out_ref[pl.ds(1, PEERS, stride=BLOCKS), :] = flat.T
-    wanted = sources.T
-    wanted = jnp.concatenate([wanted, wanted], axis=1)
-    totals = [None] * 9
-    for pair in range(CAP // 2):
-        span = slice(pair * 128, (pair + 1) * 128)
-        same = wanted == numbers[:, span]
-        for row in range(9):
-            term = jnp.where(same, summed[row : row + 1, span], 0.0)
-            totals[row] = term if pair == 0 else totals[row] + term
-    for row in range(9):
-        both = totals[row][:, 0:PEERS] + totals[row][:, PEERS:]
-        out_ref[pl.ds(2 + row, PEERS, stride=BLOCKS), :] = jnp.concatenate(
-            [both[0:PEERS], both[PEERS:]], axis=1
-        )
+    ninth = flat.T
+    odd = jnp.full((8, 128), lax.axis_index("gauss") & 1, I32) > 0
+    right = lax.broadcasted_iota(I32, (8, 128), 1) >= PEERS
+    turned = sources.T
+    wanted = jnp.concatenate([turned[0:PEERS], turned[PEERS:]], axis=1)
+    rows = [[] for _ in range(10)]
+    for k in range(CAP):
+        span = slice(k * PEERS, (k + 1) * PEERS)
+        lines = jnp.concatenate([summed[0:9, span], numbers[:, span]], axis=0)
+        lines = jnp.concatenate([lines, lines], axis=1)
+        for row in range(10):
+            rows[row].append(jnp.broadcast_to(lines[row : row + 1], (8, 128)))
+    for group in range(PEERS // 8):
+        ask = wanted[group * 8 : (group + 1) * 8]
+        totals = [None] * 9
+        for k in range(CAP):
+            same = ask == rows[9][k]
+            for row in range(9):
+                term = jnp.where(same, rows[row][k], 0.0)
+                totals[row] = term if k == 0 else totals[row] + term
+        start = group * 8 * BLOCKS
+        turn = pltpu.roll(totals[8], PEERS, axis=1)
+        keep = jnp.where(odd, totals[8], turn)
+        give = jnp.where(odd, turn, totals[8])
+        at = pl.ds(start + 1, 8, stride=BLOCKS)
+        out_ref[at, :] = jnp.where(right, keep, ninth[group * 8 : (group + 1) * 8])
+        give_ref[at, :] = jnp.where(right, give, 0.0)
+        for row in range(4):
+            at = pl.ds(start + 2 + row, 8, stride=BLOCKS)
+            out_ref[at, :] = jnp.where(odd, totals[4 + row], totals[row])
+            give_ref[at, :] = jnp.where(odd, totals[row], totals[4 + row])
 
 
 def owner_kernel(recv_ref, order_ref, shown_ref, share_ref, out_ref):
@@ -496,10 +515,23 @@
     order = order_ref[...]
     owned = add_columns(values, order, low_onehot(order), 2)
     out_ref[0:AT_MOVED, :] = owned[0:9].reshape(9, 8, 128).reshape(AT_MOVED, 128)
-    for row in range(9):
-        out_ref[AT_MOVED + row : AT_MOVED + row + 1, :] = jnp.sum(
-            recv_ref[pl.ds(2 + row, PEERS, stride=BLOCKS), :], axis=0, keepdims=True
-        )
+    odd = (lax.broadcasted_iota(I32, (PEERS, 128), 0) & 1) > 0
+
+    def sums(block):
+        values = recv_ref[pl.ds(block, PEERS, stride=BLOCKS), :]
+        return [
+            jnp.sum(jnp.where(odd, 0.0, values), axis=0, keepdims=True),
+            jnp.sum(jnp.where(odd, values, 0.0), axis=0, keepdims=True),
+        ]
+
+    for row in range(4):
+        even_sum, odd_sum = sums(2 + row)
+        out_ref[AT_MOVED + row : AT_MOVED + row + 1, :] = even_sum
+        out_ref[AT_MOVED + 4 + row : AT_MOVED + 5 + row, :] = odd_sum
+    even_sum, odd_sum = sums(1)
+    out_ref[AT_MOVED + 8 : AT_MOVED + 9, :] = jnp.concatenate(
+        [even_sum[:, PEERS:], odd_sum[:, PEERS:]], axis=1
+    )
     out_ref[AT_CAMERA : AT_CAMERA + 1, :] = shown_ref[...]
     out_ref[AT_CAMERA + 1 : AT_SHARE, :] = jnp.zeros((AT_SHARE - AT_CAMERA - 1, 128), F32)
     out_ref[AT_SHARE:SENT, :] = share_ref[...]
@@ -733,13 +765,15 @@
         in_hbm(jnp.transpose(target[0], (1, 0, 2))),
     )
     received = exchange(outgoing)
-    row_grads, share = call(
+    back = ((BLOCKS * PEERS, 128), F32)
+    row_grads, give, share = call(
         render_kernel,
-        [((BLOCKS * PEERS, 128), F32), ((SHARE, 128), F32)],
+        [back, back, ((SHARE, 128), F32)],
         "vvvv",
         [pltpu.VMEM((TILES, 256, 256), F32), pltpu.VMEM((TILES, 256, 256), F32)],
     )(received, entries, corners, wanted)
-    returned = exchange(row_grads)
+    sibling = lax.ppermute(give, "gauss", [(i, i ^ 1) for i in range(PEERS)])
+    returned = exchange(row_grads + sibling)
     (own,) = call(owner_kernel, [((SENT, 128), F32)], "vvvv")(returned, order, shown, share)
     others = [
         lax.ppermute(own, "view", [(i, i ^ flip) for i in range(VIEWS)]) for flip in (1, 2, 3)

time: 58.3 us -> 56.9 us (0.976)
  blocking collectives: 41.7 us -> 39.3 us
  waiting for transfers between devices: 3.99 us -> 5.06 us
    all_to_all x2, blocking collectives: 41.7 us -> 39.3 us  [exchange(): lax.all_to_all(parts, 'gauss', split_axis=0, concat_axis=0, tiled=True)]
    ppermute x0 -> x1, waiting for transfers between devices: none -> 1.07 us  [shards(): sibling = lax.ppermute(give, 'gauss', [(i, i ^ 1) for i in range(PEERS)])]
  transfers between devices with their start and end apart: 3 -> 4, of which waited for: 2 -> 3; matrix products, arithmetic and copies ran while one was open for 0% -> 0% of each run, Pallas kernels for 0% -> 0%
where the time goes in v6:
time: 56.9 us; the launch traced here: 56.7 us
  blocking collectives  39.3 us (69%)
  Pallas kernels  7.71 us (14%)
  waiting for transfers between devices  5.06 us (9%)
  starting transfers between devices  3.97 us (7%)
  between operations  0.69 us (1%)
    all_to_all x2, blocking collectives, exchange(): lax.all_to_all(parts, 'gauss', split_axis=0, concat_axis=0, tiled=True)  39.3 us
    ppermute x3, waiting for transfers between devices, shards(): lax.ppermute(own, 'view', [(i, i ^ flip) for i in range(VIEWS)])  3.99 us
    ppermute x3, starting transfers between devices, shards(): lax.ppermute(own, 'view', [(i, i ^ flip) for i in range(VIEWS)])  3.5 us
    pallas_call x1, Pallas kernels, shards(): call(render_kernel, [back, back, ((SHARE, 128), F32)], 'vvvv', [pltpu.VME...  3.1 us
    pallas_call x1, Pallas kernels, shards(): call(step_kernel, [whole, whole, whole, whole], 'vvvvvvvvv')  2.22 us
    pallas_call x1, Pallas kernels, shards(): call(send_kernel, [((3 * PEERS, 128), F32), columns, columns, ((2 * TILES...  1.96 us
  transfers between devices with their start and end apart: 4, of which 3 were waited for; matrix products, arithmetic and copies ran while one was open for 0% of the time, Pallas kernels for 0%

profile of v6, /device:TPU:1, one launch (start us, length us, event | category | flops | bytes accessed | tf_op | source)
XLA Modules:
  0.0 56.7 jit_solution(14824537922362451005)
XLA Ops:
  0.6 2.0 %shard_map.129 = (f32[192,128]{1,0:T(8,128)S(1)}, s32[1,1024]{1,0:T(1,128)S(1)}, s32[1,1024]{1,0:T(1,128)S(1)}, f32[8,256]{1,0:T(8,128)S(1)}, f32[3,4,256]{2,1,0...) custom-call(f32[59,1024]{1,0:T(8,128)} %params_ref.1, f32[59,1024]{1,0:T(8,128)} %first_ref.1, ...), custom_call_target="tpu_custom_call" | custom-call | tf_op jit(solution)/shard_map/pallas_call | solution.py:730
  2.6 23.3 %all_to_all.10 = f32[64,1,384]{2,1,0:T(1,128)S(1)} all-to-all(f32[64,1,384]{2,1,0:T(1,128)S(1)} %bitcast.10), channel_id=1, replica_groups=mesh['gauss'=64,'view'=4] {'gauss'}, dimensions={0} | all-to-all | bytes 196608 | tf_op jit(solution)/shard_map/all_to_all | solution.py:712
  25.9 3.1 %shard_map.130 = (f32[384,128]{1,0:T(8,128)S(1)}, f32[384,128]{1,0:T(8,128)S(1)}, f32[48,128]{1,0:T(8,128)S(1)}) custom-call(f32[192,128]{1,0:T(8,128)S(1)} %bitcast.9, s32[1,1024]{1,0:T(1,128)S(1)} %get-tuple-element.16.entries_ref, f32[8,256]{1,0:T(8,128)S(1)} %get-tuple-element.17.corner_ref, f32[3,4,256]{2,1,0:T(4,128)S(1)} %get-tuple-element.18.target_ref), custom_call_target="tpu_custom_call" | custom-call | tf_op jit(solution)/shard_map/pallas_call | solution.py:769
  29.0 0.5 collective-permute-start
  29.5 1.1 %collective-permute-done = f32[384,128]{1,0:T(8,128)S(1)} collective-permute-done((f32[384,128]{1,0:T(8,128)S(1)}, f32[384,128]{1,0:T(8,128)S(1)}, u32[]{:S(2)}, u32[]{:S(2)}) %collective-permute-start) | collective-permute-done | bytes 196640 | tf_op jit(solution)/shard_map/ppermute | solution.py:775
  30.6 0.0 copy-start.2
  30.6 0.0 copy-start
  30.6 0.0 copy-start.1
  30.6 15.9 %all_to_all.11 = f32[64,1,768]{2,1,0:T(1,128)S(1)} all-to-all(f32[64,1,768]{2,1,0:T(1,128)S(1)} %bitcast.11), channel_id=1, replica_groups=mesh['gauss'=64,'view'=4] {'gauss'}, dimensions={0} | all-to-all | bytes 393216 | tf_op jit(solution)/shard_map/all_to_all | solution.py:712
  46.6 0.4 shard_map.131.own_ref
  47.0 2.8 %collective-permute-start.3 = (f32[136,128]{1,0:T(8,128)S(1)}, f32[136,128]{1,0:T(8,128)S(1)}, u32[]{:S(2)}, u32[]{:S(2)}) collective-permute-start(f32[136,128]{1,0:T(8,128)S(1)} %shard_map.131.own_ref), channel_id=1, source_target_pairs={{0,3},{1,2},{2,1},{3,0},{4,7},{5,6},{6,5},{7,4},{8,11},{9,10},{10,... | collective-permute-start | bytes 208904 | tf_op jit(solution)/shard_map/ppermute | solution.py:779
  49.8 0.4 collective-permute-start.2
  50.2 0.2 collective-permute-start.1
  50.5 1.8 %collective-permute-done.3.last_ref = f32[136,128]{1,0:T(8,128)S(1)} collective-permute-done((f32[136,128]{1,0:T(8,128)S(1)}, f32[136,128]{1,0:T(8,128)S(1)}, u32[]{:S(2)}, u32[]{:S(2)}) %collective-permute-start.3) | collective-permute-done | bytes 69664 | tf_op jit(solution)/shard_map/ppermute | solution.py:779
  52.3 2.2 %collective-permute-done.2.far_ref = f32[136,128]{1,0:T(8,128)S(1)} collective-permute-done((f32[136,128]{1,0:T(8,128)S(1)}, f32[136,128]{1,0:T(8,128)S(1)}, u32[]{:S(2)}, u32[]{:S(2)}) %collective-permute-start.2) | collective-permute-done | bytes 69664 | tf_op jit(solution)/shard_map/ppermute | solution.py:779
  54.5 0.0 collective-permute-done.1.near_ref
  54.5 0.0 copy-done.2
  54.5 0.0 copy-done
  54.5 0.0 copy-done.1
  54.5 2.2 %shard_map.132 = (f32[59,1024]{1,0:T(8,128)}, f32[59,1024]{1,0:T(8,128)}, f32[59,1024]{1,0:T(8,128)}, f32[59,1024]{1,0:T(8,128)}) custom-call(f32[59,1024]{1,0:T(8,128)S(1)} %copy-done, f32[59,1024]{1,0:T(8,128)S(1)} %copy-done.1, f32[59,1024]{1,0:T(8,128)S(1)} %copy-done.2, f32[136,128]{1,0:T(8,128)S(1)} %shard_map.131.own_ref, ...), custom_call_target="tpu_custom_call" | custom-call | tf_op jit(solution)/shard_map/pallas_call | solution.py:781
  (1 shorter events, 0.0 us)
Async XLA Ops:
  29.0 1.5 %collective-permute-start = (f32[384,128]{1,0:T(8,128)S(1)}, f32[384,128]{1,0:T(8,128)S(1)}, u32[]{:S(2)}, u32[]{:S(2)}) collective-permute-start(f32[384,128]{1,0:T(8,128)S(1)} %get-tuple-element.20), channel_id=1, source_target_pairs={{0,4},{4,0},{8,12},{12,8},{16,20},{20,16},{24,28},{28,24},{32,36},... | collective-permute-start | bytes 589832 | tf_op jit(solution)/shard_map/ppermute | solution.py:775
  30.6 23.9 %copy-start.2 = (f32[59,1024]{1,0:T(8,128)S(1)}, f32[59,1024]{1,0:T(8,128)}, u32[]{:S(2)}) copy-start(f32[59,1024]{1,0:T(8,128)} %second_ref.1) | copy-start | bytes 724996
  30.6 23.9 %copy-start = (f32[59,1024]{1,0:T(8,128)S(1)}, f32[59,1024]{1,0:T(8,128)}, u32[]{:S(2)}) copy-start(f32[59,1024]{1,0:T(8,128)} %params_ref.1) | copy-start | bytes 724996
  30.6 23.9 %copy-start.1 = (f32[59,1024]{1,0:T(8,128)S(1)}, f32[59,1024]{1,0:T(8,128)}, u32[]{:S(2)}) copy-start(f32[59,1024]{1,0:T(8,128)} %first_ref.1) | copy-start | bytes 724996
  47.0 5.3 %collective-permute-start.3 = (f32[136,128]{1,0:T(8,128)S(1)}, f32[136,128]{1,0:T(8,128)S(1)}, u32[]{:S(2)}, u32[]{:S(2)}) collective-permute-start(f32[136,128]{1,0:T(8,128)S(1)} %shard_map.131.own_ref), channel_id=1, source_target_pairs={{0,3},{1,2},{2,1},{3,0},{4,7},{5,6},{6,5},{7,4},{8,11},{9,10},{10,... | collective-permute-start | bytes 208904 | tf_op jit(solution)/shard_map/ppermute | solution.py:779
  49.8 4.7 %collective-permute-start.2 = (f32[136,128]{1,0:T(8,128)S(1)}, f32[136,128]{1,0:T(8,128)S(1)}, u32[]{:S(2)}, u32[]{:S(2)}) collective-permute-start(f32[136,128]{1,0:T(8,128)S(1)} %shard_map.131.own_ref), channel_id=1, source_target_pairs={{0,2},{1,3},{2,0},{3,1},{4,6},{5,7},{6,4},{7,5},{8,10},{9,11},{10,... | collective-permute-start | bytes 208904 | tf_op jit(solution)/shard_map/ppermute | solution.py:779
  50.2 4.2 %collective-permute-start.1 = (f32[136,128]{1,0:T(8,128)S(1)}, f32[136,128]{1,0:T(8,128)S(1)}, u32[]{:S(2)}, u32[]{:S(2)}) collective-permute-start(f32[136,128]{1,0:T(8,128)S(1)} %shard_map.131.own_ref), channel_id=1, source_target_pairs={{0,1},{1,0},{2,3},{3,2},{4,5},{5,4},{6,7},{7,6},{8,9},{9,8},{10,11... | collective-permute-start | bytes 208904 | tf_op jit(solution)/shard_map/ppermute | solution.py:779

commit v7 on v6

--- a/solution.py
+++ b/solution.py
@@ -343,8 +343,46 @@
     shown_ref[...] = shown
 
 
+def write_sums(out_ref, summed, numbers, wanted, give, left):
+    odd = jnp.full((8, 128), lax.axis_index("gauss") & 1, I32) > 0
+    right = lax.broadcasted_iota(I32, (8, 128), 1) >= PEERS
+    upper = jnp.full((4, LOCAL), lax.axis_index("gauss") & 1, I32) > 0
+    pair = (summed[0:4], summed[4:8]) if give else (summed[4:8], summed[0:4])
+    stack = jnp.concatenate([jnp.where(upper, *pair), summed[8:9], numbers], axis=0)
+    rows = [[] for _ in range(6)]
+    for k in range(CAP):
+        lines = stack[:, k * PEERS : (k + 1) * PEERS]
+        lines = jnp.concatenate([lines, lines], axis=1)
+        for row in range(6):
+            rows[row].append(jnp.broadcast_to(lines[row : row + 1], (8, 128)))
+    for group in range(PEERS // 8):
+        span = slice(group * 8, (group + 1) * 8)
+        totals = [None] * 5
+        for k in range(CAP):
+            same = wanted[span] == rows[5][k]
+            for row in range(5):
+                term = jnp.where(same, rows[row][k], 0.0)
+                totals[row] = term if k == 0 else totals[row] + term
+        start = group * 8 * BLOCKS
+        turn = pltpu.roll(totals[4], PEERS, axis=1)
+        half = jnp.where(odd, turn, totals[4]) if give else jnp.where(odd, totals[4], turn)
+        out_ref[pl.ds(start + 1, 8, stride=BLOCKS), :] = jnp.where(right, half, left[span])
+        for row in range(4):
+            out_ref[pl.ds(start + 2 + row, 8, stride=BLOCKS), :] = totals[row]
+
+
 def render_kernel(
-    recv_ref, entries_ref, corner_ref, target_ref, out_ref, give_ref, share_ref, alpha_ref, grad_ref
+    recv_ref,
+    entries_ref,
+    corner_ref,
+    target_ref,
+    give_ref,
+    share_ref,
+    summed_ref,
+    numbers_ref,
+    wanted_ref,
+    alpha_ref,
+    grad_ref,
 ):
     lead = recv_ref[pl.ds(0, PEERS, stride=3), :]
     tail = recv_ref[pl.ds(1, PEERS, stride=3), :]
@@ -472,40 +510,20 @@
         )
     grads = jnp.concatenate(results, axis=1)
     summed = add_columns(grads, idx, hot, 2)
-    out_ref[pl.ds(0, PEERS, stride=BLOCKS), :] = pack_peers(summed[0:8])
-    give_ref[pl.ds(0, PEERS, stride=BLOCKS), :] = jnp.zeros((PEERS, 128), F32)
-    flat = jnp.concatenate([halves(summed[8:9]), jnp.zeros((112, PEERS), F32)], axis=0)
-    ninth = flat.T
-    odd = jnp.full((8, 128), lax.axis_index("gauss") & 1, I32) > 0
-    right = lax.broadcasted_iota(I32, (8, 128), 1) >= PEERS
     turned = sources.T
     wanted = jnp.concatenate([turned[0:PEERS], turned[PEERS:]], axis=1)
-    rows = [[] for _ in range(10)]
-    for k in range(CAP):
-        span = slice(k * PEERS, (k + 1) * PEERS)
-        lines = jnp.concatenate([summed[0:9, span], numbers[:, span]], axis=0)
-        lines = jnp.concatenate([lines, lines], axis=1)
-        for row in range(10):
-            rows[row].append(jnp.broadcast_to(lines[row : row + 1], (8, 128)))
-    for group in range(PEERS // 8):
-        ask = wanted[group * 8 : (group + 1) * 8]
-        totals = [None] * 9
-        for k in range(CAP):
-            same = ask == rows[9][k]
-            for row in range(9):
-                term = jnp.where(same, rows[row][k], 0.0)
-                totals[row] = term if k == 0 else totals[row] + term
-        start = group * 8 * BLOCKS
-        turn = pltpu.roll(totals[8], PEERS, axis=1)
-        keep = jnp.where(odd, totals[8], turn)
-        give = jnp.where(odd, turn, totals[8])
-        at = pl.ds(start + 1, 8, stride=BLOCKS)
-        out_ref[at, :] = jnp.where(right, keep, ninth[group * 8 : (group + 1) * 8])
-        give_ref[at, :] = jnp.where(right, give, 0.0)
-        for row in range(4):
-            at = pl.ds(start + 2 + row, 8, stride=BLOCKS)
-            out_ref[at, :] = jnp.where(odd, totals[4 + row], totals[row])
-            give_ref[at, :] = jnp.where(odd, totals[row], totals[4 + row])
+    summed_ref[...] = summed
+    numbers_ref[...] = numbers
+    wanted_ref[...] = wanted
+    give_ref[pl.ds(0, PEERS, stride=BLOCKS), :] = jnp.zeros((PEERS, 128), F32)
+    write_sums(give_ref, summed, numbers, wanted, True, jnp.zeros((PEERS, 128), F32))
+
+
+def keep_kernel(summed_ref, numbers_ref, wanted_ref, out_ref):
+    summed = summed_ref[...]
+    out_ref[pl.ds(0, PEERS, stride=BLOCKS), :] = pack_peers(summed[0:8])
+    flat = jnp.concatenate([halves(summed[8:9]), jnp.zeros((112, PEERS), F32)], axis=0)
+    write_sums(out_ref, summed, numbers_ref[...], wanted_ref[...], False, flat.T)
 
 
 def owner_kernel(recv_ref, order_ref, shown_ref, share_ref, out_ref):
@@ -631,7 +649,29 @@
     )
 
 
+def pull_view(ref, position, sigma, coeffs):
+    got = [ref[8 * i : 8 * i + 8, :] for i in range(9)]
+    shown = jnp.broadcast_to(ref[AT_CAMERA : AT_CAMERA + 1, :], (8, 128))
+    cam = [jnp.broadcast_to(shown[:, i : i + 1], (8, 128)) for i in range(16)]
+    _, pull = jax.vjp(lambda p, s, c: view_rows(p, s, c, cam), position, sigma, coeffs)
+    d_pos, d_sigma, d_coeff = pull([got[i] for i in (0, 1, 2, 3, 4, 6, 7, 8)])
+    return list(d_pos) + list(d_sigma) + list(d_coeff)
+
+
+def early_kernel(params_ref, own_ref, last_ref, dense_ref, own_part_ref, last_part_ref):
+    dense = params_ref[...].reshape(59, 8, 128)
+    dense_ref[...] = dense.reshape(59 * 8, 128)
+    rows = [dense[i] for i in range(59)]
+    sigma = covariance(rows[3:6], rows[6:10])
+    for ref, part_ref in ((own_ref, own_part_ref), (last_ref, last_part_ref)):
+        for i, piece in enumerate(pull_view(ref, rows[0:3], sigma, rows[11:59])):
+            part_ref[8 * i : 8 * i + 8, :] = piece
+
+
 def step_kernel(
+    dense_ref,
+    own_part_ref,
+    last_part_ref,
     params_ref,
     first_ref,
     second_ref,
@@ -649,24 +689,15 @@
     parts = (own_ref, near_ref, far_ref, last_ref)
     targets = targets_ref[...]
     placed = add_columns(incoming_columns(parts), targets, low_onehot(targets))
-    dense = params_ref[...].reshape(59, 8, 128)
-    rows = [dense[i] for i in range(59)]
+    rows = [dense_ref[8 * i : 8 * i + 8, :] for i in range(59)]
     sigma, pull_sigma = jax.vjp(covariance, rows[3:6], rows[6:10])
-    position, coeffs = rows[0:3], rows[11:59]
-    pos_parts, sigma_parts, coeff_parts, opacity_parts = [], [], [], []
-    for ref in parts:
-        got = [ref[8 * i : 8 * i + 8, :] for i in range(9)]
-        shown = jnp.broadcast_to(ref[AT_CAMERA : AT_CAMERA + 1, :], (8, 128))
-        cam = [jnp.broadcast_to(shown[:, i : i + 1], (8, 128)) for i in range(16)]
-        _, pull = jax.vjp(lambda p, s, c: view_rows(p, s, c, cam), position, sigma, coeffs)
-        d_pos, d_sigma, d_coeff = pull([got[i] for i in (0, 1, 2, 3, 4, 6, 7, 8)])
-        pos_parts.append(d_pos)
-        sigma_parts.append(d_sigma)
-        coeff_parts.append(d_coeff)
-        opacity_parts.append(got[5])
-    d_pos = [tree_sum([p[i] for p in pos_parts]) for i in range(3)]
-    d_sigma = [tree_sum([p[i] for p in sigma_parts]) for i in range(6)]
-    d_coeff = [tree_sum([p[i] for p in coeff_parts]) for i in range(48)]
+    near, far = [pull_view(ref, rows[0:3], sigma, rows[11:59]) for ref in (near_ref, far_ref)]
+    total = []
+    for i in range(57):
+        own, last = [ref[8 * i : 8 * i + 8, :] for ref in (own_part_ref, last_part_ref)]
+        total.append((own + near[i]) + (far[i] + last))
+    d_pos, d_sigma, d_coeff = total[0:3], total[3:9], total[9:57]
+    opacity_parts = [ref[40:48, :] for ref in parts]
     d_scale, d_quat = pull_sigma(d_sigma)
     d_logit = tree_sum(opacity_parts) * sigmoid_rest(rows[10])
     gradient = jnp.stack(d_pos + list(d_scale) + list(d_quat) + [d_logit] + d_coeff).reshape(
@@ -766,20 +797,25 @@
     )
     received = exchange(outgoing)
     back = ((BLOCKS * PEERS, 128), F32)
-    row_grads, give, share = call(
+    give, share, summed, numbers, asked = call(
         render_kernel,
-        [back, back, ((SHARE, 128), F32)],
+        [back, ((SHARE, 128), F32), ((ROWS, LOCAL), F32), ((1, LOCAL), F32), ((PEERS, 128), F32)],
         "vvvv",
         [pltpu.VMEM((TILES, 256, 256), F32), pltpu.VMEM((TILES, 256, 256), F32)],
     )(received, entries, corners, wanted)
     sibling = lax.ppermute(give, "gauss", [(i, i ^ 1) for i in range(PEERS)])
-    returned = exchange(row_grads + sibling)
+    (kept,) = call(keep_kernel, [back], "vvv")(summed, numbers, asked)
+    returned = exchange(kept + sibling)
     (own,) = call(owner_kernel, [((SENT, 128), F32)], "vvvv")(returned, order, shown, share)
     others = [
         lax.ppermute(own, "view", [(i, i ^ flip) for i in range(VIEWS)]) for flip in (1, 2, 3)
     ]
-    return call(step_kernel, [whole, whole, whole, whole], "vvvvvvvvv")(
-        params, first_moment, second_moment, own, *others, counts, landing
+    tiles = ((57 * 8, 128), F32)
+    dense, own_part, last_part = call(early_kernel, [((59 * 8, 128), F32), tiles, tiles], "vvv")(
+        params, own, others[2]
+    )
+    return call(step_kernel, [whole, whole, whole, whole], "vvvvvvvvvvvv")(
+        dense, own_part, last_part, params, first_moment, second_moment, own, *others, counts, landing
     )
 
 

time: 56.9 us -> 56.3 us (0.989)
  waiting for transfers between devices: 5.06 us -> 4.32 us
    pallas_call x2 -> x4, Pallas kernels: 5.32 us -> 5.52 us  [the longest x1 2.79 us: shards(): call(render_kernel, [back, ((SHARE, 128), F32), ((ROWS, LOCAL), F32), ((1...]
  transfers between devices with their start and end apart: 4 -> 4, of which waited for: 3 -> 3; matrix products, arithmetic and copies ran while one was open for 0% -> 0% of each run, Pallas kernels for 0% -> 1%
where the time goes in v7:
time: 56.3 us; the launch traced here: 56.1 us
  blocking collectives  39.3 us (70%)
  Pallas kernels  7.91 us (14%)
  waiting for transfers between devices  4.32 us (8%)
  starting transfers between devices  3.93 us (7%)
  between operations  0.69 us (1%)
    all_to_all x2, blocking collectives, exchange(): lax.all_to_all(parts, 'gauss', split_axis=0, concat_axis=0, tiled=True)  39.3 us
    ppermute x3, waiting for transfers between devices, shards(): lax.ppermute(own, 'view', [(i, i ^ flip) for i in range(VIEWS)])  3.64 us
    ppermute x3, starting transfers between devices, shards(): lax.ppermute(own, 'view', [(i, i ^ flip) for i in range(VIEWS)])  3.5 us
    pallas_call x1, Pallas kernels, shards(): call(render_kernel, [back, ((SHARE, 128), F32), ((ROWS, LOCAL), F32), ((1...  2.79 us
    pallas_call x1, Pallas kernels, shards(): call(step_kernel, [whole, whole, whole, whole], 'vvvvvvvvvvvv')  2 us
    pallas_call x1, Pallas kernels, shards(): call(send_kernel, [((3 * PEERS, 128), F32), columns, columns, ((2 * TILES...  1.96 us
  transfers between devices with their start and end apart: 4, of which 3 were waited for; matrix products, arithmetic and copies ran while one was open for 0% of the time, Pallas kernels for 1%

profile of v7, /device:TPU:1, one launch (start us, length us, event | category | flops | bytes accessed | tf_op | source)
XLA Modules:
  0.0 56.1 jit_solution(1734595786990806879)
XLA Ops:
  0.6 2.0 %shard_map.129 = (f32[192,128]{1,0:T(8,128)S(1)}, s32[1,1024]{1,0:T(1,128)S(1)}, s32[1,1024]{1,0:T(1,128)S(1)}, f32[8,256]{1,0:T(8,128)S(1)}, f32[3,4,256]{2,1,0...) custom-call(f32[59,1024]{1,0:T(8,128)} %params_ref.3, f32[59,1024]{1,0:T(8,128)} %first_ref.1, ...), custom_call_target="tpu_custom_call" | custom-call | tf_op jit(solution)/shard_map/pallas_call | solution.py:761
  2.6 23.3 %all_to_all.10 = f32[64,1,384]{2,1,0:T(1,128)S(1)} all-to-all(f32[64,1,384]{2,1,0:T(1,128)S(1)} %bitcast.10), channel_id=1, replica_groups=mesh['gauss'=64,'view'=4] {'gauss'}, dimensions={0} | all-to-all | bytes 196608 | tf_op jit(solution)/shard_map/all_to_all | solution.py:743
  25.9 2.8 %shard_map.130 = (f32[384,128]{1,0:T(8,128)S(1)}, f32[48,128]{1,0:T(8,128)S(1)}, f32[16,1024]{1,0:T(8,128)S(1)}, f32[1,1024]{1,0:T(1,128)S(1)}, f32[64,128]{1,0:T(8,128)S(1)}) custom-call(f32[192,128]{1,0:T(8,128)S(1)} %bitcast.9, s32[1,1024]{1,0:T(1,128)S(1)} %get-tuple-element.21.entries_ref, f32[8,256]{1,0:T(8,128)S(1)} %get-tuple-element.22.corner_ref, ...), custom_call_target="tpu_custom_call" | custom-call | tf_op jit(solution)/shard_map/pallas_call | solution.py:800
  28.7 0.4 collective-permute-start
  29.2 0.4 shard_map.131
  29.5 0.7 %collective-permute-done = f32[384,128]{1,0:T(8,128)S(1)} collective-permute-done((f32[384,128]{1,0:T(8,128)S(1)}, f32[384,128]{1,0:T(8,128)S(1)}, u32[]{:S(2)}, u32[]{:S(2)}) %collective-permute-start) | collective-permute-done | bytes 196640 | tf_op jit(solution)/shard_map/ppermute | solution.py:806
  30.2 0.0 copy-start
  30.3 15.9 %all_to_all.11 = f32[64,1,768]{2,1,0:T(1,128)S(1)} all-to-all(f32[64,1,768]{2,1,0:T(1,128)S(1)} %bitcast.11), channel_id=1, replica_groups=mesh['gauss'=64,'view'=4] {'gauss'}, dimensions={0} | all-to-all | bytes 393216 | tf_op jit(solution)/shard_map/all_to_all | solution.py:743
  46.2 0.0 copy-start.2
  46.2 0.4 shard_map.132.own_ref
  46.6 0.0 copy-start.1
  46.6 2.8 %collective-permute-start.1 = (f32[136,128]{1,0:T(8,128)S(1)}, f32[136,128]{1,0:T(8,128)S(1)}, u32[]{:S(2)}, u32[]{:S(2)}) collective-permute-start(f32[136,128]{1,0:T(8,128)S(1)} %shard_map.132.own_ref), channel_id=1, source_target_pairs={{0,3},{1,2},{2,1},{3,0},{4,7},{5,6},{6,5},{7,4},{8,11},{9,10},{10,... | collective-permute-start | bytes 208904 | tf_op jit(solution)/shard_map/ppermute | solution.py:811
  49.5 0.4 collective-permute-start.3
  49.9 0.2 collective-permute-start.2
  50.1 1.8 %collective-permute-done.1.last_ref = f32[136,128]{1,0:T(8,128)S(1)} collective-permute-done((f32[136,128]{1,0:T(8,128)S(1)}, f32[136,128]{1,0:T(8,128)S(1)}, u32[]{:S(2)}, u32[]{:S(2)}) %collective-permute-start.1) | collective-permute-done | bytes 69664 | tf_op jit(solution)/shard_map/ppermute | solution.py:811
  52.0 0.0 copy-done
  52.0 0.3 shard_map.133
  52.3 1.8 %collective-permute-done.3.far_ref = f32[136,128]{1,0:T(8,128)S(1)} collective-permute-done((f32[136,128]{1,0:T(8,128)S(1)}, f32[136,128]{1,0:T(8,128)S(1)}, u32[]{:S(2)}, u32[]{:S(2)}) %collective-permute-start.3) | collective-permute-done | bytes 69664 | tf_op jit(solution)/shard_map/ppermute | solution.py:811
  54.1 0.0 collective-permute-done.2.near_ref
  54.1 0.0 copy-done.2
  54.1 0.0 copy-done.1
  54.1 2.0 %shard_map.134 = (f32[59,1024]{1,0:T(8,128)}, f32[59,1024]{1,0:T(8,128)}, f32[59,1024]{1,0:T(8,128)}, f32[59,1024]{1,0:T(8,128)}) custom-call(f32[472,128]{1,0:T(8,128)S(1)} %get-tuple-element.31.dense_ref, f32[456,128]{1,0:T(8,128)S(1)} %get-tuple-element.32.own_part_ref, f32[456,128]{1,0:T(8,128)S(1)} %get-tuple-element.33.last_part_ref, ...), custom_call_target="tpu_custom_call" | custom-call | tf_op jit(solution)/shard_map/pallas_call | solution.py:817
  (1 shorter events, 0.0 us)
Async XLA Ops:
  28.7 1.5 %collective-permute-start = (f32[384,128]{1,0:T(8,128)S(1)}, f32[384,128]{1,0:T(8,128)S(1)}, u32[]{:S(2)}, u32[]{:S(2)}) collective-permute-start(f32[384,128]{1,0:T(8,128)S(1)} %get-tuple-element.27), channel_id=1, source_target_pairs={{0,4},{4,0},{8,12},{12,8},{16,20},{20,16},{24,28},{28,24},{32,36},... | collective-permute-start | bytes 589832 | tf_op jit(solution)/shard_map/ppermute | solution.py:806
  30.2 21.7 %copy-start = (f32[59,1024]{1,0:T(8,128)S(1)}, f32[59,1024]{1,0:T(8,128)}, u32[]{:S(2)}) copy-start(f32[59,1024]{1,0:T(8,128)} %params_ref.3) | copy-start | bytes 724996
  46.2 7.9 %copy-start.2 = (f32[59,1024]{1,0:T(8,128)S(1)}, f32[59,1024]{1,0:T(8,128)}, u32[]{:S(2)}) copy-start(f32[59,1024]{1,0:T(8,128)} %second_ref.1) | copy-start | bytes 724996
  46.6 7.5 %copy-start.1 = (f32[59,1024]{1,0:T(8,128)S(1)}, f32[59,1024]{1,0:T(8,128)}, u32[]{:S(2)}) copy-start(f32[59,1024]{1,0:T(8,128)} %first_ref.1) | copy-start | bytes 724996
  46.6 5.3 %collective-permute-start.1 = (f32[136,128]{1,0:T(8,128)S(1)}, f32[136,128]{1,0:T(8,128)S(1)}, u32[]{:S(2)}, u32[]{:S(2)}) collective-permute-start(f32[136,128]{1,0:T(8,128)S(1)} %shard_map.132.own_ref), channel_id=1, source_target_pairs={{0,3},{1,2},{2,1},{3,0},{4,7},{5,6},{6,5},{7,4},{8,11},{9,10},{10,... | collective-permute-start | bytes 208904 | tf_op jit(solution)/shard_map/ppermute | solution.py:811
  49.5 4.7 %collective-permute-start.3 = (f32[136,128]{1,0:T(8,128)S(1)}, f32[136,128]{1,0:T(8,128)S(1)}, u32[]{:S(2)}, u32[]{:S(2)}) collective-permute-start(f32[136,128]{1,0:T(8,128)S(1)} %shard_map.132.own_ref), channel_id=1, source_target_pairs={{0,2},{1,3},{2,0},{3,1},{4,6},{5,7},{6,4},{7,5},{8,10},{9,11},{10,... | collective-permute-start | bytes 208904 | tf_op jit(solution)/shard_map/ppermute | solution.py:811
  49.9 4.2 %collective-permute-start.2 = (f32[136,128]{1,0:T(8,128)S(1)}, f32[136,128]{1,0:T(8,128)S(1)}, u32[]{:S(2)}, u32[]{:S(2)}) collective-permute-start(f32[136,128]{1,0:T(8,128)S(1)} %shard_map.132.own_ref), channel_id=1, source_target_pairs={{0,1},{1,0},{2,3},{3,2},{4,5},{5,4},{6,7},{7,6},{8,9},{9,8},{10,11... | collective-permute-start | bytes 208904 | tf_op jit(solution)/shard_map/ppermute | solution.py:811

commit v8 on v7

--- a/solution.py
+++ b/solution.py
@@ -343,12 +343,14 @@
     shown_ref[...] = shown
 
 
-def write_sums(out_ref, summed, numbers, wanted, give, left):
-    odd = jnp.full((8, 128), lax.axis_index("gauss") & 1, I32) > 0
+def odd_core(shape):
+    return jnp.full(shape, lax.axis_index("gauss") & 1, I32) > 0
+
+
+def write_sums(out_ref, four, ninth, numbers, wanted, give, left):
+    odd = odd_core((8, 128))
     right = lax.broadcasted_iota(I32, (8, 128), 1) >= PEERS
-    upper = jnp.full((4, LOCAL), lax.axis_index("gauss") & 1, I32) > 0
-    pair = (summed[0:4], summed[4:8]) if give else (summed[4:8], summed[0:4])
-    stack = jnp.concatenate([jnp.where(upper, *pair), summed[8:9], numbers], axis=0)
+    stack = jnp.concatenate([four, ninth, numbers], axis=0)
     rows = [[] for _ in range(6)]
     for k in range(CAP):
         lines = stack[:, k * PEERS : (k + 1) * PEERS]
@@ -378,7 +380,9 @@
     target_ref,
     give_ref,
     share_ref,
-    summed_ref,
+    given_ref,
+    rest_ref,
+    index_ref,
     numbers_ref,
     wanted_ref,
     alpha_ref,
@@ -509,21 +513,35 @@
             )
         )
     grads = jnp.concatenate(results, axis=1)
-    summed = add_columns(grads, idx, hot, 2)
+    odd = odd_core((4, LOCAL))
+    first = jnp.where(odd, grads[0:4], grads[4:8])
+    first = jnp.concatenate([first, grads[8:9], jnp.zeros((3, LOCAL), F32)], axis=0)
+    given = add_columns(first, idx, hot, 2)
+    given_ref[...] = given
+    rest_ref[...] = jnp.concatenate(
+        [jnp.where(odd, grads[4:8], grads[0:4]), jnp.zeros((4, LOCAL), F32)], axis=0
+    )
+    index_ref[...] = idx
     turned = sources.T
     wanted = jnp.concatenate([turned[0:PEERS], turned[PEERS:]], axis=1)
-    summed_ref[...] = summed
     numbers_ref[...] = numbers
     wanted_ref[...] = wanted
-    give_ref[pl.ds(0, PEERS, stride=BLOCKS), :] = jnp.zeros((PEERS, 128), F32)
-    write_sums(give_ref, summed, numbers, wanted, True, jnp.zeros((PEERS, 128), F32))
-
-
-def keep_kernel(summed_ref, numbers_ref, wanted_ref, out_ref):
-    summed = summed_ref[...]
-    out_ref[pl.ds(0, PEERS, stride=BLOCKS), :] = pack_peers(summed[0:8])
-    flat = jnp.concatenate([halves(summed[8:9]), jnp.zeros((112, PEERS), F32)], axis=0)
-    write_sums(out_ref, summed, numbers_ref[...], wanted_ref[...], False, flat.T)
+    blank = jnp.zeros((PEERS, 128), F32)
+    give_ref[pl.ds(0, PEERS, stride=BLOCKS), :] = blank
+    write_sums(give_ref, given[0:4], given[4:5], numbers, wanted, True, blank)
+
+
+def keep_kernel(given_ref, rest_ref, index_ref, numbers_ref, wanted_ref, out_ref):
+    idx = index_ref[...]
+    given = given_ref[...]
+    kept = add_columns(rest_ref[...], idx, low_onehot(idx), 2)[0:4]
+    odd = odd_core((4, LOCAL))
+    halves_in_order = [jnp.where(odd, given[0:4], kept), jnp.where(odd, kept, given[0:4])]
+    out_ref[pl.ds(0, PEERS, stride=BLOCKS), :] = pack_peers(
+        jnp.concatenate(halves_in_order, axis=0)
+    )
+    flat = jnp.concatenate([halves(given[4:5]), jnp.zeros((112, PEERS), F32)], axis=0)
+    write_sums(out_ref, kept, given[4:5], numbers_ref[...], wanted_ref[...], False, flat.T)
 
 
 def owner_kernel(recv_ref, order_ref, shown_ref, share_ref, out_ref):
@@ -797,14 +815,23 @@
     )
     received = exchange(outgoing)
     back = ((BLOCKS * PEERS, 128), F32)
-    give, share, summed, numbers, asked = call(
+    eight = ((8, LOCAL), F32)
+    give, share, given, rest, index, numbers, asked = call(
         render_kernel,
-        [back, ((SHARE, 128), F32), ((ROWS, LOCAL), F32), ((1, LOCAL), F32), ((PEERS, 128), F32)],
+        [
+            back,
+            ((SHARE, 128), F32),
+            eight,
+            eight,
+            columns,
+            ((1, LOCAL), F32),
+            ((PEERS, 128), F32),
+        ],
         "vvvv",
         [pltpu.VMEM((TILES, 256, 256), F32), pltpu.VMEM((TILES, 256, 256), F32)],
     )(received, entries, corners, wanted)
     sibling = lax.ppermute(give, "gauss", [(i, i ^ 1) for i in range(PEERS)])
-    (kept,) = call(keep_kernel, [back], "vvv")(summed, numbers, asked)
+    (kept,) = call(keep_kernel, [back], "vvvvv")(given, rest, index, numbers, asked)
     returned = exchange(kept + sibling)
     (own,) = call(owner_kernel, [((SENT, 128), F32)], "vvvv")(returned, order, shown, share)
     others = [

time: 56.3 us -> 56.2 us (level)
  transfers between devices with their start and end apart: 4 -> 4, of which waited for: 3 -> 3; matrix products, arithmetic and copies ran while one was open for 0% -> 0% of each run, Pallas kernels for 1% -> 2%
where the time goes in v8:
time: 56.2 us; the launch traced here: 56.1 us
  blocking collectives  39.3 us (70%)
  Pallas kernels  8.07 us (14%)
  waiting for transfers between devices  4.08 us (7%)
  starting transfers between devices  3.93 us (7%)
  between operations  0.69 us (1%)
    all_to_all x2, blocking collectives, exchange(): lax.all_to_all(parts, 'gauss', split_axis=0, concat_axis=0, tiled=True)  39.3 us
    ppermute x3, waiting for transfers between devices, shards(): lax.ppermute(own, 'view', [(i, i ^ flip) for i in range(VIEWS)])  3.64 us
    ppermute x3, starting transfers between devices, shards(): lax.ppermute(own, 'view', [(i, i ^ flip) for i in range(VIEWS)])  3.5 us
    pallas_call x1, Pallas kernels, shards(): call(render_kernel, [back, ((SHARE, 128), F32), eight, eight, columns, ((...  2.72 us
    pallas_call x1, Pallas kernels, shards(): call(step_kernel, [whole, whole, whole, whole], 'vvvvvvvvvvvv')  2 us
    pallas_call x1, Pallas kernels, shards(): call(send_kernel, [((3 * PEERS, 128), F32), columns, columns, ((2 * TILES...  1.96 us
  transfers between devices with their start and end apart: 4, of which 3 were waited for; matrix products, arithmetic and copies ran while one was open for 0% of the time, Pallas kernels for 2%

profile of v8, /device:TPU:1, one launch (start us, length us, event | category | flops | bytes accessed | tf_op | source)
XLA Modules:
  0.0 56.1 jit_solution(13417005495560376604)
XLA Ops:
  0.6 2.0 %shard_map.129 = (f32[192,128]{1,0:T(8,128)S(1)}, s32[1,1024]{1,0:T(1,128)S(1)}, s32[1,1024]{1,0:T(1,128)S(1)}, f32[8,256]{1,0:T(8,128)S(1)}, f32[3,4,256]{2,1,0...) custom-call(f32[59,1024]{1,0:T(8,128)} %params_ref.3, f32[59,1024]{1,0:T(8,128)} %first_ref.1, ...), custom_call_target="tpu_custom_call" | custom-call | tf_op jit(solution)/shard_map/pallas_call | solution.py:779
  2.6 23.3 %all_to_all.10 = f32[64,1,384]{2,1,0:T(1,128)S(1)} all-to-all(f32[64,1,384]{2,1,0:T(1,128)S(1)} %bitcast.10), channel_id=1, replica_groups=mesh['gauss'=64,'view'=4] {'gauss'}, dimensions={0} | all-to-all | bytes 196608 | tf_op jit(solution)/shard_map/all_to_all | solution.py:761
  25.9 2.7 %shard_map.130 = (f32[384,128]{1,0:T(8,128)S(1)}, f32[48,128]{1,0:T(8,128)S(1)}, f32[8,1024]{1,0:T(8,128)S(1)}, f32[8,1024]{1,0:T(8,128)S(1)}, s32[1,1024]{1,0:T...) custom-call(f32[192,128]{1,0:T(8,128)S(1)} %bitcast.9, s32[1,1024]{1,0:T(1,128)S(1)} %get-tuple-element.23.entries_ref, ...), custom_call_target="tpu_custom_call" | custom-call | tf_op jit(solution)/shard_map/pallas_call | solution.py:819
  28.7 0.4 collective-permute-start
  29.1 0.6 %shard_map.131 = f32[384,128]{1,0:T(8,128)S(1)} custom-call(f32[8,1024]{1,0:T(8,128)S(1)} %get-tuple-element.26.given_ref, f32[8,1024]{1,0:T(8,128)S(1)} %get-tuple-element.27.rest_ref, s32[1,1024]{1,0:T(1,128)S(1)} %get-tuple-element.28.index_ref, f32[1,1024]{1,0:T(1,128)S(1)} %get-tuple-element.29.numbers_ref, f32[64,128]{1,0:T(8,128)S(1)} %get-tuple-element.30.wanted_ref), custom_call_target="tpu_custom_call" | custom-call | tf_op jit(solution)/shard_map/pallas_call | solution.py:834
  29.7 0.4 collective-permute-done
  30.2 0.0 copy-start
  30.2 15.9 %all_to_all.11 = f32[64,1,768]{2,1,0:T(1,128)S(1)} all-to-all(f32[64,1,768]{2,1,0:T(1,128)S(1)} %bitcast.11), channel_id=1, replica_groups=mesh['gauss'=64,'view'=4] {'gauss'}, dimensions={0} | all-to-all | bytes 393216 | tf_op jit(solution)/shard_map/all_to_all | solution.py:761
  46.1 0.0 copy-start.2
  46.1 0.4 shard_map.132.own_ref
  46.5 0.0 copy-start.1
  46.6 2.8 %collective-permute-start.1 = (f32[136,128]{1,0:T(8,128)S(1)}, f32[136,128]{1,0:T(8,128)S(1)}, u32[]{:S(2)}, u32[]{:S(2)}) collective-permute-start(f32[136,128]{1,0:T(8,128)S(1)} %shard_map.132.own_ref), channel_id=1, source_target_pairs={{0,3},{1,2},{2,1},{3,0},{4,7},{5,6},{6,5},{7,4},{8,11},{9,10},{10,... | collective-permute-start | bytes 208904 | tf_op jit(solution)/shard_map/ppermute | solution.py:838
  49.4 0.4 collective-permute-start.3
  49.8 0.2 collective-permute-start.2
  50.1 1.8 %collective-permute-done.1.last_ref = f32[136,128]{1,0:T(8,128)S(1)} collective-permute-done((f32[136,128]{1,0:T(8,128)S(1)}, f32[136,128]{1,0:T(8,128)S(1)}, u32[]{:S(2)}, u32[]{:S(2)}) %collective-permute-start.1) | collective-permute-done | bytes 69664 | tf_op jit(solution)/shard_map/ppermute | solution.py:838
  51.9 0.0 copy-done
  51.9 0.3 shard_map.133
  52.2 1.8 %collective-permute-done.3.far_ref = f32[136,128]{1,0:T(8,128)S(1)} collective-permute-done((f32[136,128]{1,0:T(8,128)S(1)}, f32[136,128]{1,0:T(8,128)S(1)}, u32[]{:S(2)}, u32[]{:S(2)}) %collective-permute-start.3) | collective-permute-done | bytes 69664 | tf_op jit(solution)/shard_map/ppermute | solution.py:838
  54.0 0.0 collective-permute-done.2.near_ref
  54.0 0.0 copy-done.2
  54.1 0.0 copy-done.1
  54.1 2.0 %shard_map.134 = (f32[59,1024]{1,0:T(8,128)}, f32[59,1024]{1,0:T(8,128)}, f32[59,1024]{1,0:T(8,128)}, f32[59,1024]{1,0:T(8,128)}) custom-call(f32[472,128]{1,0:T(8,128)S(1)} %get-tuple-element.35.dense_ref, f32[456,128]{1,0:T(8,128)S(1)} %get-tuple-element.36.own_part_ref, f32[456,128]{1,0:T(8,128)S(1)} %get-tuple-element.37.last_part_ref, ...), custom_call_target="tpu_custom_call" | custom-call | tf_op jit(solution)/shard_map/pallas_call | solution.py:844
  (1 shorter events, 0.0 us)
Async XLA Ops:
  28.7 1.5 %collective-permute-start = (f32[384,128]{1,0:T(8,128)S(1)}, f32[384,128]{1,0:T(8,128)S(1)}, u32[]{:S(2)}, u32[]{:S(2)}) collective-permute-start(f32[384,128]{1,0:T(8,128)S(1)} %get-tuple-element.31), channel_id=1, source_target_pairs={{0,4},{4,0},{8,12},{12,8},{16,20},{20,16},{24,28},{28,24},{32,36},... | collective-permute-start | bytes 589832 | tf_op jit(solution)/shard_map/ppermute | solution.py:833
  30.2 21.7 %copy-start = (f32[59,1024]{1,0:T(8,128)S(1)}, f32[59,1024]{1,0:T(8,128)}, u32[]{:S(2)}) copy-start(f32[59,1024]{1,0:T(8,128)} %params_ref.3) | copy-start | bytes 724996
  46.1 7.9 %copy-start.2 = (f32[59,1024]{1,0:T(8,128)S(1)}, f32[59,1024]{1,0:T(8,128)}, u32[]{:S(2)}) copy-start(f32[59,1024]{1,0:T(8,128)} %second_ref.1) | copy-start | bytes 724996
  46.5 7.5 %copy-start.1 = (f32[59,1024]{1,0:T(8,128)S(1)}, f32[59,1024]{1,0:T(8,128)}, u32[]{:S(2)}) copy-start(f32[59,1024]{1,0:T(8,128)} %first_ref.1) | copy-start | bytes 724996
  46.6 5.3 %collective-permute-start.1 = (f32[136,128]{1,0:T(8,128)S(1)}, f32[136,128]{1,0:T(8,128)S(1)}, u32[]{:S(2)}, u32[]{:S(2)}) collective-permute-start(f32[136,128]{1,0:T(8,128)S(1)} %shard_map.132.own_ref), channel_id=1, source_target_pairs={{0,3},{1,2},{2,1},{3,0},{4,7},{5,6},{6,5},{7,4},{8,11},{9,10},{10,... | collective-permute-start | bytes 208904 | tf_op jit(solution)/shard_map/ppermute | solution.py:838
  49.4 4.7 %collective-permute-start.3 = (f32[136,128]{1,0:T(8,128)S(1)}, f32[136,128]{1,0:T(8,128)S(1)}, u32[]{:S(2)}, u32[]{:S(2)}) collective-permute-start(f32[136,128]{1,0:T(8,128)S(1)} %shard_map.132.own_ref), channel_id=1, source_target_pairs={{0,2},{1,3},{2,0},{3,1},{4,6},{5,7},{6,4},{7,5},{8,10},{9,11},{10,... | collective-permute-start | bytes 208904 | tf_op jit(solution)/shard_map/ppermute | solution.py:838
  49.8 4.2 %collective-permute-start.2 = (f32[136,128]{1,0:T(8,128)S(1)}, f32[136,128]{1,0:T(8,128)S(1)}, u32[]{:S(2)}, u32[]{:S(2)}) collective-permute-start(f32[136,128]{1,0:T(8,128)S(1)} %shard_map.132.own_ref), channel_id=1, source_target_pairs={{0,1},{1,0},{2,3},{3,2},{4,5},{5,4},{6,7},{7,6},{8,9},{9,8},{10,11... | collective-permute-start | bytes 208904 | tf_op jit(solution)/shard_map/ppermute | solution.py:838

commit v9 on v8

--- a/solution.py
+++ b/solution.py
@@ -427,9 +427,11 @@
         heres.append(here)
         offs_u.append(off_u)
         offs_w.append(off_w)
-    log_keeps = [jnp.log(1.0 - alpha_ref[t]) for t in tiles]
-    logs = [jnp.concatenate(split(x, 2), axis=1) for x in log_keeps]
-    befores = [jnp.dot(x, before_mask, preferred_element_type=F32) for x in logs]
+    log_keeps, befores = [], []
+    for t in tiles:
+        log_keeps.append(jnp.log(1.0 - alpha_ref[t]))
+        logs = jnp.concatenate(split(log_keeps[t], 2), axis=1)
+        befores.append(jnp.dot(logs, before_mask, preferred_element_type=F32))
     weights = [jnp.exp(befores[t]) * alpha_ref[t] for t in tiles]
     weight_parts = [split(x, 2) for x in weights]
     colour_parts = [split(here[6:9], 3) for here in heres]
@@ -462,9 +464,11 @@
                 preferred_element_type=F32,
             )
         )
-    weighteds = [pulls[t] * weights[t] for t in tiles]
-    flows = [jnp.concatenate(split(x, 2), axis=1) for x in weighteds]
-    afters = [jnp.dot(x, after_mask, preferred_element_type=F32) for x in flows]
+    weighteds, afters = [], []
+    for t in tiles:
+        weighteds.append(pulls[t] * weights[t])
+        flow = jnp.concatenate(split(weighteds[t], 2), axis=1)
+        afters.append(jnp.dot(flow, after_mask, preferred_element_type=F32))
     for t in tiles:
         grad_ref[t] = weighteds[t] - afters[t] * (alpha_ref[t] * jnp.exp(-log_keeps[t]))
     results = []
@@ -605,7 +609,8 @@
 def adam(params, first_old, second_old, gradient):
     first = 0.9 * first_old + 0.1 * gradient
     second = 0.999 * second_old + 0.001 * gradient * gradient
-    stepped = params - rates_column() * (first / BIAS_ONE) / (jnp.sqrt(second / BIAS_TWO) + 1e-15)
+    scale = rates_column() * (1.0 / BIAS_ONE)
+    stepped = params - scale * first / (jnp.sqrt(second * (1.0 / BIAS_TWO)) + 1e-15)
     return stepped, first, second
 
 

time: 56.2 us -> 56.2 us (level)
  no operation moved by 1% of the time
where the time goes in v9:
time: 56.2 us; the launch traced here: 56.1 us
  blocking collectives  39.3 us (70%)
  Pallas kernels  8.07 us (14%)
  waiting for transfers between devices  4.08 us (7%)
  starting transfers between devices  3.93 us (7%)
  between operations  0.69 us (1%)
    all_to_all x2, blocking collectives, exchange(): lax.all_to_all(parts, 'gauss', split_axis=0, concat_axis=0, tiled=True)  39.3 us
    ppermute x3, waiting for transfers between devices, shards(): lax.ppermute(own, 'view', [(i, i ^ flip) for i in range(VIEWS)])  3.64 us
    ppermute x3, starting transfers between devices, shards(): lax.ppermute(own, 'view', [(i, i ^ flip) for i in range(VIEWS)])  3.5 us
    pallas_call x1, Pallas kernels, shards(): call(render_kernel, [back, ((SHARE, 128), F32), eight, eight, columns, ((...  2.72 us
    pallas_call x1, Pallas kernels, shards(): call(step_kernel, [whole, whole, whole, whole], 'vvvvvvvvvvvv')  2 us
    pallas_call x1, Pallas kernels, shards(): call(send_kernel, [((3 * PEERS, 128), F32), columns, columns, ((2 * TILES...  1.96 us
  transfers between devices with their start and end apart: 4, of which 3 were waited for; matrix products, arithmetic and copies ran while one was open for 0% of the time, Pallas kernels for 2%

profile of v9, /device:TPU:1, one launch (start us, length us, event | category | flops | bytes accessed | tf_op | source)
XLA Modules:
  0.0 56.1 jit_solution(18437418486934693731)
XLA Ops:
  0.6 2.0 %shard_map.129 = (f32[192,128]{1,0:T(8,128)S(1)}, s32[1,1024]{1,0:T(1,128)S(1)}, s32[1,1024]{1,0:T(1,128)S(1)}, f32[8,256]{1,0:T(8,128)S(1)}, f32[3,4,256]{2,1,0...) custom-call(f32[59,1024]{1,0:T(8,128)} %params_ref.3, f32[59,1024]{1,0:T(8,128)} %first_ref.1, ...), custom_call_target="tpu_custom_call" | custom-call | tf_op jit(solution)/shard_map/pallas_call | solution.py:784
  2.6 23.3 %all_to_all.10 = f32[64,1,384]{2,1,0:T(1,128)S(1)} all-to-all(f32[64,1,384]{2,1,0:T(1,128)S(1)} %bitcast.10), channel_id=1, replica_groups=mesh['gauss'=64,'view'=4] {'gauss'}, dimensions={0} | all-to-all | bytes 196608 | tf_op jit(solution)/shard_map/all_to_all | solution.py:766
  25.9 2.7 %shard_map.130 = (f32[384,128]{1,0:T(8,128)S(1)}, f32[48,128]{1,0:T(8,128)S(1)}, f32[8,1024]{1,0:T(8,128)S(1)}, f32[8,1024]{1,0:T(8,128)S(1)}, s32[1,1024]{1,0:T...) custom-call(f32[192,128]{1,0:T(8,128)S(1)} %bitcast.9, s32[1,1024]{1,0:T(1,128)S(1)} %get-tuple-element.23.entries_ref, ...), custom_call_target="tpu_custom_call" | custom-call | tf_op jit(solution)/shard_map/pallas_call | solution.py:824
  28.7 0.4 collective-permute-start
  29.1 0.6 %shard_map.131 = f32[384,128]{1,0:T(8,128)S(1)} custom-call(f32[8,1024]{1,0:T(8,128)S(1)} %get-tuple-element.26.given_ref, f32[8,1024]{1,0:T(8,128)S(1)} %get-tuple-element.27.rest_ref, s32[1,1024]{1,0:T(1,128)S(1)} %get-tuple-element.28.index_ref, f32[1,1024]{1,0:T(1,128)S(1)} %get-tuple-element.29.numbers_ref, f32[64,128]{1,0:T(8,128)S(1)} %get-tuple-element.30.wanted_ref), custom_call_target="tpu_custom_call" | custom-call | tf_op jit(solution)/shard_map/pallas_call | solution.py:839
  29.7 0.4 collective-permute-done
  30.2 0.0 copy-start
  30.2 15.9 %all_to_all.11 = f32[64,1,768]{2,1,0:T(1,128)S(1)} all-to-all(f32[64,1,768]{2,1,0:T(1,128)S(1)} %bitcast.11), channel_id=1, replica_groups=mesh['gauss'=64,'view'=4] {'gauss'}, dimensions={0} | all-to-all | bytes 393216 | tf_op jit(solution)/shard_map/all_to_all | solution.py:766
  46.1 0.0 copy-start.2
  46.1 0.4 shard_map.132.own_ref
  46.5 0.0 copy-start.1
  46.6 2.8 %collective-permute-start.1 = (f32[136,128]{1,0:T(8,128)S(1)}, f32[136,128]{1,0:T(8,128)S(1)}, u32[]{:S(2)}, u32[]{:S(2)}) collective-permute-start(f32[136,128]{1,0:T(8,128)S(1)} %shard_map.132.own_ref), channel_id=1, source_target_pairs={{0,3},{1,2},{2,1},{3,0},{4,7},{5,6},{6,5},{7,4},{8,11},{9,10},{10,... | collective-permute-start | bytes 208904 | tf_op jit(solution)/shard_map/ppermute | solution.py:843
  49.4 0.4 collective-permute-start.3
  49.8 0.2 collective-permute-start.2
  50.1 1.8 %collective-permute-done.1.last_ref = f32[136,128]{1,0:T(8,128)S(1)} collective-permute-done((f32[136,128]{1,0:T(8,128)S(1)}, f32[136,128]{1,0:T(8,128)S(1)}, u32[]{:S(2)}, u32[]{:S(2)}) %collective-permute-start.1) | collective-permute-done | bytes 69664 | tf_op jit(solution)/shard_map/ppermute | solution.py:843
  51.9 0.0 copy-done
  51.9 0.3 shard_map.133
  52.2 1.8 %collective-permute-done.3.far_ref = f32[136,128]{1,0:T(8,128)S(1)} collective-permute-done((f32[136,128]{1,0:T(8,128)S(1)}, f32[136,128]{1,0:T(8,128)S(1)}, u32[]{:S(2)}, u32[]{:S(2)}) %collective-permute-start.3) | collective-permute-done | bytes 69664 | tf_op jit(solution)/shard_map/ppermute | solution.py:843
  54.0 0.0 collective-permute-done.2.near_ref
  54.0 0.0 copy-done.2
  54.1 0.0 copy-done.1
  54.1 2.0 %shard_map.134 = (f32[59,1024]{1,0:T(8,128)}, f32[59,1024]{1,0:T(8,128)}, f32[59,1024]{1,0:T(8,128)}, f32[59,1024]{1,0:T(8,128)}) custom-call(f32[472,128]{1,0:T(8,128)S(1)} %get-tuple-element.35.dense_ref, f32[456,128]{1,0:T(8,128)S(1)} %get-tuple-element.36.own_part_ref, f32[456,128]{1,0:T(8,128)S(1)} %get-tuple-element.37.last_part_ref, ...), custom_call_target="tpu_custom_call" | custom-call | tf_op jit(solution)/shard_map/pallas_call | solution.py:849
  (1 shorter events, 0.0 us)
Async XLA Ops:
  28.7 1.5 %collective-permute-start = (f32[384,128]{1,0:T(8,128)S(1)}, f32[384,128]{1,0:T(8,128)S(1)}, u32[]{:S(2)}, u32[]{:S(2)}) collective-permute-start(f32[384,128]{1,0:T(8,128)S(1)} %get-tuple-element.31), channel_id=1, source_target_pairs={{0,4},{4,0},{8,12},{12,8},{16,20},{20,16},{24,28},{28,24},{32,36},... | collective-permute-start | bytes 589832 | tf_op jit(solution)/shard_map/ppermute | solution.py:838
  30.2 21.7 %copy-start = (f32[59,1024]{1,0:T(8,128)S(1)}, f32[59,1024]{1,0:T(8,128)}, u32[]{:S(2)}) copy-start(f32[59,1024]{1,0:T(8,128)} %params_ref.3) | copy-start | bytes 724996
  46.1 7.9 %copy-start.2 = (f32[59,1024]{1,0:T(8,128)S(1)}, f32[59,1024]{1,0:T(8,128)}, u32[]{:S(2)}) copy-start(f32[59,1024]{1,0:T(8,128)} %second_ref.1) | copy-start | bytes 724996
  46.5 7.5 %copy-start.1 = (f32[59,1024]{1,0:T(8,128)S(1)}, f32[59,1024]{1,0:T(8,128)}, u32[]{:S(2)}) copy-start(f32[59,1024]{1,0:T(8,128)} %first_ref.1) | copy-start | bytes 724996
  46.6 5.3 %collective-permute-start.1 = (f32[136,128]{1,0:T(8,128)S(1)}, f32[136,128]{1,0:T(8,128)S(1)}, u32[]{:S(2)}, u32[]{:S(2)}) collective-permute-start(f32[136,128]{1,0:T(8,128)S(1)} %shard_map.132.own_ref), channel_id=1, source_target_pairs={{0,3},{1,2},{2,1},{3,0},{4,7},{5,6},{6,5},{7,4},{8,11},{9,10},{10,... | collective-permute-start | bytes 208904 | tf_op jit(solution)/shard_map/ppermute | solution.py:843
  49.4 4.7 %collective-permute-start.3 = (f32[136,128]{1,0:T(8,128)S(1)}, f32[136,128]{1,0:T(8,128)S(1)}, u32[]{:S(2)}, u32[]{:S(2)}) collective-permute-start(f32[136,128]{1,0:T(8,128)S(1)} %shard_map.132.own_ref), channel_id=1, source_target_pairs={{0,2},{1,3},{2,0},{3,1},{4,6},{5,7},{6,4},{7,5},{8,10},{9,11},{10,... | collective-permute-start | bytes 208904 | tf_op jit(solution)/shard_map/ppermute | solution.py:843
  49.8 4.2 %collective-permute-start.2 = (f32[136,128]{1,0:T(8,128)S(1)}, f32[136,128]{1,0:T(8,128)S(1)}, u32[]{:S(2)}, u32[]{:S(2)}) collective-permute-start(f32[136,128]{1,0:T(8,128)S(1)} %shard_map.132.own_ref), channel_id=1, source_target_pairs={{0,1},{1,0},{2,3},{3,2},{4,5},{5,4},{6,7},{7,6},{8,9},{9,8},{10,11... | collective-permute-start | bytes 208904 | tf_op jit(solution)/shard_map/ppermute | solution.py:843
